TPU v7x, 32 devices: a whole 2x2x4 slice. The times are simulated.
32 devices in a mesh: scen: 8 (over z, x), rep: 4 (over y, core).
Axes of the slice: x: 2, y: 2, z: 4, core: 2. Of those that a mesh axis runs over, the one named last changes fastest.
Arguments:
- scenarios: bfloat16 [8192, 16384], P('scen', 'rep'), may hold values from -24 to 24, as said below
- rep_index: int32 [1024], replicated, may hold values from 0 to 8191, as said below
Outputs:
- scen_potential: float32 [8192], P('scen')
- rep_potential: float32 [1024], P('rep')
- membership: bfloat16 [1024, 8192], P('rep', 'scen')
Inputs may be any that keep to these rules, and one draw needn't show every extreme that they name: `rep_index`: the entries are distinct scenario numbers; each aligned block of 1024 consecutive scenarios holds exactly 128 of them. `scenarios`: finite surge values.
All inputs are finite; a program needn't handle non-finite values.
Results may differ from a plain program's by a relative error of at most 0.0035.
Values may be sent and summed in bfloat16 or wider, within the bound.
No kernel may reach another device: no remote copies, remote signals or barrier semaphores. Data moves between devices by JAX's collectives and lax.ppermute only.
A program may use at most 64 MiB of HBM per device.

v0:
```python
import math

import jax
import jax.numpy as jnp
from jax import lax
from jax.sharding import PartitionSpec as P

F = 16384
ITERS = 3


eps_blur = 0.1


def scen_lse(score):
    local_peak = jnp.max(score, axis=0)
    peak = lax.pmax(local_peak, "rep")
    total = lax.psum(jnp.sum(jnp.exp(score - peak[None, :]), axis=0), "rep")
    return peak + jnp.log(total)


def rep_lse(score):
    local_peak = jnp.max(score, axis=1)
    peak = lax.pmax(local_peak, "scen")
    total = lax.psum(jnp.sum(jnp.exp(score - peak[:, None]), axis=1), "scen")
    return peak + jnp.log(total)


def on_device(scenarios, rep_index):
    scen_rows = scenarios.shape[0]
    offset = lax.axis_index("scen") * scen_rows
    sq_scen = jnp.sum(jnp.square(scenarios.astype(jnp.float32)), axis=1)
    count_r = rep_index.shape[0]
    per_block = count_r // lax.axis_size("scen")
    position = jnp.arange(count_r, dtype=jnp.int32)
    block_of = rep_index // scen_rows
    mine = block_of == lax.axis_index("scen")
    local_order = jnp.argsort(jnp.where(mine, 0, 1) * count_r + position)[:per_block]
    picked = jnp.take(scenarios, rep_index[local_order] - offset, axis=0)
    gathered = lax.all_gather(picked, "scen", axis=0, tiled=True)
    order = jnp.argsort(block_of * count_r + position)
    inverse = jnp.argsort(order)
    reps = jnp.take(gathered, inverse, axis=0)
    sq_rep = jnp.sum(jnp.square(reps.astype(jnp.float32)), axis=1)
    cross = lax.dot_general(
        reps, scenarios, (((1,), (1,)), ((), ())), preferred_element_type=jnp.float32
    )
    cost = (
        lax.psum_scatter(
            sq_rep[:, None] + sq_scen[None, :] - 2.0 * cross, "rep", scatter_dimension=0, tiled=True
        )
        / F
    )
    count_s = scen_rows * lax.axis_size("scen")
    rep_pot = jnp.zeros((cost.shape[0],), jnp.float32)
    scen_pot = jnp.zeros((scen_rows,), jnp.float32)
    for step in range(ITERS):
        scen_pot = -eps_blur * math.log(count_s) - eps_blur * scen_lse(
            (rep_pot[:, None] - cost) / eps_blur
        )
        rep_pot = -eps_blur * math.log(count_r) - eps_blur * rep_lse(
            (scen_pot[None, :] - cost) / eps_blur
        )
    member = (count_s * jnp.exp((scen_pot[None, :] + rep_pot[:, None] - cost) / eps_blur)).astype(
        jnp.bfloat16
    )
    return (scen_pot, rep_pot, member)


def solution(mesh):
    return jax.shard_map(
        on_device,
        mesh=mesh,
        in_specs=(P("scen", "rep"), P()),
        out_specs=(P("scen"), P("rep"), P("rep", "scen")),
        check_vma=False,
    )
```

profile of v0, /device:TPU:0, one launch (start us, length us, event | category | flops | bytes accessed | tf_op | source)
XLA Modules:
  0.0 399.7 jit_solution(6303462063394616003)
XLA Ops:
  7.2 0.0 all-gather.2.cloned.1.call-start
  7.2 0.7 iota_add_fusion.1
  7.9 4.4 %sort.47 = (s32[1024]{0:T(1024)}, s32[1024]{0:T(1024)S(1)}) sort(s32[1024]{0:T(1024)S(1)} %get-tuple-element.10, s32[1024]{0:T(1024)S(1)} %iota.19), dimensions={0}, to_apply=%region_2.3 | sort | flops 10240 | bytes 16384 | tf_op jit(solution)/shard_map/jit(argsort)/sort | solution.py:38
  12.3 1.6 gather_fusion
  13.9 6.7 %gather_fusion.1 = bf16[128,4096]{1,0:T(8,128)(2,1)S(1)} fusion(bf16[1024,4096]{1,0:T(8,128)(2,1)} %param.2, s32[1024]{0:T(1024)S(1)} %pad_clamp_fusion), kind=kCustom, calls=%fused_computation.1 | custom fusion | bytes 2097664 | tf_op jit(solution)/shard_map/jit(_take)/gather | solution.py:39
  20.6 1.2 broadcast_select_fusion.4
  21.9 0.0 all-gather.2.cloned.1.call-update
  21.9 0.2 reduce-scatter.2.cloned.1.call-start
  22.1 4.4 %sort.45 = (s32[1024]{0:T(1024)}, s32[1024]{0:T(1024)S(1)}) sort(s32[1024]{0:T(1024)S(1)} %get-tuple-element.9, s32[1024]{0:T(1024)S(1)} %iota.16), dimensions={0}, to_apply=%region_0.0 | sort | flops 10240 | bytes 16384 | tf_op jit(solution)/shard_map/jit(argsort)/sort | solution.py:41
  26.5 4.4 %sort.46 = (s32[1024]{0:T(1024)}, s32[1024]{0:T(1024)S(1)}) sort(s32[1024]{0:T(1024)S(1)} %get-tuple-element.6, s32[1024]{0:T(1024)S(1)} %iota.17), dimensions={0}, to_apply=%region_1.2 | sort | flops 10240 | bytes 16384 | tf_op jit(solution)/shard_map/jit(argsort)/sort | solution.py:42
  30.9 5.9 %multiply_reduce_fusion = f32[1024]{0:T(1024)S(1)} fusion(bf16[1024,4096]{1,0:T(8,128)(2,1)} %param.2), kind=kLoop, calls=%fused_computation.3 | loop fusion | flops 12581888 | bytes 8392704 | tf_op jit(solution)/shard_map/reduce_sum | solution.py:32
  36.7 113.6 %all-gather.2.cloned.1.call-done = bf16[1024,4096]{1,0:T(8,128)(2,1)} async-done(((bf16[128,4096]{1,0:T(8,128)(2,1)}), bf16[1024,4096]{1,0:T(8,128)(2,1)}) %all-gather.2.cloned.1.call-update) | async-done | bytes 8388624 | tf_op jit(solution)/shard_map/all_gather | solution.py:40
  150.3 19.5 %gather_fusion.2 = bf16[1024,4096]{1,0:T(8,128)(2,1)} fusion(bf16[1024,4096]{1,0:T(8,128)(2,1)} %all-gather.2.cloned.1.call-done, s32[1024]{0:T(1024)S(1)} %fusion.9), kind=kCustom, calls=%fused_computation.2 | custom fusion | bytes 16781312 | tf_op jit(solution)/shard_map/jit(_take)/gather | solution.py:43
  169.8 0.0 copy-start.1
  169.8 5.9 %multiply_reduce_fusion.1 = f32[1024]{0:T(1024)S(1)} fusion(bf16[1024,4096]{1,0:T(8,128)(2,1)} %gather_fusion.2, pred[1024]{0:T(1024)(128)(4,1)S(1)} %compare_and_fusion), kind=kLoop, calls=%fused_computation.4 | loop fusion | flops 16776192 | bytes 8393728 | tf_op jit(solution)/shard_map/reduce_sum | solution.py:44
  175.7 0.0 copy-done.1
  175.7 12.8 %multiply_subtract_fusion = f32[1024,1024]{1,0:T(8,128)} fusion(f32[1024]{0:T(1024)S(1)} %multiply_reduce_fusion, f32[1024]{0:T(1024)S(1)} %multiply_reduce_fusion.1, bf16[1024,4096]{1,0:T(8,128)(2,1)} %param.2, bf16[1024,4096]{1,0:T(8,128)(2,1)S(1)} %copy-done.1, pred[1024]{0:T(1024)(128)(4,1)S(1)} %compare_and_fusion), kind=kOutput, calls=%fused_computation.6 | convolution fusion | flops 8597274624 | bytes 20980736 | tf_op jit(solution)/shard_map/dot_general | solution.py:45
  188.5 0.0 reduce-scatter.2.cloned.1.call-update
  188.5 42.9 %reduce-scatter.2.cloned.1.call-done = f32[256,1024]{1,0:T(8,128)} async-done(((f32[1024,1024]{1,0:T(8,128)}), f32[256,1024]{1,0:T(8,128)}) %reduce-scatter.2.cloned.1.call-update) | async-done | bytes 1048592 | tf_op jit(solution)/shard_map/reduce_scatter | solution.py:49
  231.4 0.0 copy-start
  231.4 1.5 fusion.1
  232.8 5.8 %pmax.42 = f32[1024]{0:T(1024)S(1)} all-reduce(f32[1024]{0:T(1024)S(1)} %fusion.1), channel_id=1, replica_groups=mesh['scen'=8,'rep'=4] {'rep'}, use_global_device_ids=true, to_apply=%region_7.8 | all-reduce | flops 1024 | bytes 8192 | tf_op jit(solution)/shard_map/pmax | solution.py:17
  238.6 1.5 exponential_reduce_fusion.5
  240.1 5.7 %psum.42 = f32[1024]{0:T(1024)S(1)} all-reduce(f32[1024]{0:T(1024)S(1)} %exponential_reduce_fusion.5), channel_id=1, replica_groups=mesh['scen'=8,'rep'=4] {'rep'}, use_global_device_ids=true, to_apply=%region_9.10 | all-reduce | flops 1024 | bytes 8192 | tf_op jit(solution)/shard_map/psum | solution.py:18
  245.8 1.4 fusion.2
  247.2 21.8 %pmax.43 = f32[256]{0:T(256)S(1)} all-reduce(f32[256]{0:T(256)S(1)} %fusion.2), channel_id=1, replica_groups=mesh['scen'=8,'rep'=4] {'scen'}, use_global_device_ids=true, to_apply=%region_11.12 | all-reduce | flops 256 | bytes 2048 | tf_op jit(solution)/shard_map/pmax | solution.py:24
  269.0 1.6 exponential_reduce_fusion.4
  270.5 17.1 %psum.43 = f32[256]{0:T(256)S(1)} all-reduce(f32[256]{0:T(256)S(1)} %exponential_reduce_fusion.4), channel_id=1, replica_groups=mesh['scen'=8,'rep'=4] {'scen'}, use_global_device_ids=true, to_apply=%region_13.14 | all-reduce | flops 256 | bytes 2048 | tf_op jit(solution)/shard_map/psum | solution.py:25
  287.7 1.4 fusion.3
  289.1 5.7 %pmax.44 = f32[1024]{0:T(1024)S(1)} all-reduce(f32[1024]{0:T(1024)S(1)} %fusion.3), channel_id=1, replica_groups=mesh['scen'=8,'rep'=4] {'rep'}, use_global_device_ids=true, to_apply=%region_15.16 | all-reduce | flops 1024 | bytes 8192 | tf_op jit(solution)/shard_map/pmax | solution.py:17
  294.8 1.5 exponential_reduce_fusion.3
  296.3 6.9 %psum.44 = f32[1024]{0:T(1024)S(1)} all-reduce(f32[1024]{0:T(1024)S(1)} %exponential_reduce_fusion.3), channel_id=1, replica_groups=mesh['scen'=8,'rep'=4] {'rep'}, use_global_device_ids=true, to_apply=%region_17.18 | all-reduce | flops 1024 | bytes 8192 | tf_op jit(solution)/shard_map/psum | solution.py:18
  303.2 1.4 fusion.4
  304.7 19.1 %pmax.45 = f32[256]{0:T(256)S(1)} all-reduce(f32[256]{0:T(256)S(1)} %fusion.4), channel_id=1, replica_groups=mesh['scen'=8,'rep'=4] {'scen'}, use_global_device_ids=true, to_apply=%region_19.20 | all-reduce | flops 256 | bytes 2048 | tf_op jit(solution)/shard_map/pmax | solution.py:24
  323.8 1.6 exponential_reduce_fusion.2
  325.4 17.1 %psum.45 = f32[256]{0:T(256)S(1)} all-reduce(f32[256]{0:T(256)S(1)} %exponential_reduce_fusion.2), channel_id=1, replica_groups=mesh['scen'=8,'rep'=4] {'scen'}, use_global_device_ids=true, to_apply=%region_21.22 | all-reduce | flops 256 | bytes 2048 | tf_op jit(solution)/shard_map/psum | solution.py:25
  342.5 0.0 copy-done
  342.5 0.2 fusion.5
  342.7 5.7 %pmax.46 = f32[1024]{0:T(1024)S(1)} all-reduce(f32[1024]{0:T(1024)S(1)} %fusion.5), channel_id=1, replica_groups=mesh['scen'=8,'rep'=4] {'rep'}, use_global_device_ids=true, to_apply=%region_23.24 | all-reduce | flops 1024 | bytes 8192 | tf_op jit(solution)/shard_map/pmax | solution.py:17
  348.4 0.3 exponential_reduce_fusion.1
  348.7 6.1 %psum.46 = f32[1024]{0:T(1024)S(1)} all-reduce(f32[1024]{0:T(1024)S(1)} %exponential_reduce_fusion.1), channel_id=1, replica_groups=mesh['scen'=8,'rep'=4] {'rep'}, use_global_device_ids=true, to_apply=%region_25.26 | all-reduce | flops 1024 | bytes 8192 | tf_op jit(solution)/shard_map/psum | solution.py:18
  354.9 0.2 fusion.6
  355.1 19.2 %pmax.47 = f32[256]{0:T(256)S(1)} all-reduce(f32[256]{0:T(256)S(1)} %fusion.6), channel_id=1, replica_groups=mesh['scen'=8,'rep'=4] {'scen'}, use_global_device_ids=true, to_apply=%region_27.28 | all-reduce | flops 256 | bytes 2048 | tf_op jit(solution)/shard_map/pmax | solution.py:24
  374.2 0.4 exponential_reduce_fusion
  374.6 17.1 %psum.47 = f32[256]{0:T(256)S(1)} all-reduce(f32[256]{0:T(256)S(1)} %exponential_reduce_fusion), channel_id=1, replica_groups=mesh['scen'=8,'rep'=4] {'scen'}, use_global_device_ids=true, to_apply=%region_29.30 | all-reduce | flops 256 | bytes 2048 | tf_op jit(solution)/shard_map/psum | solution.py:25
  391.8 1.1 multiply_convert_fusion
  392.9 0.0 copy-done.2
  392.9 0.0 copy-done.3
  (18 shorter events, 0.1 us)
Async XLA Ops:
  7.2 143.1 %all-gather.2.cloned.1.call-start = ((), (), s32[]{:S(2)}) async-start(), calls=%async_computation.1 | async-start | bytes 9437184 | tf_op jit(solution)/shard_map/all_gather | solution.py:40
  21.9 209.5 %reduce-scatter.2.cloned.1.call-start = ((), (), s32[]{:S(2)}) async-start(), calls=%async_computation.2 | async-start | bytes 5242880 | tf_op jit(solution)/shard_map/reduce_scatter | solution.py:49
  169.8 5.9 %copy-start.1 = (bf16[1024,4096]{1,0:T(8,128)(2,1)S(1)}, bf16[1024,4096]{1,0:T(8,128)(2,1)}, u32[]{:S(2)}) copy-start(bf16[1024,4096]{1,0:T(8,128)(2,1)} %gather_fusion.2) | copy-start | bytes 25165828
  231.4 111.1 %copy-start = (f32[256,1024]{1,0:T(8,128)S(1)}, f32[256,1024]{1,0:T(8,128)}, u32[]{:S(2)}) copy-start(f32[256,1024]{1,0:T(8,128)} %reduce-scatter.2.cloned.1.call-done) | copy-start | bytes 3145732
  354.9 38.0 %copy-start.2 = (f32[1024]{0:T(1024)}, f32[1024]{0:T(1024)S(1)}, u32[]{:S(2)}) copy-start(f32[1024]{0:T(1024)S(1)} %multiply_subtract_fusion.1) | copy-start | bytes 12292
  391.8 1.1 copy-start.3
Sparse Core Ops, SparseCore 0:
  22.0 128.2 all-gather.1
  188.6 42.7 reduce-scatter.1
where the time goes:
time: 401 us; the launch traced here: 400 us
  waiting for transfers between devices  156 us (39%)
  blocking collectives  147 us (37%)
  other arithmetic  41 us (10%)
  local copies, waits for them, and re-layouts  27.9 us (7%)
  between operations  14.1 us (4%)
  matrix products  12.8 us (3%)
    all_gather x1, waiting for transfers between devices, on_device(): gathered = lax.all_gather(picked, 'scen', axis=0, tiled=True)  114 us
    pmax x3, blocking collectives, rep_lse(): peak = lax.pmax(local_peak, 'scen')  60.1 us
    psum x3, blocking collectives, rep_lse(): total = lax.psum(jnp.sum(jnp.exp(score - peak[:, None]), axis=1), 'scen')  51.4 us
    reduce_scatter x1, waiting for transfers between devices, on_device(): lax.psum_scatter(sq_rep[:, None] + sq_scen[None, :] - 2.0 * cross, 'rep',...  42.9 us
    gather x1, local copies, waits for them, and re-layouts, on_device(): reps = jnp.take(gathered, inverse, axis=0)  19.5 us
    psum x3, blocking collectives, scen_lse(): total = lax.psum(jnp.sum(jnp.exp(score - peak[None, :]), axis=0), 'rep')  18.7 us
    pmax x3, blocking collectives, scen_lse(): peak = lax.pmax(local_peak, 'rep')  17.1 us
    dot_general x1, matrix products, on_device(): lax.dot_general(reps, scenarios, (((1,), (1,)), ((), ())), preferred_elem...  12.8 us
  transfers between devices with their start and end apart: 2, of which 2 were waited for; matrix products, arithmetic and copies ran while one was open for 4% of the time, Pallas kernels for 0%

commit v1 on v0

v1 whole, which is shorter than its diff:
```python
import functools
import math

import jax
import jax.numpy as jnp
from jax import lax
from jax.experimental import pallas as pl
from jax.experimental.pallas import tpu as pltpu
from jax.sharding import PartitionSpec as P

ITERS = 3
eps_blur = 0.1

LANES = 128
SUB = 8
NT = (((1,), (1,)), ((), ()))
VMEM = pl.BlockSpec(memory_space=pltpu.VMEM)
SMEM = pl.BlockSpec(memory_space=pltpu.SMEM)


def square_sums(x):
    gram = lax.dot_general(x, x, NT, preferred_element_type=jnp.float32)
    n = x.shape[0]
    eye = lax.broadcasted_iota(jnp.int32, (n, n), 0) == lax.broadcasted_iota(jnp.int32, (n, n), 1)
    return jnp.sum(jnp.where(eye, gram, 0.0), axis=0, keepdims=True)


def pick_kernel(sel_ref, scen_ref, out_ref, *, step):
    for at in range(0, scen_ref.shape[1], step):
        out_ref[:, at : at + step] = jnp.dot(
            sel_ref[...], scen_ref[:, at : at + step], preferred_element_type=jnp.float32
        ).astype(out_ref.dtype)


def pick(sel, scenarios):
    rows, width = sel.shape[0], scenarios.shape[1]
    return pl.pallas_call(
        functools.partial(pick_kernel, step=min(512, width)),
        out_shape=jax.ShapeDtypeStruct((rows, width), scenarios.dtype),
        in_specs=[VMEM] * 2,
        out_specs=VMEM,
        cost_estimate=pl.CostEstimate(
            flops=2 * rows * scenarios.size, bytes_accessed=2 * scenarios.size, transcendentals=0
        ),
        name="pick",
    )(sel, scenarios)


def norm_kernel(scen_ref, out_ref):
    def body(i, carry):
        rows = pl.ds(pl.multiple_of(i * 16, 16), 16)
        x = scen_ref[rows, :].astype(jnp.float32)
        out_ref[rows, :] = jnp.broadcast_to(jnp.sum(x * x, axis=1, keepdims=True), (16, LANES))
        return carry

    lax.fori_loop(0, scen_ref.shape[0] // 16, body, 0, unroll=2)


def norms(scenarios):
    return pl.pallas_call(
        norm_kernel,
        out_shape=jax.ShapeDtypeStruct((scenarios.shape[0], LANES), jnp.float32),
        in_specs=[VMEM],
        out_specs=VMEM,
        cost_estimate=pl.CostEstimate(
            flops=2 * scenarios.size, bytes_accessed=2 * scenarios.size, transcendentals=0
        ),
        name="norms",
    )(scenarios)


def cost_kernel(core_ref, scen_ref, sq_ref, *refs, tile):
    *chunks, send_ref, keep_ref = refs
    reps = jnp.concatenate([c[...] for c in chunks], axis=0)
    sq_rep = square_sums(reps)
    half = send_ref.shape[0]
    core = core_ref[0]
    for out_ref, which in ((send_ref, 1 - core), (keep_ref, core)):
        for at in range(0, half, tile):
            rows = pl.ds(pl.multiple_of(which * half + at, tile), tile)
            cross = lax.dot_general(scen_ref[rows, :], reps, NT, preferred_element_type=jnp.float32)
            out_ref[at : at + tile, :] = sq_rep + sq_ref[rows, 0:1] - 2.0 * cross


def cost_share(core, scenarios, sq_scen, chunks):
    rows, width = scenarios.shape
    cols = sum(c.shape[0] for c in chunks)
    half = jax.ShapeDtypeStruct((rows // 2, cols), jnp.float32)
    return pl.pallas_call(
        functools.partial(cost_kernel, tile=min(256, rows // 2)),
        out_shape=(half, half),
        in_specs=[SMEM] + [VMEM] * (2 + len(chunks)),
        out_specs=(VMEM, VMEM),
        cost_estimate=pl.CostEstimate(
            flops=2 * rows * cols * width, bytes_accessed=2 * rows * width, transcendentals=0
        ),
        name="cost_share",
    )(core, scenarios, sq_scen, *chunks)


def tree(op, xs):
    while len(xs) > 1:
        xs = [op(*xs[i : i + 2]) if i + 1 < len(xs) else xs[i] for i in range(0, len(xs), 2)]
    return xs[0]


def put_sums(acc, out_ref, shift):
    at = lax.broadcasted_iota(jnp.int32, (len(acc), LANES), 0)
    total = jnp.zeros((len(acc), LANES), jnp.float32)
    for i, a in enumerate(acc):
        total = jnp.where(at == i, jnp.sum(a, axis=0, keepdims=True), total)
    if shift is not None:
        total = pltpu.roll(total, shift, 0)
    for k in range(out_ref.shape[0]):
        out_ref[k] = total


def get_factors(got_ref, scale, shift):
    total = tree(jnp.add, [got_ref[k] for k in range(got_ref.shape[0])])
    if shift is not None:
        total = pltpu.roll(total, shift, 0)
    return scale / total


def spread(w):
    return [jnp.broadcast_to(w[i : i + 1, :], (SUB, LANES)) for i in range(w.shape[0])]


def first_kernel(ids_ref, *refs, pieces, scale, rolled):
    stages = len(refs) // 2 - 1
    mine, other = refs[:stages], refs[stages : 2 * stages]
    e_ref, peak_ref, out_ref = refs[2 * stages :]
    half = mine[0].shape[0]
    core = ids_ref[0]

    def body(i, acc, h):
        src = pl.ds(pl.multiple_of(i * SUB, SUB), SUB)
        dst = pl.ds(pl.multiple_of(h * half + i * SUB, SUB), SUB)
        z = []
        for s, at in pieces:
            cols = slice(at, at + LANES)
            z.append(jnp.where(core == h, mine[s][src, cols], other[s][src, cols]) * scale)
        peak = jnp.max(tree(jnp.maximum, z), axis=1, keepdims=True)
        e = [jnp.exp(x - peak) for x in z]
        q = 1.0 / jnp.sum(tree(jnp.add, e), axis=1, keepdims=True)
        for k, x in enumerate(e):
            e_ref[dst, k * LANES : (k + 1) * LANES] = x
        peak_ref[dst, :] = jnp.broadcast_to(peak, (SUB, LANES))
        return tuple(a + x * q for a, x in zip(acc, e, strict=True))

    acc = tuple(jnp.zeros((SUB, LANES), jnp.float32) for _ in pieces)
    for h in range(2):
        acc = lax.fori_loop(0, half // SUB, functools.partial(body, h=h), acc, unroll=4)
    put_sums(acc, out_ref, ids_ref[1] if rolled else None)


def step_kernel(ids_ref, got_ref, e_ref, out_ref, *, scale, rolled):
    tiles = e_ref.shape[1] // LANES
    w = spread(get_factors(got_ref, scale, ids_ref[2] if rolled else None))

    def body(i, acc):
        rows = pl.ds(pl.multiple_of(i * SUB, SUB), SUB)
        e = [e_ref[rows, k * LANES : (k + 1) * LANES] for k in range(tiles)]
        q = 1.0 / jnp.sum(tree(jnp.add, [x * f for x, f in zip(e, w)]), axis=1, keepdims=True)
        return tuple(a + x * q for a, x in zip(acc, e, strict=True))

    acc = tuple(jnp.zeros((SUB, LANES), jnp.float32) for _ in range(tiles))
    acc = lax.fori_loop(0, e_ref.shape[0] // SUB, body, acc, unroll=4)
    put_sums(acc, out_ref, ids_ref[1] if rolled else None)


def last_kernel(ids_ref, got_ref, e_ref, peak_ref, out_ref, pot_ref, scaled_ref, col_ref, *, scale, rolled, log_count):
    rows_all = e_ref.shape[0]
    tiles = e_ref.shape[1] // LANES
    w = spread(get_factors(got_ref, scale, ids_ref[2] if rolled else None))

    def body(i, acc):
        rows = pl.ds(pl.multiple_of(i * SUB, SUB), SUB)
        e = [e_ref[rows, k * LANES : (k + 1) * LANES] for k in range(tiles)]
        total = jnp.sum(tree(jnp.add, [x * f for x, f in zip(e, w)]), axis=1, keepdims=True)
        col_ref[rows, :] = -eps_blur * (log_count + peak_ref[rows, :] + jnp.log(total))
        e = [x * (1.0 / total) for x in e]
        for k, x in enumerate(e):
            scaled_ref[rows, k * LANES : (k + 1) * LANES] = x
        return tuple(a + x for a, x in zip(acc, e, strict=True))

    acc = tuple(jnp.zeros((SUB, LANES), jnp.float32) for _ in range(tiles))
    acc = lax.fori_loop(0, rows_all // SUB, body, acc, unroll=4)
    put_sums(acc, out_ref, ids_ref[1] if rolled else None)
    for i in range(rows_all // LANES):
        block = col_ref[i * LANES : (i + 1) * LANES, :]
        pot_ref[i : i + 1, :] = jnp.transpose(block)[0:1, :]


def out_kernel(ids_ref, got_ref, scaled_ref, perm_ref, pot_ref, member_ref, *, scale, rolled):
    tiles = scaled_ref.shape[1] // LANES
    factors = get_factors(got_ref, scale, ids_ref[2] if rolled else None)
    w = jnp.concatenate([factors[i : i + 1, :] for i in range(tiles)], axis=1)
    v = eps_blur * jnp.log(w)
    high = v.astype(jnp.bfloat16).astype(jnp.float32)
    mid = (v - high).astype(jnp.bfloat16).astype(jnp.float32)
    low = v - high - mid
    at = lax.broadcasted_iota(jnp.int32, (16, w.shape[1]), 0)
    parts = jnp.where(at == 0, high, jnp.where(at == 1, mid, jnp.where(at == 2, low, 0.0)))
    moved = lax.dot_general(
        parts.astype(jnp.bfloat16), perm_ref[...], NT, preferred_element_type=jnp.float32
    )
    pot_ref[...] = moved[0:1, :] + moved[1:2, :] + moved[2:3, :]
    step = min(256, scaled_ref.shape[0])
    for i in range(0, scaled_ref.shape[0], step):
        plan = (scaled_ref[i : i + step, :] * w).astype(jnp.bfloat16)
        member_ref[:, i : i + step] = lax.dot_general(
            perm_ref[...], plan, NT, preferred_element_type=jnp.float32
        ).astype(member_ref.dtype)


def on_device(scenarios, rep_index):
    scen_rows, width = scenarios.shape
    n = lax.axis_size("scen")
    n_rep = lax.axis_size("rep")
    d = lax.axis_index("scen")
    rep = lax.axis_index("rep")
    count_r = rep_index.shape[0]
    count_s = scen_rows * n
    per = count_r // n
    features = width * n_rep
    rolled = per == LANES
    as_int = lambda x: x.astype(jnp.int32)

    ring = list(range(0, n, 2)) + list(range(n - 1, 0, -2))
    up = [(ring[i], ring[(i + 1) % n]) for i in range(n)]
    down = [(b, a) for a, b in up]
    place = jnp.where(d % 2 == 0, d // 2, n - 1 - d // 2)

    local = as_int(rep_index - d * scen_rows)
    i_scen = jnp.arange(scen_rows, dtype=jnp.int32)
    chosen = jnp.sum(as_int(local[:, None] == i_scen[None, :]), axis=0)
    before = jnp.sum(as_int((local[:, None] >= 0) & (local[:, None] < i_scen[None, :])), axis=0)
    key = jnp.where(chosen > 0, before, -1)
    sel = (key[None, :] == jnp.arange(per, dtype=jnp.int32)[:, None]).astype(scenarios.dtype)
    mine = pick(sel, scenarios)

    core = rep % 2
    ids = jnp.stack([core, place, (n - place) % n]).astype(jnp.int32)
    sq_scen = norms(scenarios)

    def swap(x, bit):
        return lax.ppermute(x, "rep", [(i, i ^ bit) for i in range(n_rep)])

    def total(chunks):
        send, keep = cost_share(ids, scenarios, sq_scen, chunks)
        part = keep + swap(send, 1)
        bit = 2
        while bit < n_rep:
            part = part + swap(part, bit)
            bit *= 2
        return part, swap(part, 1)

    halves = [mine[: per // 2], mine[per // 2 :]]
    a, b = halves, halves[::-1]
    stages = [total(halves)]
    slots = [[(0, 0)]]
    for k in range(1, n // 2 + 1):
        if k == n // 2:
            a, b = a[:1], b[:1]
        a = [lax.ppermute(c, "scen", up) for c in a]
        b = [lax.ppermute(c, "scen", down) for c in b]
        stages.append(total(a + b[::-1]))
    where = {0: (0, 0), n // 2: (n // 2, 0)}
    for k in range(1, n // 2):
        where[n - k], where[k] = (k, 0), (k, per)

    own, other = [s[0] for s in stages], [s[1] for s in stages]
    if not rolled:
        join = lambda xs: [
            jnp.concatenate([xs[where[q][0]][:, where[q][1] : where[q][1] + per] for q in range(n)], axis=1)
        ]
        own, other = join(own), join(other)
        pieces = [(0, i * LANES) for i in range(count_r // LANES)]
    else:
        pieces = [where[q] for q in range(n)]

    rows_out = count_r // n_rep
    wanted = lax.dynamic_slice_in_dim(rep_index, rep * rows_out, rows_out)
    rank = jnp.sum(as_int(rep_index[None, :] < wanted[:, None]), axis=1)
    block = rank // per
    slot = (jnp.where(block % 2 == 0, block // 2, n - 1 - block // 2) - place) % n
    at = slot * per + rank % per
    perm = (at[:, None] == jnp.arange(count_r, dtype=jnp.int32)[None, :]).astype(jnp.bfloat16)

    f32 = lambda *shape: jax.ShapeDtypeStruct(shape, jnp.float32)
    tiles = count_r // LANES
    sums = f32(n, tiles, LANES)

    def exchange(x):
        if not rolled:
            x = jnp.roll(x.reshape(n, count_r), place * per, axis=1).reshape(x.shape)
        x = lax.all_to_all(x, "scen", 0, 0, tiled=False)
        if not rolled:
            x = jnp.roll(x.reshape(n, count_r), -place * per, axis=1).reshape(x.shape)
        return x

    e, peak, x = pl.pallas_call(
        functools.partial(first_kernel, pieces=pieces, scale=-1.0 / (features * eps_blur), rolled=rolled),
        out_shape=(f32(scen_rows, count_r), f32(scen_rows, LANES), sums),
        in_specs=[SMEM] + [VMEM] * (2 * len(own)),
        out_specs=(VMEM,) * 3,
        name="first",
    )(ids, *own, *other)
    scale = count_s / count_r
    for _ in range(ITERS - 2):
        x = pl.pallas_call(
            functools.partial(step_kernel, scale=scale, rolled=rolled),
            out_shape=sums,
            in_specs=[SMEM, VMEM, VMEM],
            out_specs=VMEM,
            name="step",
        )(ids, exchange(x), e)
    x, scen_pot, scaled = pl.pallas_call(
        functools.partial(last_kernel, scale=scale, rolled=rolled, log_count=math.log(count_s)),
        out_shape=(sums, f32(scen_rows // LANES, LANES), f32(scen_rows, count_r)),
        in_specs=[SMEM] + [VMEM] * 3,
        out_specs=(VMEM,) * 3,
        scratch_shapes=[pltpu.VMEM((scen_rows, LANES), jnp.float32)],
        name="last",
    )(ids, exchange(x), e, peak)
    rep_pot, member = pl.pallas_call(
        functools.partial(out_kernel, scale=scale, rolled=rolled),
        out_shape=(f32(1, rows_out), jax.ShapeDtypeStruct((rows_out, scen_rows), jnp.bfloat16)),
        in_specs=[SMEM] + [VMEM] * 3,
        out_specs=(VMEM, VMEM),
        name="out",
    )(ids, exchange(x), scaled, perm)
    return scen_pot.reshape(scen_rows), rep_pot.reshape(rows_out), member


def solution(mesh):
    return jax.shard_map(
        on_device,
        mesh=mesh,
        in_specs=(P("scen", "rep"), P()),
        out_specs=(P("scen"), P("rep"), P("rep", "scen")),
        check_vma=False,
    )
```

time: 401 us -> 212 us (0.53)
  blocking collectives: 147 us -> 0 us
  Pallas kernels: 0 us -> 80.2 us
  waiting for transfers between devices: 156 us -> 76.5 us
  starting transfers between devices: 0.26 us -> 38.7 us
  other arithmetic: 41 us -> 10.1 us
  local copies, waits for them, and re-layouts: 27.9 us -> 4.96 us
  between operations: 14.1 us -> 1.01 us
  matrix products: 12.8 us -> 0 us
    all_gather x1 -> x0, waiting for transfers between devices: 114 us -> none  [on_device(): gathered = lax.all_gather(picked, 'scen', axis=0, tiled=True)]
    pallas_call x0 -> x11, Pallas kernels: none -> 80.2 us  [the longest x5 37.4 us: cost_share(): pl.pallas_call(functools.partial(cost_kernel, tile=min(256, rows // 2)),...]
    pmax x6 -> x0, blocking collectives: 77.2 us -> none  [the longest x3 60.1 us: rep_lse(): peak = lax.pmax(local_peak, 'scen')]
    psum x6 -> x0, blocking collectives: 70.1 us -> none  [the longest x3 51.4 us: rep_lse(): total = lax.psum(jnp.sum(jnp.exp(score - peak[:, None]), axis=1), 'scen')]
    ppermute x0 -> x29, waiting for transfers between devices: none -> 57.8 us  [the longest x7 36 us: on_device(): a = [lax.ppermute(c, 'scen', up) for c in a]]
    reduce_scatter x1 -> x0, waiting for transfers between devices: 42.9 us -> none  [on_device(): lax.psum_scatter(sq_rep[:, None] + sq_scen[None, :] - 2.0 * cross, 'rep',...]
    gather x3 -> x0, local copies, waits for them, and re-layouts: 27.8 us -> none  [the longest x1 19.5 us: on_device(): reps = jnp.take(gathered, inverse, axis=0)]
    ppermute x0 -> x29, starting transfers between devices: none -> 27.2 us  [the longest x7 13.4 us: on_device(): a = [lax.ppermute(c, 'scen', up) for c in a]]
  transfers between devices with their start and end apart: 2 -> 32, of which waited for: 2 -> 13; matrix products, arithmetic and copies ran while one was open for 4% -> 4% of each run, Pallas kernels for 0% -> 22%
where the time goes in v1:
time: 212 us; the launch traced here: 211 us
  Pallas kernels  80.2 us (38%)
  waiting for transfers between devices  76.5 us (36%)
  starting transfers between devices  38.7 us (18%)
  other arithmetic  10.1 us (5%)
  local copies, waits for them, and re-layouts  4.96 us (2%)
    pallas_call x5, Pallas kernels, cost_share(): pl.pallas_call(functools.partial(cost_kernel, tile=min(256, rows // 2)),...  37.4 us
    ppermute x7, waiting for transfers between devices, on_device(): a = [lax.ppermute(c, 'scen', up) for c in a]  36 us
    ppermute x15, waiting for transfers between devices, swap(): return lax.ppermute(x, 'rep', [(i, i ^ bit) for i in range(n_rep)])  21.6 us
    all_to_all x3, waiting for transfers between devices, exchange(): x = lax.all_to_all(x, 'scen', 0, 0, tiled=False)  18.7 us
    ppermute x7, starting transfers between devices, on_device(): a = [lax.ppermute(c, 'scen', up) for c in a]  13.4 us
    all_to_all x3, starting transfers between devices, exchange(): x = lax.all_to_all(x, 'scen', 0, 0, tiled=False)  11.5 us
    pallas_call x1, Pallas kernels, on_device(): pl.pallas_call(functools.partial(first_kernel, pieces=pieces, scale=-1.0...  10.5 us
    pallas_call x1, Pallas kernels, norms(): pl.pallas_call(norm_kernel, out_shape=jax.ShapeDtypeStruct((scenarios.sha...  8.69 us
  transfers between devices with their start and end apart: 32, of which 13 were waited for; matrix products, arithmetic and copies ran while one was open for 4% of the time, Pallas kernels for 22%

profile of v1, /device:TPU:0, one launch (start us, length us, event | category | flops | bytes accessed | tf_op | source)
XLA Modules:
  0.0 211.4 jit_solution(245667717372398316)
XLA Ops:
  1.3 1.2 convert_reduce_fusion.1
  2.5 0.8 fusion.2.sel_ref
  3.3 5.8 %pick.1 = bf16[128,4096]{1,0:T(8,128)(2,1)} custom-call(bf16[128,1024]{1,0:T(8,128)(2,1)} %fusion.2.sel_ref, bf16[1024,4096]{1,0:T(8,128)(2,1)} %scen_ref.13), custom_call_target="tpu_custom_call" | custom-call | flops 1073741824 | bytes 8388608 | tf_op jit(solution)/shard_map/pick/pallas_call | solution.py:37
  9.1 1.3 fusion.6
  10.4 3.1 %collective-permute-start.2 = (bf16[64,4096]{1,0:T(8,128)(2,1)S(1)}, bf16[64,4096]{1,0:T(8,128)(2,1)S(1)}, u32[]{:S(2)}, u32[]{:S(2)}) collective-permute-start(bf16[64,4096]{1,0:T(8,128)(2,1)S(1)} %get-tuple-element.44.refs_0_), channel_id=1, source_target_pairs={{0,8},{8,16},{16,24},{24,28},{28,20},{20,12},{12,4},{4,0},{1,9},{9... | collective-permute-start | bytes 1572872 | tf_op jit(solution)/shard_map/ppermute | solution.py:266
  13.4 1.6 collective-permute-start.3
  15.5 10.6 %collective-permute-done.2.refs_0_ = bf16[64,4096]{1,0:T(8,128)(2,1)S(1)} collective-permute-done((bf16[64,4096]{1,0:T(8,128)(2,1)S(1)}, bf16[64,4096]{1,0:T(8,128)(2,1)S(1)}, u32[]{:S(2)}, u32[]{:S(2)}) %collective-permute-start.2) | collective-permute-done | bytes 524320 | tf_op jit(solution)/shard_map/ppermute | solution.py:266
  26.1 2.1 %collective-permute-start.8 = (bf16[64,4096]{1,0:T(8,128)(2,1)S(1)}, bf16[64,4096]{1,0:T(8,128)(2,1)}, u32[]{:S(2)}, u32[]{:S(2)}) collective-permute-start(bf16[64,4096]{1,0:T(8,128)(2,1)S(1)} %collective-permute-done.2.refs_0_), channel_id=1, source_target_pairs={{0,8},{8,16},{16,24},{24,28},{28,20},{20,12},{12,4},{4,0},{1,9},{9... | collective-permute-start | bytes 1572872 | tf_op jit(solution)/shard_map/ppermute | solution.py:266
  28.3 9.1 %collective-permute-done.3.refs_1_ = bf16[64,4096]{1,0:T(8,128)(2,1)S(1)} collective-permute-done((bf16[64,4096]{1,0:T(8,128)(2,1)S(1)}, bf16[64,4096]{1,0:T(8,128)(2,1)S(1)}, u32[]{:S(2)}, u32[]{:S(2)}) %collective-permute-start.3) | collective-permute-done | bytes 524320 | tf_op jit(solution)/shard_map/ppermute | solution.py:266
  37.3 2.1 %collective-permute-start.9 = (bf16[64,4096]{1,0:T(8,128)(2,1)S(1)}, bf16[64,4096]{1,0:T(8,128)(2,1)}, u32[]{:S(2)}, u32[]{:S(2)}) collective-permute-start(bf16[64,4096]{1,0:T(8,128)(2,1)S(1)} %collective-permute-done.3.refs_1_), channel_id=1, source_target_pairs={{0,8},{8,16},{16,24},{24,28},{28,20},{20,12},{12,4},{4,0},{1,9},{9... | collective-permute-start | bytes 1572872 | tf_op jit(solution)/shard_map/ppermute | solution.py:266
  39.5 1.9 collective-permute-start.11
  41.4 7.2 %collective-permute-done.8.refs_0_ = bf16[64,4096]{1,0:T(8,128)(2,1)} collective-permute-done((bf16[64,4096]{1,0:T(8,128)(2,1)S(1)}, bf16[64,4096]{1,0:T(8,128)(2,1)}, u32[]{:S(2)}, u32[]{:S(2)}) %collective-permute-start.8) | collective-permute-done | bytes 524320 | tf_op jit(solution)/shard_map/ppermute | solution.py:266
  48.7 2.1 %collective-permute-start.14 = (bf16[64,4096]{1,0:T(8,128)(2,1)}, bf16[64,4096]{1,0:T(8,128)(2,1)S(1)}, u32[]{:S(2)}, u32[]{:S(2)}) collective-permute-start(bf16[64,4096]{1,0:T(8,128)(2,1)} %collective-permute-done.8.refs_0_), channel_id=1, source_target_pairs={{0,8},{8,16},{16,24},{24,28},{28,20},{20,12},{12,4},{4,0},{1,9},{9... | collective-permute-start | bytes 1572872 | tf_op jit(solution)/shard_map/ppermute | solution.py:266
  50.8 9.1 %collective-permute-done.9.refs_1_ = bf16[64,4096]{1,0:T(8,128)(2,1)} collective-permute-done((bf16[64,4096]{1,0:T(8,128)(2,1)S(1)}, bf16[64,4096]{1,0:T(8,128)(2,1)}, u32[]{:S(2)}, u32[]{:S(2)}) %collective-permute-start.9) | collective-permute-done | bytes 524320 | tf_op jit(solution)/shard_map/ppermute | solution.py:266
  59.9 2.1 %collective-permute-start.15 = (bf16[64,4096]{1,0:T(8,128)(2,1)}, bf16[64,4096]{1,0:T(8,128)(2,1)}, u32[]{:S(2)}, u32[]{:S(2)}) collective-permute-start(bf16[64,4096]{1,0:T(8,128)(2,1)} %collective-permute-done.9.refs_1_), channel_id=1, source_target_pairs={{0,8},{8,16},{16,24},{24,28},{28,20},{20,12},{12,4},{4,0},{1,9},{9... | collective-permute-start | bytes 1572872 | tf_op jit(solution)/shard_map/ppermute | solution.py:266
  62.2 1.9 collective-permute-start.17
  64.1 8.7 %norms.1.sq_ref = f32[1024,128]{1,0:T(8,128)} custom-call(bf16[1024,4096]{1,0:T(8,128)(2,1)} %scen_ref.13), custom_call_target="tpu_custom_call" | custom-call | flops 8388608 | bytes 8388608 | tf_op jit(solution)/shard_map/norms/pallas_call | solution.py:60
  73.3 7.8 %cost_share.6 = (f32[512,256]{1,0:T(8,128)}, f32[512,256]{1,0:T(8,128)}) custom-call(s32[3]{0:T(128)} %pad_add_fusion.core_ref.ids_ref, bf16[1024,4096]{1,0:T(8,128)(2,1)} %scen_ref.13, f32[1024,128]{1,0:T(8,128)} %norms.1.sq_ref, bf16[64,4096]{1,0:T(8,128)(2,1)} %copy-done.9, bf16[64,4096]{1,0:T(8,128)(2,1)} %copy-done.10, bf16[64,4096]{1,0:T(8,128)(2,1)} %copy-done.11, ...), custom_call_target="tpu_custom_call" | custom-call | flops 2147483648 | bytes 8388608 | tf_op jit(solution)/shard_map/cost_share/pallas_call | solution.py:89
  81.1 7.8 %cost_share.7 = (f32[512,256]{1,0:T(8,128)}, f32[512,256]{1,0:T(8,128)}) custom-call(s32[3]{0:T(128)} %pad_add_fusion.core_ref.ids_ref, bf16[1024,4096]{1,0:T(8,128)(2,1)} %scen_ref.13, f32[1024,128]{1,0:T(8,128)} %norms.1.sq_ref, bf16[64,4096]{1,0:T(8,128)(2,1)} %collective-permute-done.8.refs_0_, bf16[64,4096]{1,0:T(8,128)(2,1)} %collective-permute-done.9.refs_1_, ...), custom_call_target="tpu_custom_call" | custom-call | flops 2147483648 | bytes 8388608 | tf_op jit(solution)/shard_map/cost_share/pallas_call | solution.py:89
  89.7 0.8 copy-done.8
  90.5 7.8 %cost_share.8 = (f32[512,256]{1,0:T(8,128)}, f32[512,256]{1,0:T(8,128)}) custom-call(s32[3]{0:T(128)} %pad_add_fusion.core_ref.ids_ref, bf16[1024,4096]{1,0:T(8,128)(2,1)} %scen_ref.13, f32[1024,128]{1,0:T(8,128)} %norms.1.sq_ref, bf16[64,4096]{1,0:T(8,128)(2,1)} %copy-done.7, bf16[64,4096]{1,0:T(8,128)(2,1)} %collective-permute-done.15.refs_1_, ...), custom_call_target="tpu_custom_call" | custom-call | flops 2147483648 | bytes 8388608 | tf_op jit(solution)/shard_map/cost_share/pallas_call | solution.py:89
  98.9 1.9 collective-permute-start.21
  100.8 1.6 collective-permute-start.7
  102.4 1.1 add.94
  104.1 1.1 add.96
  105.2 1.6 collective-permute-start.19
  106.8 7.0 %cost_share.5 = (f32[512,128]{1,0:T(8,128)}, f32[512,128]{1,0:T(8,128)}) custom-call(s32[3]{0:T(128)} %pad_add_fusion.core_ref.ids_ref, bf16[1024,4096]{1,0:T(8,128)(2,1)} %scen_ref.13, f32[1024,128]{1,0:T(8,128)} %norms.1.sq_ref, bf16[64,4096]{1,0:T(8,128)(2,1)} %copy-done.4, bf16[64,4096]{1,0:T(8,128)(2,1)} %copy-done.3), custom_call_target="tpu_custom_call" | custom-call | flops 1073741824 | bytes 8388608 | tf_op jit(solution)/shard_map/cost_share/pallas_call | solution.py:89
  114.7 7.1 %cost_share.9 = (f32[512,128]{1,0:T(8,128)}, f32[512,128]{1,0:T(8,128)}) custom-call(s32[3]{0:T(128)} %pad_add_fusion.core_ref.ids_ref, bf16[1024,4096]{1,0:T(8,128)(2,1)} %scen_ref.13, f32[1024,128]{1,0:T(8,128)} %norms.1.sq_ref, bf16[64,4096]{1,0:T(8,128)(2,1)} %copy-done.15, bf16[64,4096]{1,0:T(8,128)(2,1)} %collective-permute-done.21.refs_1_), custom_call_target="tpu_custom_call" | custom-call | flops 1073741824 | bytes 8388608 | tf_op jit(solution)/shard_map/cost_share/pallas_call | solution.py:89
  121.8 1.0 add.90
  123.7 3.3 %collective-permute-done.13 = f32[512,256]{1,0:T(8,128)S(1)} collective-permute-done((f32[512,256]{1,0:T(8,128)S(1)}, f32[512,256]{1,0:T(8,128)S(1)}, u32[]{:S(2)}, u32[]{:S(2)}) %collective-permute-start.13) | collective-permute-done | bytes 524320 | tf_op jit(solution)/shard_map/ppermute | solution.py:248
  127.2 1.1 add.98
  128.3 1.6 collective-permute-start.23
  129.9 8.5 %collective-permute-done.19 = f32[512,256]{1,0:T(8,128)} collective-permute-done((f32[512,256]{1,0:T(8,128)S(1)}, f32[512,256]{1,0:T(8,128)}, u32[]{:S(2)}, u32[]{:S(2)}) %collective-permute-start.19) | collective-permute-done | bytes 524320 | tf_op jit(solution)/shard_map/ppermute | solution.py:248
  138.3 1.1 add.97.refs_3_
  139.5 4.3 %collective-permute-done.1 = f32[512,128]{1,0:T(8,128)S(1)} collective-permute-done((f32[512,128]{1,0:T(8,128)S(1)}, f32[512,128]{1,0:T(8,128)S(1)}, u32[]{:S(2)}, u32[]{:S(2)}) %collective-permute-start.1) | collective-permute-done | bytes 262176 | tf_op jit(solution)/shard_map/ppermute | solution.py:248
  144.0 4.0 %collective-permute-done.23 = f32[512,128]{1,0:T(8,128)S(1)} collective-permute-done((f32[512,128]{1,0:T(8,128)S(1)}, f32[512,128]{1,0:T(8,128)S(1)}, u32[]{:S(2)}, u32[]{:S(2)}) %collective-permute-start.23) | collective-permute-done | bytes 262176 | tf_op jit(solution)/shard_map/ppermute | solution.py:248
  148.2 1.5 collective-permute-done.28.refs_9_
  149.8 10.5 %first.1 = (f32[1024,1024]{1,0:T(8,128)}, f32[1024,128]{1,0:T(8,128)}, f32[8,8,128]{2,1,0:T(8,128)}) custom-call(s32[3]{0:T(128)} %pad_add_fusion.core_ref.ids_ref, f32[512,128]{1,0:T(8,128)} %copy-done.5, f32[512,256]{1,0:T(8,128)} %copy-done, f32[512,256]{1,0:T(8,128)} %copy-done.1, f32[512,256]{1,0:T(8,128)} %copy-done.2, f32[512,128]{1,0:T(8,128)} %copy-done.6, ...), custom_call_target="tpu_custom_call" | custom-call | tf_op jit(solution)/shard_map/first/pallas_call | solution.py:303
  160.3 4.8 %all-to-all-start = ((f32[8,8,128]{2,1,0:T(8,128)}), f32[8,8,128]{2,1,0:T(8,128)S(1)}, u32[]{:S(2)}, u32[]{:S(2)}) async-start(f32[8,8,128]{2,1,0:T(8,128)} %get-tuple-element.31), calls=%async_computation | async-start | bytes 65536 | tf_op jit(solution)/shard_map/all_to_all | solution.py:298
  165.4 6.4 %all-to-all-done.got_ref = f32[8,8,128]{2,1,0:T(8,128)S(1)} async-done(((f32[8,8,128]{2,1,0:T(8,128)}), f32[8,8,128]{2,1,0:T(8,128)S(1)}, u32[]{:S(2)}, u32[]{:S(2)}) %all-to-all-start) | async-done | bytes 32800 | tf_op jit(solution)/shard_map/all_to_all | solution.py:298
  172.4 6.0 %step.1 = f32[8,8,128]{2,1,0:T(8,128)} custom-call(s32[3]{0:T(128)} %pad_add_fusion.core_ref.ids_ref, f32[8,8,128]{2,1,0:T(8,128)} %copy-done.22, f32[1024,1024]{1,0:T(8,128)} %get-tuple-element.32.e_ref), custom_call_target="tpu_custom_call" | custom-call | tf_op jit(solution)/shard_map/step/pallas_call | solution.py:312
  178.5 3.3 %all-to-all-start.1 = ((f32[8,8,128]{2,1,0:T(8,128)}), f32[8,8,128]{2,1,0:T(8,128)S(1)}, u32[]{:S(2)}, u32[]{:S(2)}) async-start(f32[8,8,128]{2,1,0:T(8,128)} %step.1), calls=%async_computation.1 | async-start | bytes 65536 | tf_op jit(solution)/shard_map/all_to_all | solution.py:298
  181.9 6.6 %all-to-all-done.1.got_ref = f32[8,8,128]{2,1,0:T(8,128)S(1)} async-done(((f32[8,8,128]{2,1,0:T(8,128)}), f32[8,8,128]{2,1,0:T(8,128)S(1)}, u32[]{:S(2)}, u32[]{:S(2)}) %all-to-all-start.1) | async-done | bytes 32800 | tf_op jit(solution)/shard_map/all_to_all | solution.py:298
  189.1 7.8 %last.1 = (f32[8,8,128]{2,1,0:T(8,128)}, f32[8,128]{1,0:T(8,128)}, f32[1024,1024]{1,0:T(8,128)}) custom-call(s32[3]{0:T(128)} %pad_add_fusion.core_ref.ids_ref, f32[8,8,128]{2,1,0:T(8,128)} %copy-done.20, f32[1024,1024]{1,0:T(8,128)} %get-tuple-element.32.e_ref, f32[1024,128]{1,0:T(8,128)} %get-tuple-element.33.peak_ref), custom_call_target="tpu_custom_call" | custom-call | tf_op jit(solution)/shard_map/last/pallas_call | solution.py:319
  196.9 3.3 %all-to-all-start.2 = ((f32[8,8,128]{2,1,0:T(8,128)}), f32[8,8,128]{2,1,0:T(8,128)S(1)}, u32[]{:S(2)}, u32[]{:S(2)}) async-start(f32[8,8,128]{2,1,0:T(8,128)} %get-tuple-element.35), calls=%async_computation.2 | async-start | bytes 65536 | tf_op jit(solution)/shard_map/all_to_all | solution.py:298
  200.2 1.0 fusion.1.perm_ref
  201.2 5.7 %all-to-all-done.2.got_ref = f32[8,8,128]{2,1,0:T(8,128)S(1)} async-done(((f32[8,8,128]{2,1,0:T(8,128)}), f32[8,8,128]{2,1,0:T(8,128)S(1)}, u32[]{:S(2)}, u32[]{:S(2)}) %all-to-all-start.2) | async-done | bytes 32800 | tf_op jit(solution)/shard_map/all_to_all | solution.py:298
  207.4 4.0 %out.1 = (f32[1,256]{1,0:T(1,128)}, bf16[256,1024]{1,0:T(8,128)(2,1)}) custom-call(s32[3]{0:T(128)} %pad_add_fusion.core_ref.ids_ref, f32[8,8,128]{2,1,0:T(8,128)} %copy-done.21, f32[1024,1024]{1,0:T(8,128)} %get-tuple-element.36.scaled_ref, bf16[256,1024]{1,0:T(8,128)(2,1)} %fusion.1.perm_ref), custom_call_target="tpu_custom_call" | custom-call | tf_op jit(solution)/shard_map/out/pallas_call | solution.py:327
  (95 shorter events, 8.4 us)
Async XLA Ops:
  10.3 62.4 %copy-start.3 = (bf16[64,4096]{1,0:T(8,128)(2,1)}, bf16[64,4096]{1,0:T(8,128)(2,1)S(1)}, u32[]{:S(2)}) copy-start(bf16[64,4096]{1,0:T(8,128)(2,1)S(1)} %get-tuple-element.43.refs_1_) | copy-start | bytes 1572868
  10.3 62.4 %copy-start.4 = (bf16[64,4096]{1,0:T(8,128)(2,1)}, bf16[64,4096]{1,0:T(8,128)(2,1)S(1)}, u32[]{:S(2)}) copy-start(bf16[64,4096]{1,0:T(8,128)(2,1)S(1)} %get-tuple-element.44.refs_0_) | copy-start | bytes 1572868
  10.4 15.7 %collective-permute-start.2 = (bf16[64,4096]{1,0:T(8,128)(2,1)S(1)}, bf16[64,4096]{1,0:T(8,128)(2,1)S(1)}, u32[]{:S(2)}, u32[]{:S(2)}) collective-permute-start(bf16[64,4096]{1,0:T(8,128)(2,1)S(1)} %get-tuple-element.44.refs_0_), channel_id=1, source_target_pairs={{0,8},{8,16},{16,24},{24,28},{28,20},{20,12},{12,4},{4,0},{1,9},{9... | collective-permute-start | bytes 1572872 | tf_op jit(solution)/shard_map/ppermute | solution.py:266
  13.4 23.9 %collective-permute-start.3 = (bf16[64,4096]{1,0:T(8,128)(2,1)S(1)}, bf16[64,4096]{1,0:T(8,128)(2,1)S(1)}, u32[]{:S(2)}, u32[]{:S(2)}) collective-permute-start(bf16[64,4096]{1,0:T(8,128)(2,1)S(1)} %get-tuple-element.43.refs_1_), channel_id=1, source_target_pairs={{0,8},{8,16},{16,24},{24,28},{28,20},{20,12},{12,4},{4,0},{1,9},{9... | collective-permute-start | bytes 1572872 | tf_op jit(solution)/shard_map/ppermute | solution.py:266
  15.0 24.5 %collective-permute-start.4 = (bf16[64,4096]{1,0:T(8,128)(2,1)S(1)}, bf16[64,4096]{1,0:T(8,128)(2,1)S(1)}, u32[]{:S(2)}, u32[]{:S(2)}) collective-permute-start(bf16[64,4096]{1,0:T(8,128)(2,1)S(1)} %get-tuple-element.44.refs_0_), channel_id=1, source_target_pairs={{8,0},{16,8},{24,16},{28,24},{20,28},{12,20},{4,12},{0,4},{9,1},{1... | collective-permute-start | bytes 1572872 | tf_op jit(solution)/shard_map/ppermute | solution.py:267
  15.5 24.0 %collective-permute-start.5 = (bf16[64,4096]{1,0:T(8,128)(2,1)S(1)}, bf16[64,4096]{1,0:T(8,128)(2,1)S(1)}, u32[]{:S(2)}, u32[]{:S(2)}) collective-permute-start(bf16[64,4096]{1,0:T(8,128)(2,1)S(1)} %get-tuple-element.43.refs_1_), channel_id=1, source_target_pairs={{8,0},{16,8},{24,16},{28,24},{20,28},{12,20},{4,12},{0,4},{9,1},{1... | collective-permute-start | bytes 1572872 | tf_op jit(solution)/shard_map/ppermute | solution.py:267
  26.1 46.7 %copy-start.9 = (bf16[64,4096]{1,0:T(8,128)(2,1)}, bf16[64,4096]{1,0:T(8,128)(2,1)S(1)}, u32[]{:S(2)}) copy-start(bf16[64,4096]{1,0:T(8,128)(2,1)S(1)} %collective-permute-done.2.refs_0_) | copy-start | bytes 1572868
  26.1 22.6 %collective-permute-start.8 = (bf16[64,4096]{1,0:T(8,128)(2,1)S(1)}, bf16[64,4096]{1,0:T(8,128)(2,1)}, u32[]{:S(2)}, u32[]{:S(2)}) collective-permute-start(bf16[64,4096]{1,0:T(8,128)(2,1)S(1)} %collective-permute-done.2.refs_0_), channel_id=1, source_target_pairs={{0,8},{8,16},{16,24},{24,28},{28,20},{20,12},{12,4},{4,0},{1,9},{9... | collective-permute-start | bytes 1572872 | tf_op jit(solution)/shard_map/ppermute | solution.py:266
  37.3 35.4 %copy-start.10 = (bf16[64,4096]{1,0:T(8,128)(2,1)}, bf16[64,4096]{1,0:T(8,128)(2,1)S(1)}, u32[]{:S(2)}) copy-start(bf16[64,4096]{1,0:T(8,128)(2,1)S(1)} %collective-permute-done.3.refs_1_) | copy-start | bytes 1572868
  37.3 22.6 %collective-permute-start.9 = (bf16[64,4096]{1,0:T(8,128)(2,1)S(1)}, bf16[64,4096]{1,0:T(8,128)(2,1)}, u32[]{:S(2)}, u32[]{:S(2)}) collective-permute-start(bf16[64,4096]{1,0:T(8,128)(2,1)S(1)} %collective-permute-done.3.refs_1_), channel_id=1, source_target_pairs={{0,8},{8,16},{16,24},{24,28},{28,20},{20,12},{12,4},{4,0},{1,9},{9... | collective-permute-start | bytes 1572872 | tf_op jit(solution)/shard_map/ppermute | solution.py:266
  39.5 22.6 %copy-start.11 = (bf16[64,4096]{1,0:T(8,128)(2,1)}, bf16[64,4096]{1,0:T(8,128)(2,1)S(1)}, u32[]{:S(2)}) copy-start(bf16[64,4096]{1,0:T(8,128)(2,1)S(1)} %collective-permute-done.4.refs_2_) | copy-start | bytes 1572868
  39.5 22.6 %collective-permute-start.10 = (bf16[64,4096]{1,0:T(8,128)(2,1)S(1)}, bf16[64,4096]{1,0:T(8,128)(2,1)}, u32[]{:S(2)}, u32[]{:S(2)}) collective-permute-start(bf16[64,4096]{1,0:T(8,128)(2,1)S(1)} %collective-permute-done.4.refs_2_), channel_id=1, source_target_pairs={{8,0},{16,8},{24,16},{28,24},{20,28},{12,20},{4,12},{0,4},{9,1},{1... | collective-permute-start | bytes 1572872 | tf_op jit(solution)/shard_map/ppermute | solution.py:267
  39.5 22.7 %copy-start.12 = (bf16[64,4096]{1,0:T(8,128)(2,1)}, bf16[64,4096]{1,0:T(8,128)(2,1)S(1)}, u32[]{:S(2)}) copy-start(bf16[64,4096]{1,0:T(8,128)(2,1)S(1)} %collective-permute-done.5.refs_3_) | copy-start | bytes 1572868
  39.5 22.7 %collective-permute-start.11 = (bf16[64,4096]{1,0:T(8,128)(2,1)S(1)}, bf16[64,4096]{1,0:T(8,128)(2,1)}, u32[]{:S(2)}, u32[]{:S(2)}) collective-permute-start(bf16[64,4096]{1,0:T(8,128)(2,1)S(1)} %collective-permute-done.5.refs_3_), channel_id=1, source_target_pairs={{8,0},{16,8},{24,16},{28,24},{20,28},{12,20},{4,12},{0,4},{9,1},{1... | collective-permute-start | bytes 1572872 | tf_op jit(solution)/shard_map/ppermute | solution.py:267
  48.7 40.2 %collective-permute-start.14 = (bf16[64,4096]{1,0:T(8,128)(2,1)}, bf16[64,4096]{1,0:T(8,128)(2,1)S(1)}, u32[]{:S(2)}, u32[]{:S(2)}) collective-permute-start(bf16[64,4096]{1,0:T(8,128)(2,1)} %collective-permute-done.8.refs_0_), channel_id=1, source_target_pairs={{0,8},{8,16},{16,24},{24,28},{28,20},{20,12},{12,4},{4,0},{1,9},{9... | collective-permute-start | bytes 1572872 | tf_op jit(solution)/shard_map/ppermute | solution.py:266
  59.9 29.6 %collective-permute-start.15 = (bf16[64,4096]{1,0:T(8,128)(2,1)}, bf16[64,4096]{1,0:T(8,128)(2,1)}, u32[]{:S(2)}, u32[]{:S(2)}) collective-permute-start(bf16[64,4096]{1,0:T(8,128)(2,1)} %collective-permute-done.9.refs_1_), channel_id=1, source_target_pairs={{0,8},{8,16},{16,24},{24,28},{28,20},{20,12},{12,4},{4,0},{1,9},{9... | collective-permute-start | bytes 1572872 | tf_op jit(solution)/shard_map/ppermute | solution.py:266
  62.1 27.4 %collective-permute-start.16 = (bf16[64,4096]{1,0:T(8,128)(2,1)}, bf16[64,4096]{1,0:T(8,128)(2,1)}, u32[]{:S(2)}, u32[]{:S(2)}) collective-permute-start(bf16[64,4096]{1,0:T(8,128)(2,1)} %collective-permute-done.10.refs_2_), channel_id=1, source_target_pairs={{8,0},{16,8},{24,16},{28,24},{20,28},{12,20},{4,12},{0,4},{9,1},{1... | collective-permute-start | bytes 1572872 | tf_op jit(solution)/shard_map/ppermute | solution.py:267
  62.2 27.3 %collective-permute-start.17 = (bf16[64,4096]{1,0:T(8,128)(2,1)}, bf16[64,4096]{1,0:T(8,128)(2,1)S(1)}, u32[]{:S(2)}, u32[]{:S(2)}) collective-permute-start(bf16[64,4096]{1,0:T(8,128)(2,1)} %collective-permute-done.11.refs_3_), channel_id=1, source_target_pairs={{8,0},{16,8},{24,16},{28,24},{20,28},{12,20},{4,12},{0,4},{9,1},{1... | collective-permute-start | bytes 1572872 | tf_op jit(solution)/shard_map/ppermute | solution.py:267
  81.1 19.7 %collective-permute-start.6 = (f32[512,256]{1,0:T(8,128)}, f32[512,256]{1,0:T(8,128)S(1)}, u32[]{:S(2)}, u32[]{:S(2)}) collective-permute-start(f32[512,256]{1,0:T(8,128)} %get-tuple-element.24), channel_id=1, source_target_pairs={{0,1},{1,0},{2,3},{3,2},{4,5},{5,4},{6,7},{7,6},{8,9},{9,8},{10,11... | collective-permute-start | bytes 1572872 | tf_op jit(solution)/shard_map/ppermute | solution.py:248
  88.9 11.9 %copy-start.17 = (f32[512,256]{1,0:T(8,128)S(1)}, f32[512,256]{1,0:T(8,128)}, u32[]{:S(2)}) copy-start(f32[512,256]{1,0:T(8,128)} %get-tuple-element.23) | copy-start | bytes 1572868
  88.9 13.6 %copy-start.16 = (f32[512,256]{1,0:T(8,128)S(1)}, f32[512,256]{1,0:T(8,128)}, u32[]{:S(2)}) copy-start(f32[512,256]{1,0:T(8,128)} %get-tuple-element.25) | copy-start | bytes 1572868
  88.9 13.5 %collective-permute-start.12 = (f32[512,256]{1,0:T(8,128)}, f32[512,256]{1,0:T(8,128)}, u32[]{:S(2)}, u32[]{:S(2)}) collective-permute-start(f32[512,256]{1,0:T(8,128)} %get-tuple-element.26), channel_id=1, source_target_pairs={{0,1},{1,0},{2,3},{3,2},{4,5},{5,4},{6,7},{7,6},{8,9},{9,8},{10,11... | collective-permute-start | bytes 1572872 | tf_op jit(solution)/shard_map/ppermute | solution.py:248
  98.2 5.9 %collective-permute-start.18 = (f32[512,256]{1,0:T(8,128)}, f32[512,256]{1,0:T(8,128)S(1)}, u32[]{:S(2)}, u32[]{:S(2)}) collective-permute-start(f32[512,256]{1,0:T(8,128)} %get-tuple-element.28), channel_id=1, source_target_pairs={{0,1},{1,0},{2,3},{3,2},{4,5},{5,4},{6,7},{7,6},{8,9},{9,8},{10,11... | collective-permute-start | bytes 1572872 | tf_op jit(solution)/shard_map/ppermute | solution.py:248
  98.7 15.1 %collective-permute-start.20 = (bf16[64,4096]{1,0:T(8,128)(2,1)}, bf16[64,4096]{1,0:T(8,128)(2,1)S(1)}, u32[]{:S(2)}, u32[]{:S(2)}) collective-permute-start(bf16[64,4096]{1,0:T(8,128)(2,1)} %copy-done.7), channel_id=1, source_target_pairs={{0,8},{8,16},{16,24},{24,28},{28,20},{20,12},{12,4},{4,0},{1,9},{9... | collective-permute-start | bytes 1572872 | tf_op jit(solution)/shard_map/ppermute | solution.py:266
  98.9 15.1 %collective-permute-start.21 = (bf16[64,4096]{1,0:T(8,128)(2,1)}, bf16[64,4096]{1,0:T(8,128)(2,1)}, u32[]{:S(2)}, u32[]{:S(2)}) collective-permute-start(bf16[64,4096]{1,0:T(8,128)(2,1)} %copy-done.8), channel_id=1, source_target_pairs={{8,0},{16,8},{24,16},{28,24},{20,28},{12,20},{4,12},{0,4},{9,1},{1... | collective-permute-start | bytes 1572872 | tf_op jit(solution)/shard_map/ppermute | solution.py:267
  100.8 22.5 %collective-permute-start.7 = (f32[512,256]{1,0:T(8,128)S(1)}, f32[512,256]{1,0:T(8,128)S(1)}, u32[]{:S(2)}, u32[]{:S(2)}) collective-permute-start(f32[512,256]{1,0:T(8,128)S(1)} %add.92), channel_id=1, source_target_pairs={{0,2},{1,3},{2,0},{3,1},{4,6},{5,7},{6,4},{7,5},{8,10},{9,11},{10,... | collective-permute-start | bytes 1572872 | tf_op jit(solution)/shard_map/ppermute | solution.py:248
  103.6 23.4 %collective-permute-start.13 = (f32[512,256]{1,0:T(8,128)S(1)}, f32[512,256]{1,0:T(8,128)S(1)}, u32[]{:S(2)}, u32[]{:S(2)}) collective-permute-start(f32[512,256]{1,0:T(8,128)S(1)} %add.94), channel_id=1, source_target_pairs={{0,2},{1,3},{2,0},{3,1},{4,6},{5,7},{6,4},{7,5},{8,10},{9,11},{10,... | collective-permute-start | bytes 1572872 | tf_op jit(solution)/shard_map/ppermute | solution.py:248
  105.2 33.1 %collective-permute-start.19 = (f32[512,256]{1,0:T(8,128)S(1)}, f32[512,256]{1,0:T(8,128)}, u32[]{:S(2)}, u32[]{:S(2)}) collective-permute-start(f32[512,256]{1,0:T(8,128)S(1)} %add.96), channel_id=1, source_target_pairs={{0,2},{1,3},{2,0},{3,1},{4,6},{5,7},{6,4},{7,5},{8,10},{9,11},{10,... | collective-permute-start | bytes 1572872 | tf_op jit(solution)/shard_map/ppermute | solution.py:248
  113.9 7.9 %copy-start.19 = (f32[512,128]{1,0:T(8,128)S(1)}, f32[512,128]{1,0:T(8,128)}, u32[]{:S(2)}) copy-start(f32[512,128]{1,0:T(8,128)} %get-tuple-element.21) | copy-start | bytes 786436
  113.9 7.9 %collective-permute-start = (f32[512,128]{1,0:T(8,128)}, f32[512,128]{1,0:T(8,128)}, u32[]{:S(2)}, u32[]{:S(2)}) collective-permute-start(f32[512,128]{1,0:T(8,128)} %get-tuple-element.22), channel_id=1, source_target_pairs={{0,1},{1,0},{2,3},{3,2},{4,5},{5,4},{6,7},{7,6},{8,9},{9,8},{10,11... | collective-permute-start | bytes 786440 | tf_op jit(solution)/shard_map/ppermute | solution.py:248
  121.8 26.3 %copy-start.23 = (s32[1024]{0:T(1024)S(1)}, s32[1024]{0:T(1024)}, u32[]{:S(2)}) copy-start(s32[1024]{0:T(1024)} %param.3) | copy-start | bytes 12292
  121.8 5.4 %collective-permute-start.22 = (f32[512,128]{1,0:T(8,128)}, f32[512,128]{1,0:T(8,128)S(1)}, u32[]{:S(2)}, u32[]{:S(2)}) collective-permute-start(f32[512,128]{1,0:T(8,128)} %get-tuple-element.30), channel_id=1, source_target_pairs={{0,1},{1,0},{2,3},{3,2},{4,5},{5,4},{6,7},{7,6},{8,9},{9,8},{10,11... | collective-permute-start | bytes 786440 | tf_op jit(solution)/shard_map/ppermute | solution.py:248
  122.8 21.1 %collective-permute-start.1 = (f32[512,128]{1,0:T(8,128)S(1)}, f32[512,128]{1,0:T(8,128)S(1)}, u32[]{:S(2)}, u32[]{:S(2)}) collective-permute-start(f32[512,128]{1,0:T(8,128)S(1)} %add.90), channel_id=1, source_target_pairs={{0,2},{1,3},{2,0},{3,1},{4,6},{5,7},{6,4},{7,5},{8,10},{9,11},{10,... | collective-permute-start | bytes 786440 | tf_op jit(solution)/shard_map/ppermute | solution.py:248
  123.4 26.3 %copy-start = (f32[512,256]{1,0:T(8,128)}, f32[512,256]{1,0:T(8,128)S(1)}, u32[]{:S(2)}) copy-start(f32[512,256]{1,0:T(8,128)S(1)} %add.93.refs_1_) | copy-start | bytes 1572868
  123.4 24.8 %collective-permute-start.25 = (f32[512,256]{1,0:T(8,128)S(1)}, f32[512,256]{1,0:T(8,128)S(1)}, u32[]{:S(2)}, u32[]{:S(2)}) collective-permute-start(f32[512,256]{1,0:T(8,128)S(1)} %add.93.refs_1_), channel_id=1, source_target_pairs={{0,1},{1,0},{2,3},{3,2},{4,5},{5,4},{6,7},{7,6},{8,9},{9,8},{10,11... | collective-permute-start | bytes 1572872 | tf_op jit(solution)/shard_map/ppermute | solution.py:248
  127.1 22.7 %copy-start.1 = (f32[512,256]{1,0:T(8,128)}, f32[512,256]{1,0:T(8,128)S(1)}, u32[]{:S(2)}) copy-start(f32[512,256]{1,0:T(8,128)S(1)} %add.95.refs_2_) | copy-start | bytes 1572868
  127.1 21.1 %collective-permute-start.26 = (f32[512,256]{1,0:T(8,128)S(1)}, f32[512,256]{1,0:T(8,128)S(1)}, u32[]{:S(2)}, u32[]{:S(2)}) collective-permute-start(f32[512,256]{1,0:T(8,128)S(1)} %add.95.refs_2_), channel_id=1, source_target_pairs={{0,1},{1,0},{2,3},{3,2},{4,5},{5,4},{6,7},{7,6},{8,9},{9,8},{10,11... | collective-permute-start | bytes 1572872 | tf_op jit(solution)/shard_map/ppermute | solution.py:248
  128.3 19.7 %collective-permute-start.23 = (f32[512,128]{1,0:T(8,128)S(1)}, f32[512,128]{1,0:T(8,128)S(1)}, u32[]{:S(2)}, u32[]{:S(2)}) collective-permute-start(f32[512,128]{1,0:T(8,128)S(1)} %add.98), channel_id=1, source_target_pairs={{0,2},{1,3},{2,0},{3,1},{4,6},{5,7},{6,4},{7,5},{8,10},{9,11},{10,... | collective-permute-start | bytes 786440 | tf_op jit(solution)/shard_map/ppermute | solution.py:248
  139.5 10.3 %copy-start.2 = (f32[512,256]{1,0:T(8,128)}, f32[512,256]{1,0:T(8,128)S(1)}, u32[]{:S(2)}) copy-start(f32[512,256]{1,0:T(8,128)S(1)} %add.97.refs_3_) | copy-start | bytes 1572868
  139.5 10.3 %collective-permute-start.27 = (f32[512,256]{1,0:T(8,128)S(1)}, f32[512,256]{1,0:T(8,128)}, u32[]{:S(2)}, u32[]{:S(2)}) collective-permute-start(f32[512,256]{1,0:T(8,128)S(1)} %add.97.refs_3_), channel_id=1, source_target_pairs={{0,1},{1,0},{2,3},{3,2},{4,5},{5,4},{6,7},{7,6},{8,9},{9,8},{10,11... | collective-permute-start | bytes 1572872 | tf_op jit(solution)/shard_map/ppermute | solution.py:248
  143.9 5.9 %copy-start.5 = (f32[512,128]{1,0:T(8,128)}, f32[512,128]{1,0:T(8,128)S(1)}, u32[]{:S(2)}) copy-start(f32[512,128]{1,0:T(8,128)S(1)} %add.91.refs_0_) | copy-start | bytes 786436
  143.9 4.3 %collective-permute-start.24 = (f32[512,128]{1,0:T(8,128)S(1)}, f32[512,128]{1,0:T(8,128)S(1)}, u32[]{:S(2)}, u32[]{:S(2)}) collective-permute-start(f32[512,128]{1,0:T(8,128)S(1)} %add.91.refs_0_), channel_id=1, source_target_pairs={{0,1},{1,0},{2,3},{3,2},{4,5},{5,4},{6,7},{7,6},{8,9},{9,8},{10,11... | collective-permute-start | bytes 786440 | tf_op jit(solution)/shard_map/ppermute | solution.py:248
  148.0 1.8 copy-start.6
  148.0 1.7 collective-permute-start.28
  148.2 1.6 copy-start.13
  160.3 11.5 %all-to-all-start = ((f32[8,8,128]{2,1,0:T(8,128)}), f32[8,8,128]{2,1,0:T(8,128)S(1)}, u32[]{:S(2)}, u32[]{:S(2)}) async-start(f32[8,8,128]{2,1,0:T(8,128)} %get-tuple-element.31), calls=%async_computation | async-start | bytes 65536 | tf_op jit(solution)/shard_map/all_to_all | solution.py:298
  178.5 10.0 %all-to-all-start.1 = ((f32[8,8,128]{2,1,0:T(8,128)}), f32[8,8,128]{2,1,0:T(8,128)S(1)}, u32[]{:S(2)}, u32[]{:S(2)}) async-start(f32[8,8,128]{2,1,0:T(8,128)} %step.1), calls=%async_computation.1 | async-start | bytes 65536 | tf_op jit(solution)/shard_map/all_to_all | solution.py:298
  196.9 10.0 %all-to-all-start.2 = ((f32[8,8,128]{2,1,0:T(8,128)}), f32[8,8,128]{2,1,0:T(8,128)S(1)}, u32[]{:S(2)}, u32[]{:S(2)}) async-start(f32[8,8,128]{2,1,0:T(8,128)} %get-tuple-element.35), calls=%async_computation.2 | async-start | bytes 65536 | tf_op jit(solution)/shard_map/all_to_all | solution.py:298
  (8 other events, 7.4 us)

commit v2 on v1

v2 whole, which is shorter than its diff:
```python
import functools
import math

import jax
import jax.numpy as jnp
from jax import lax
from jax.experimental import pallas as pl
from jax.experimental.pallas import tpu as pltpu
from jax.sharding import PartitionSpec as P

ITERS = 3
eps_blur = 0.1

LANES = 128
SUB = 8
NT = (((1,), (1,)), ((), ()))
VMEM = pl.BlockSpec(memory_space=pltpu.VMEM)
SMEM = pl.BlockSpec(memory_space=pltpu.SMEM)
ROOM = pltpu.CompilerParams(vmem_limit_bytes=10 * 2**20)


def kept(*xs):
    return [pltpu.with_memory_space_constraint(x, pltpu.VMEM) for x in xs]


def square_sums(x):
    gram = lax.dot_general(x, x, NT, preferred_element_type=jnp.float32)
    n = x.shape[0]
    eye = lax.broadcasted_iota(jnp.int32, (n, n), 0) == lax.broadcasted_iota(jnp.int32, (n, n), 1)
    return jnp.sum(jnp.where(eye, gram, 0.0), axis=0, keepdims=True)


def pick_kernel(sel_ref, scen_ref, low_ref, high_ref, *, step):
    half = low_ref.shape[0]
    for at in range(0, scen_ref.shape[1], step):
        cols = slice(at, at + step)
        rows = jnp.dot(sel_ref[...], scen_ref[:, cols], preferred_element_type=jnp.float32)
        low_ref[:, cols] = rows[:half].astype(low_ref.dtype)
        high_ref[:, cols] = rows[half:].astype(high_ref.dtype)


def pick(sel, scenarios):
    rows, width = sel.shape[0], scenarios.shape[1]
    return pl.pallas_call(
        functools.partial(pick_kernel, step=min(512, width)),
        out_shape=(pltpu.VMEM((rows // 2, width), scenarios.dtype),) * 2,
        in_specs=[VMEM] * 2,
        out_specs=(VMEM, VMEM),
        cost_estimate=pl.CostEstimate(
            flops=2 * rows * scenarios.size, bytes_accessed=2 * scenarios.size, transcendentals=0
        ),
        compiler_params=ROOM,
        name="pick",
    )(*kept(sel, scenarios))


def norm_kernel(scen_ref, out_ref):
    def body(i, carry):
        rows = pl.ds(pl.multiple_of(i * 16, 16), 16)
        x = scen_ref[rows, :].astype(jnp.float32)
        out_ref[rows, :] = jnp.broadcast_to(jnp.sum(x * x, axis=1, keepdims=True), (16, LANES))
        return carry

    lax.fori_loop(0, scen_ref.shape[0] // 16, body, 0, unroll=2)


def norms(scenarios):
    return pl.pallas_call(
        norm_kernel,
        out_shape=pltpu.VMEM((scenarios.shape[0], LANES), jnp.float32),
        in_specs=[VMEM],
        out_specs=VMEM,
        cost_estimate=pl.CostEstimate(
            flops=2 * scenarios.size, bytes_accessed=2 * scenarios.size, transcendentals=0
        ),
        compiler_params=ROOM,
        name="norms",
    )(*kept(scenarios))


def cost_kernel(core_ref, scen_ref, sq_ref, *refs, tile, merge):
    *refs, send_ref, keep_ref = refs
    chunks, before = (refs[:-2], refs[-2:]) if merge else (refs, (None, None))
    reps = jnp.concatenate([c[...] for c in chunks], axis=0)
    sq_rep = square_sums(reps)
    half = send_ref.shape[0]
    core = core_ref[0]
    cols = reps.shape[0]
    first = lax.broadcasted_iota(jnp.int32, (tile, cols), 1) < cols // 2
    for out_ref, old_ref, which in ((send_ref, before[0], 1 - core), (keep_ref, before[1], core)):
        for at in range(0, half, tile):
            rows = pl.ds(pl.multiple_of(which * half + at, tile), tile)
            cross = lax.dot_general(scen_ref[rows, :], reps, NT, preferred_element_type=jnp.float32)
            new = sq_rep + sq_ref[rows, 0:1] - 2.0 * cross
            if merge:
                old = old_ref[at : at + tile, :]
                out_ref[at : at + tile, :cols] = jnp.where(first, old, new)
                out_ref[at : at + tile, cols:] = jnp.where(first, new, old)
            else:
                out_ref[at : at + tile, :] = new


def cost_share(core, scenarios, sq_scen, chunks, before=()):
    rows, width = scenarios.shape
    cols = sum(c.shape[0] for c in chunks)
    half = pltpu.VMEM((rows // 2, cols * (2 if before else 1)), jnp.float32)
    return pl.pallas_call(
        functools.partial(cost_kernel, tile=min(256, rows // 2), merge=bool(before)),
        out_shape=(half, half),
        in_specs=[SMEM] + [VMEM] * (2 + len(chunks) + len(before)),
        out_specs=(VMEM, VMEM),
        cost_estimate=pl.CostEstimate(
            flops=2 * rows * cols * width, bytes_accessed=2 * rows * width, transcendentals=0
        ),
        compiler_params=ROOM,
        name="cost_share",
    )(core, *kept(scenarios, sq_scen, *chunks, *before))


def tree(op, xs):
    while len(xs) > 1:
        xs = [op(*xs[i : i + 2]) if i + 1 < len(xs) else xs[i] for i in range(0, len(xs), 2)]
    return xs[0]


def put_sums(acc, out_ref, shift):
    at = lax.broadcasted_iota(jnp.int32, (len(acc), LANES), 0)
    total = jnp.zeros((len(acc), LANES), jnp.float32)
    for i, a in enumerate(acc):
        total = jnp.where(at == i, jnp.sum(a, axis=0, keepdims=True), total)
    if shift is not None:
        total = pltpu.roll(total, shift, 0)
    for k in range(out_ref.shape[0]):
        out_ref[k] = total


def get_factors(got_ref, scale, shift):
    total = tree(jnp.add, [got_ref[k] for k in range(got_ref.shape[0])])
    if shift is not None:
        total = pltpu.roll(total, shift, 0)
    return scale / total


def spread(w):
    return [jnp.broadcast_to(w[i : i + 1, :], (SUB, LANES)) for i in range(w.shape[0])]


GROUP = 8


def load(ref, rows):
    return [ref[rows, k * LANES : (k + 1) * LANES] for k in range(ref.shape[1] // LANES)]


def store(ref, rows, tiles):
    for k, x in enumerate(tiles):
        ref[rows, k * LANES : (k + 1) * LANES] = x


def group_rows(i, g, base=0):
    return pl.ds(pl.multiple_of(base + (i * GROUP + g) * SUB, SUB), SUB)


def first_kernel(ids_ref, *refs, pieces, scale, rolled):
    stages = len(refs) // 2 - 1
    mine, other = refs[:stages], refs[stages : 2 * stages]
    e_ref, peak_ref, out_ref = refs[2 * stages :]
    half = mine[0].shape[0]
    core = ids_ref[0]
    left = lax.broadcasted_iota(jnp.int32, (SUB, LANES), 1) < LANES // 2

    def body(i, acc, h):
        peaks, sums = [], []
        for g in range(GROUP):
            src = group_rows(i, g)
            z = []
            for piece in pieces:
                part = [
                    jnp.where(core == h, mine[s][src, at : at + LANES], other[s][src, at : at + LANES])
                    for s, at in piece
                ]
                part = part[0] if len(part) == 1 else jnp.where(left, part[0], part[1])
                z.append(part * scale)
            store(e_ref, group_rows(i, g, h * half), z)
            peaks.append(tree(jnp.maximum, z))
        peaks = [jnp.max(p, axis=1, keepdims=True) for p in peaks]
        for g in range(GROUP):
            dst = group_rows(i, g, h * half)
            e = [jnp.exp2(x - peaks[g]) for x in load(e_ref, dst)]
            store(e_ref, dst, e)
            peak_ref[dst, :] = jnp.broadcast_to(peaks[g], (SUB, LANES))
            sums.append(tree(jnp.add, e))
        sums = [1.0 / jnp.sum(x, axis=1, keepdims=True) for x in sums]
        for g in range(GROUP):
            acc = [a + x * sums[g] for a, x in zip(acc, load(e_ref, group_rows(i, g, h * half)))]
        return tuple(acc)

    acc = tuple(jnp.zeros((SUB, LANES), jnp.float32) for _ in pieces)
    for h in range(2):
        acc = lax.fori_loop(0, half // (GROUP * SUB), functools.partial(body, h=h), acc)
    put_sums(acc, out_ref, ids_ref[1] if rolled else None)


def step_kernel(ids_ref, got_ref, e_ref, out_ref, *, scale, rolled):
    tiles = e_ref.shape[1] // LANES
    w = spread(get_factors(got_ref, scale, ids_ref[2] if rolled else None))

    def body(i, acc):
        sums = [tree(jnp.add, [x * f for x, f in zip(load(e_ref, group_rows(i, g)), w)]) for g in range(GROUP)]
        sums = [1.0 / jnp.sum(x, axis=1, keepdims=True) for x in sums]
        for g in range(GROUP):
            acc = [a + x * sums[g] for a, x in zip(acc, load(e_ref, group_rows(i, g)))]
        return tuple(acc)

    acc = tuple(jnp.zeros((SUB, LANES), jnp.float32) for _ in range(tiles))
    acc = lax.fori_loop(0, e_ref.shape[0] // (GROUP * SUB), body, acc)
    put_sums(acc, out_ref, ids_ref[1] if rolled else None)


def last_kernel(ids_ref, got_ref, e_ref, peak_ref, out_ref, pot_ref, scaled_ref, col_ref, *, scale, rolled, log_count):
    rows_all = e_ref.shape[0]
    tiles = e_ref.shape[1] // LANES
    w = spread(get_factors(got_ref, scale, ids_ref[2] if rolled else None))

    def body(i, acc):
        sums = [tree(jnp.add, [x * f for x, f in zip(load(e_ref, group_rows(i, g)), w)]) for g in range(GROUP)]
        sums = [jnp.sum(x, axis=1, keepdims=True) for x in sums]
        for g in range(GROUP):
            rows = group_rows(i, g)
            col_ref[rows, :] = -eps_blur * (log_count + math.log(2) * peak_ref[rows, :] + jnp.log(sums[g]))
            q = 1.0 / sums[g]
            e = [x * q for x in load(e_ref, rows)]
            store(scaled_ref, rows, e)
            acc = [a + x for a, x in zip(acc, e)]
        return tuple(acc)

    acc = tuple(jnp.zeros((SUB, LANES), jnp.float32) for _ in range(tiles))
    acc = lax.fori_loop(0, rows_all // (GROUP * SUB), body, acc)
    put_sums(acc, out_ref, ids_ref[1] if rolled else None)
    for i in range(rows_all // LANES):
        block = col_ref[i * LANES : (i + 1) * LANES, :]
        pot_ref[i : i + 1, :] = jnp.transpose(block)[0:1, :]


def out_kernel(ids_ref, got_ref, scaled_ref, perm_ref, pot_ref, member_ref, *, scale, rolled):
    tiles = scaled_ref.shape[1] // LANES
    factors = get_factors(got_ref, scale, ids_ref[2] if rolled else None)
    w = jnp.concatenate([factors[i : i + 1, :] for i in range(tiles)], axis=1)
    v = eps_blur * jnp.log(w)
    high = v.astype(jnp.bfloat16).astype(jnp.float32)
    mid = (v - high).astype(jnp.bfloat16).astype(jnp.float32)
    low = v - high - mid
    at = lax.broadcasted_iota(jnp.int32, (16, w.shape[1]), 0)
    parts = jnp.where(at == 0, high, jnp.where(at == 1, mid, jnp.where(at == 2, low, 0.0)))
    moved = lax.dot_general(
        parts.astype(jnp.bfloat16), perm_ref[...], NT, preferred_element_type=jnp.float32
    )
    pot_ref[...] = moved[0:1, :] + moved[1:2, :] + moved[2:3, :]
    step = min(256, scaled_ref.shape[0])
    for i in range(0, scaled_ref.shape[0], step):
        plan = (scaled_ref[i : i + step, :] * w).astype(jnp.bfloat16)
        member_ref[:, i : i + step] = lax.dot_general(
            perm_ref[...], plan, NT, preferred_element_type=jnp.float32
        ).astype(member_ref.dtype)


def on_device(scenarios, rep_index):
    scen_rows, width = scenarios.shape
    n = lax.axis_size("scen")
    n_rep = lax.axis_size("rep")
    count_r = rep_index.shape[0]
    count_s = scen_rows * n
    per = count_r // n
    features = width * n_rep
    rows_out = count_r // n_rep
    rolled = per == LANES
    as_int = lambda x: x.astype(jnp.int32)

    def tied(xs, *after):
        return list(lax.optimization_barrier((tuple(xs), after))[0])

    ring = list(range(0, n, 2)) + list(range(n - 1, 0, -2))
    up = [(ring[i], ring[(i + 1) % n]) for i in range(n)]
    down = [(b, a) for a, b in up]
    at_ring = [ring.index(i) for i in range(n)]

    d = lax.axis_index("scen")
    rep = lax.axis_index("rep")
    place = jnp.where((d & 1) == 0, d >> 1, n - 1 - (d >> 1))
    back = jnp.where(place == 0, 0, n - place)
    scalars = tuple(x.astype(jnp.int32) for x in (rep & 1, place, back, d * scen_rows, rep * rows_out))
    rep_index, *scalars = tied([rep_index, *scalars])
    core, place, back, scen_from, out_from = scalars
    ids = jnp.stack([core, place, back])
    wanted = lax.dynamic_slice_in_dim(rep_index, out_from, rows_out)
    rep_index, ids, wanted, place, scen_from = tied([rep_index, ids, wanted, place, scen_from])

    local = rep_index - scen_from
    i_scen = jnp.arange(scen_rows, dtype=jnp.int32)
    chosen = jnp.sum(as_int(local[:, None] == i_scen[None, :]), axis=0)
    before = jnp.sum(as_int((local[:, None] >= 0) & (local[:, None] < i_scen[None, :])), axis=0)
    key = jnp.where(chosen > 0, before, -1)
    sel = (key[None, :] == jnp.arange(per, dtype=jnp.int32)[:, None]).astype(scenarios.dtype)
    halves = list(pick(sel, scenarios))

    rank = jnp.sum(as_int(rep_index[None, :] < wanted[:, None]), axis=1)
    block = rank // per
    at = sum(jnp.where(block == i, at_ring[i], 0) for i in range(n)) - place
    at = jnp.where(at < 0, at + n, at) * per + rank % per
    perm = (at[:, None] == jnp.arange(count_r, dtype=jnp.int32)[None, :]).astype(jnp.bfloat16)

    def swap(x, bit):
        return lax.ppermute(x, "rep", [(i, i ^ bit) for i in range(n_rep)])

    def rest(part):
        bit = 2
        while bit < n_rep:
            part = part + swap(part, bit)
            bit *= 2
        return part

    stages = []
    where = [None] * n

    def finish(send, keep):
        part = keep + swap(send, 1)
        whole = rest(part)
        other = swap(whole, 1)
        stages.append((whole, other))
        return part, whole, other

    sq_scen = norms(scenarios)
    shares = cost_share(ids, scenarios, sq_scen, halves)
    ties = {1: [*shares, perm], 2: [], 3: [], 4: []}
    part, whole, other = finish(*shares)
    ties[2] += [part]
    ties[4] += [whole]
    where[0] = [(0, 0)]
    a, b = halves, halves[::-1]
    for h in range(1, n):
        i, k = (h + 1) % 2, (h + 1) // 2
        x = lax.ppermute(a[i], "scen", up)
        y = lax.ppermute(b[i], "scen", down)
        x, y = tied([x, y], *ties.pop(h, []))
        if i == 0:
            a, b = [x, a[1]], [y, b[1]]
            shares = cost_share(ids, scenarios, sq_scen, [x, y])
        else:
            a, b = [a[0], x], [b[0], y]
            joined = h < n - 3
            shares = cost_share(ids, scenarios, sq_scen, [y, x], shares if joined else ())
        ties.setdefault(h + 1, []).extend(shares)
        if i == 1 or h >= n - 3:
            part, whole, other = finish(*shares)
            ties.setdefault(h + 2, []).append(part)
            ties.setdefault(h + 4, []).append(whole)
            ties.setdefault(h + 5, []).append(other)
            s = len(stages) - 1
            if h == n - 1:
                where[k] = [(s, 0)]
            elif i == 1 and h < n - 3:
                where[n - k], where[k] = [(s, 0)], [(s, per)]
            elif i == 1:
                where[n - k], where[k] = [(s - 1, 0), (s, 0)], [(s, 0), (s - 1, 0)]

    own, other = [s[0] for s in stages], [s[1] for s in stages]
    if not rolled:

        def join(xs):
            cols = []
            for piece in where:
                part = [xs[s][:, at : at + per] for s, at in piece]
                cols += part if len(part) == 1 else [part[0][:, : per // 2], part[1][:, per // 2 :]]
            return [jnp.concatenate(cols, axis=1)]

        own, other = join(own), join(other)
        pieces = [[(0, i * LANES)] for i in range(count_r // LANES)]
    else:
        pieces = where

    f32 = lambda *shape: pltpu.VMEM(shape, jnp.float32)
    tiles = count_r // LANES
    sums = f32(n, tiles, LANES)

    def exchange(x):
        if not rolled:
            x = jnp.roll(x.reshape(n, count_r), place * per, axis=1).reshape(x.shape)
        x = lax.all_to_all(x, "scen", 0, 0, tiled=False)
        if not rolled:
            x = jnp.roll(x.reshape(n, count_r), -place * per, axis=1).reshape(x.shape)
        return x

    e, peak, x = pl.pallas_call(
        functools.partial(first_kernel, pieces=pieces, scale=-1.0 / (features * eps_blur * math.log(2)), rolled=rolled),
        out_shape=(f32(scen_rows, count_r), f32(scen_rows, LANES), sums),
        in_specs=[SMEM] + [VMEM] * (2 * len(own)),
        out_specs=(VMEM,) * 3,
        compiler_params=ROOM,
        name="first",
    )(ids, *kept(*own, *other))
    scale = count_s / count_r
    for _ in range(ITERS - 2):
        x = pl.pallas_call(
            functools.partial(step_kernel, scale=scale, rolled=rolled),
            out_shape=sums,
            in_specs=[SMEM, VMEM, VMEM],
            out_specs=VMEM,
            compiler_params=ROOM,
            name="step",
        )(ids, *kept(exchange(x), e))
    x, scen_pot, scaled = pl.pallas_call(
        functools.partial(last_kernel, scale=scale, rolled=rolled, log_count=math.log(count_s)),
        out_shape=(
            sums,
            jax.ShapeDtypeStruct((scen_rows // LANES, LANES), jnp.float32),
            f32(scen_rows, count_r),
        ),
        in_specs=[SMEM] + [VMEM] * 3,
        out_specs=(VMEM,) * 3,
        scratch_shapes=[pltpu.VMEM((scen_rows, LANES), jnp.float32)],
        compiler_params=ROOM,
        name="last",
    )(ids, *kept(exchange(x), e, peak))
    rep_pot, member = pl.pallas_call(
        functools.partial(out_kernel, scale=scale, rolled=rolled),
        out_shape=(
            jax.ShapeDtypeStruct((1, rows_out), jnp.float32),
            jax.ShapeDtypeStruct((rows_out, scen_rows), jnp.bfloat16),
        ),
        in_specs=[SMEM] + [VMEM] * 3,
        out_specs=(VMEM, VMEM),
        compiler_params=ROOM,
        name="out",
    )(ids, *kept(exchange(x), scaled, perm))
    return scen_pot.reshape(scen_rows), rep_pot.reshape(rows_out), member


def solution(mesh):
    return jax.shard_map(
        on_device,
        mesh=mesh,
        in_specs=(P("scen", "rep"), P()),
        out_specs=(P("scen"), P("rep"), P("rep", "scen")),
        check_vma=False,
    )
```

time: 212 us -> 161 us (0.76)
  Pallas kernels: 80.2 us -> 43.9 us
  blocking collectives: 0 us -> 28.4 us
  waiting for transfers between devices: 76.5 us -> 54.7 us
  starting transfers between devices: 38.7 us -> 25.6 us
  other arithmetic: 10.1 us -> 2.93 us
    all_to_all x0 -> x3, blocking collectives: none -> 28.4 us  [exchange(): x = lax.all_to_all(x, 'scen', 0, 0, tiled=False)]
    all_to_all x3 -> x0, waiting for transfers between devices: 18.7 us -> none  [exchange(): x = lax.all_to_all(x, 'scen', 0, 0, tiled=False)]
    pallas_call x6 -> x9, Pallas kernels: 46.1 us -> 29.7 us  [the longest x8 25.2 us: cost_share(): pl.pallas_call(functools.partial(cost_kernel, tile=min(256, rows // 2), m...]
    all_to_all x3 -> x0, starting transfers between devices: 11.5 us -> none  [exchange(): x = lax.all_to_all(x, 'scen', 0, 0, tiled=False)]
    pallas_call x1, Pallas kernels: 10.5 us -> 5.21 us  [on_device(): pl.pallas_call(functools.partial(first_kernel, pieces=pieces, scale=-1.0...]
    add x11 -> x13, other arithmetic: 5.69 us -> 0.52 us  [the longest x6 0.25 us: finish(): part = keep + swap(send, 1)]
    pallas_call x1, Pallas kernels: 7.8 us -> 3.16 us  [on_device(): pl.pallas_call(functools.partial(last_kernel, scale=scale, rolled=rolled,...]
    pallas_call x1, Pallas kernels: 5.78 us -> 1.27 us  [pick(): pl.pallas_call(functools.partial(pick_kernel, step=min(512, width)), out_...]
  transfers between devices with their start and end apart: 32 -> 32, of which waited for: 13 -> 14; matrix products, arithmetic and copies ran while one was open for 4% -> 1% of each run, Pallas kernels for 22% -> 19%
where the time goes in v2:
time: 161 us
  waiting for transfers between devices  54.7 us (34%)
  Pallas kernels  43.9 us (27%)
  blocking collectives  28.4 us (18%)
  starting transfers between devices  25.6 us (16%)
  local copies, waits for them, and re-layouts  4.15 us (3%)
  other arithmetic  2.93 us (2%)
    all_to_all x3, blocking collectives, exchange(): x = lax.all_to_all(x, 'scen', 0, 0, tiled=False)  28.4 us
    ppermute x7, waiting for transfers between devices, on_device(): y = lax.ppermute(b[i], 'scen', down)  28.2 us
    pallas_call x8, Pallas kernels, cost_share(): pl.pallas_call(functools.partial(cost_kernel, tile=min(256, rows // 2), m...  25.2 us
    ppermute x18, waiting for transfers between devices, swap(): return lax.ppermute(x, 'rep', [(i, i ^ bit) for i in range(n_rep)])  17.9 us
    ppermute x7, starting transfers between devices, on_device(): x = lax.ppermute(a[i], 'scen', up)  11.1 us
    ppermute x18, starting transfers between devices, swap(): return lax.ppermute(x, 'rep', [(i, i ^ bit) for i in range(n_rep)])  10.2 us
    ppermute x7, waiting for transfers between devices, on_device(): x = lax.ppermute(a[i], 'scen', up)  8.59 us
    pallas_call x1, Pallas kernels, on_device(): pl.pallas_call(functools.partial(first_kernel, pieces=pieces, scale=-1.0...  5.21 us
  transfers between devices with their start and end apart: 32, of which 14 were waited for; matrix products, arithmetic and copies ran while one was open for 1% of the time, Pallas kernels for 19%

profile of v2, /device:TPU:0, one launch (start us, length us, event | category | flops | bytes accessed | tf_op | source)
XLA Modules:
  0.0 160.6 jit_solution(4970519334455891459)
XLA Ops:
  0.6 0.8 dynamic_slice.3
  1.5 0.7 broadcast_compare_fusion
  2.2 1.2 convert_reduce_fusion.1
  3.5 3.4 %copy-done = bf16[1024,4096]{1,0:T(8,128)(2,1)S(1)} copy-done((bf16[1024,4096]{1,0:T(8,128)(2,1)S(1)}, bf16[1024,4096]{1,0:T(8,128)(2,1)}, u32[]{:S(2)}) %copy-start) | copy-done | bytes 8388632
  6.8 1.3 pick.1
  8.1 3.1 %collective-permute-start.4 = (bf16[64,4096]{1,0:T(8,128)(2,1)S(1)}, bf16[64,4096]{1,0:T(8,128)(2,1)S(1)}, u32[]{:S(2)}, u32[]{:S(2)}) collective-permute-start(bf16[64,4096]{1,0:T(8,128)(2,1)S(1)} %get-tuple-element.63.refs_0_), channel_id=1, source_target_pairs={{0,8},{8,16},{16,24},{24,28},{28,20},{20,12},{12,4},{4,0},{1,9},{9... | collective-permute-start | bytes 1572872 | tf_op jit(solution)/shard_map/ppermute | solution.py:342
  11.2 1.9 %collective-permute-start.5 = (bf16[64,4096]{1,0:T(8,128)(2,1)S(1)}, bf16[64,4096]{1,0:T(8,128)(2,1)S(1)}, u32[]{:S(2)}, u32[]{:S(2)}) collective-permute-start(bf16[64,4096]{1,0:T(8,128)(2,1)S(1)} %get-tuple-element.64.refs_1_), channel_id=1, source_target_pairs={{8,0},{16,8},{24,16},{28,24},{20,28},{12,20},{4,12},{0,4},{9,1},{1... | collective-permute-start | bytes 1572872 | tf_op jit(solution)/shard_map/ppermute | solution.py:343
  13.2 4.5 %norms.1.sq_ref = f32[1024,128]{1,0:T(8,128)S(1)} custom-call(bf16[1024,4096]{1,0:T(8,128)(2,1)S(1)} %copy-done), custom_call_target="tpu_custom_call" | custom-call | flops 8388608 | bytes 8388608 | tf_op jit(solution)/shard_map/norms/pallas_call | solution.py:68
  17.8 3.1 %cost_share.8 = (f32[512,128]{1,0:T(8,128)S(1)}, f32[512,128]{1,0:T(8,128)S(1)}) custom-call(s32[3]{0:T(128)S(1)} %pad_add_fusion.core_ref.ids_ref, bf16[1024,4096]{1,0:T(8,128)(2,1)S(1)} %copy-done, f32[1024,128]{1,0:T(8,128)S(1)} %norms.1.sq_ref, bf16[64,4096]{1,0:T(8,128)(2,1)S(1)} %get-tuple-element.63.refs_0_, ...), custom_call_target="tpu_custom_call" | custom-call | flops 1073741824 | bytes 8388608 | tf_op jit(solution)/shard_map/cost_share/pallas_call | solution.py:107
  21.4 1.1 collective-permute-done
  22.5 2.0 %collective-permute-start.1 = (f32[512,128]{1,0:T(8,128)S(1)}, f32[512,128]{1,0:T(8,128)S(1)}, u32[]{:S(2)}, u32[]{:S(2)}) collective-permute-start(f32[512,128]{1,0:T(8,128)S(1)} %add.115), channel_id=1, source_target_pairs={{0,2},{1,3},{2,0},{3,1},{4,6},{5,7},{6,4},{7,5},{8,10},{9,11},{10,... | collective-permute-start | bytes 786440 | tf_op jit(solution)/shard_map/ppermute | solution.py:313
  24.5 11.2 %collective-permute-done.5.refs_1_ = bf16[64,4096]{1,0:T(8,128)(2,1)S(1)} collective-permute-done((bf16[64,4096]{1,0:T(8,128)(2,1)S(1)}, bf16[64,4096]{1,0:T(8,128)(2,1)S(1)}, u32[]{:S(2)}, u32[]{:S(2)}) %collective-permute-start.5) | collective-permute-done | bytes 524320 | tf_op jit(solution)/shard_map/ppermute | solution.py:343
  35.8 1.6 collective-permute-start.10
  37.8 3.2 %cost_share.9 = (f32[512,128]{1,0:T(8,128)S(1)}, f32[512,128]{1,0:T(8,128)S(1)}) custom-call(s32[3]{0:T(128)S(1)} %pad_add_fusion.core_ref.ids_ref, bf16[1024,4096]{1,0:T(8,128)(2,1)S(1)} %bitcast.6, f32[1024,128]{1,0:T(8,128)S(1)} %norms.1.sq_ref, bf16[64,4096]{1,0:T(8,128)(2,1)S(1)} %collective-permute-done.4.refs_0_, ...), custom_call_target="tpu_custom_call" | custom-call | flops 1073741824 | bytes 8388608 | tf_op jit(solution)/shard_map/cost_share/pallas_call | solution.py:107
  41.0 3.2 %cost_share.10 = (f32[512,256]{1,0:T(8,128)S(1)}, f32[512,256]{1,0:T(8,128)S(1)}) custom-call(s32[3]{0:T(128)S(1)} %pad_add_fusion.core_ref.ids_ref, bf16[1024,4096]{1,0:T(8,128)(2,1)S(1)} %bitcast.6, f32[1024,128]{1,0:T(8,128)S(1)} %norms.1.sq_ref, bf16[64,4096]{1,0:T(8,128)(2,1)S(1)} %collective-permute-done.3.refs_0_, ...), custom_call_target="tpu_custom_call" | custom-call | flops 1073741824 | bytes 8388608 | tf_op jit(solution)/shard_map/cost_share/pallas_call | solution.py:107
  44.6 1.7 %collective-permute-start.8 = (bf16[64,4096]{1,0:T(8,128)(2,1)S(1)}, bf16[64,4096]{1,0:T(8,128)(2,1)S(1)}, u32[]{:S(2)}, u32[]{:S(2)}) collective-permute-start(bf16[64,4096]{1,0:T(8,128)(2,1)S(1)} %collective-permute-done.2.refs_1_), channel_id=1, source_target_pairs={{0,8},{8,16},{16,24},{24,28},{28,20},{20,12},{12,4},{4,0},{1,9},{9... | collective-permute-start | bytes 1572872 | tf_op jit(solution)/shard_map/ppermute | solution.py:342
  46.4 2.7 %collective-permute-done.10.refs_0_ = bf16[64,4096]{1,0:T(8,128)(2,1)S(1)} collective-permute-done((bf16[64,4096]{1,0:T(8,128)(2,1)S(1)}, bf16[64,4096]{1,0:T(8,128)(2,1)S(1)}, u32[]{:S(2)}, u32[]{:S(2)}) %collective-permute-start.10) | collective-permute-done | bytes 524320 | tf_op jit(solution)/shard_map/ppermute | solution.py:342
  49.1 2.6 %collective-permute-done.11.refs_1_ = bf16[64,4096]{1,0:T(8,128)(2,1)S(1)} collective-permute-done((bf16[64,4096]{1,0:T(8,128)(2,1)S(1)}, bf16[64,4096]{1,0:T(8,128)(2,1)S(1)}, u32[]{:S(2)}, u32[]{:S(2)}) %collective-permute-start.11) | collective-permute-done | bytes 524320 | tf_op jit(solution)/shard_map/ppermute | solution.py:343
  51.7 1.6 collective-permute-start.14
  53.8 1.6 collective-permute-start.7
  55.4 3.1 %cost_share.11 = (f32[512,128]{1,0:T(8,128)S(1)}, f32[512,128]{1,0:T(8,128)S(1)}) custom-call(s32[3]{0:T(128)S(1)} %pad_add_fusion.core_ref.ids_ref, bf16[1024,4096]{1,0:T(8,128)(2,1)S(1)} %bitcast.6, f32[1024,128]{1,0:T(8,128)S(1)} %norms.1.sq_ref, bf16[64,4096]{1,0:T(8,128)(2,1)S(1)} %collective-permute-done.10.refs_0_, ...), custom_call_target="tpu_custom_call" | custom-call | flops 1073741824 | bytes 8388608 | tf_op jit(solution)/shard_map/cost_share/pallas_call | solution.py:107
  58.5 4.4 %collective-permute-done.9.refs_0_ = bf16[64,4096]{1,0:T(8,128)(2,1)S(1)} collective-permute-done((bf16[64,4096]{1,0:T(8,128)(2,1)S(1)}, bf16[64,4096]{1,0:T(8,128)(2,1)S(1)}, u32[]{:S(2)}, u32[]{:S(2)}) %collective-permute-start.9) | collective-permute-done | bytes 524320 | tf_op jit(solution)/shard_map/ppermute | solution.py:343
  63.0 3.2 %cost_share.12 = (f32[512,256]{1,0:T(8,128)S(1)}, f32[512,256]{1,0:T(8,128)S(1)}) custom-call(s32[3]{0:T(128)S(1)} %pad_add_fusion.core_ref.ids_ref, bf16[1024,4096]{1,0:T(8,128)(2,1)S(1)} %bitcast.6, f32[1024,128]{1,0:T(8,128)S(1)} %norms.1.sq_ref, bf16[64,4096]{1,0:T(8,128)(2,1)S(1)} %collective-permute-done.9.refs_0_, ...), custom_call_target="tpu_custom_call" | custom-call | flops 1073741824 | bytes 8388608 | tf_op jit(solution)/shard_map/cost_share/pallas_call | solution.py:107
  66.2 0.7 collective-permute-start.19
  66.9 1.4 collective-permute-start.18
  68.4 3.2 %collective-permute-done.14.refs_0_ = bf16[64,4096]{1,0:T(8,128)(2,1)S(1)} collective-permute-done((bf16[64,4096]{1,0:T(8,128)(2,1)S(1)}, bf16[64,4096]{1,0:T(8,128)(2,1)S(1)}, u32[]{:S(2)}, u32[]{:S(2)}) %collective-permute-start.14) | collective-permute-done | bytes 524320 | tf_op jit(solution)/shard_map/ppermute | solution.py:342
  71.6 2.6 %collective-permute-done.15.refs_1_ = bf16[64,4096]{1,0:T(8,128)(2,1)S(1)} collective-permute-done((bf16[64,4096]{1,0:T(8,128)(2,1)S(1)}, bf16[64,4096]{1,0:T(8,128)(2,1)S(1)}, u32[]{:S(2)}, u32[]{:S(2)}) %collective-permute-start.15) | collective-permute-done | bytes 524320 | tf_op jit(solution)/shard_map/ppermute | solution.py:343
  74.2 1.6 collective-permute-start.22
  76.2 3.1 %cost_share.13 = (f32[512,128]{1,0:T(8,128)S(1)}, f32[512,128]{1,0:T(8,128)S(1)}) custom-call(s32[3]{0:T(128)S(1)} %pad_add_fusion.core_ref.ids_ref, bf16[1024,4096]{1,0:T(8,128)(2,1)S(1)} %bitcast.6, f32[1024,128]{1,0:T(8,128)S(1)} %norms.1.sq_ref, bf16[64,4096]{1,0:T(8,128)(2,1)S(1)} %collective-permute-done.14.refs_0_, ...), custom_call_target="tpu_custom_call" | custom-call | flops 1073741824 | bytes 8388608 | tf_op jit(solution)/shard_map/cost_share/pallas_call | solution.py:107
  79.4 6.1 %collective-permute-done.19.refs_0_ = bf16[64,4096]{1,0:T(8,128)(2,1)S(1)} collective-permute-done((bf16[64,4096]{1,0:T(8,128)(2,1)S(1)}, bf16[64,4096]{1,0:T(8,128)(2,1)S(1)}, u32[]{:S(2)}, u32[]{:S(2)}) %collective-permute-start.19) | collective-permute-done | bytes 524320 | tf_op jit(solution)/shard_map/ppermute | solution.py:343
  85.5 1.6 collective-permute-start.13
  87.1 3.1 %cost_share.14 = (f32[512,128]{1,0:T(8,128)S(1)}, f32[512,128]{1,0:T(8,128)S(1)}) custom-call(s32[3]{0:T(128)S(1)} %pad_add_fusion.core_ref.ids_ref, bf16[1024,4096]{1,0:T(8,128)(2,1)S(1)} %bitcast.6, f32[1024,128]{1,0:T(8,128)S(1)} %norms.1.sq_ref, bf16[64,4096]{1,0:T(8,128)(2,1)S(1)} %collective-permute-done.19.refs_0_, ...), custom_call_target="tpu_custom_call" | custom-call | flops 1073741824 | bytes 8388608 | tf_op jit(solution)/shard_map/cost_share/pallas_call | solution.py:107
  90.6 2.6 %collective-permute-done.22.refs_0_ = bf16[64,4096]{1,0:T(8,128)(2,1)S(1)} collective-permute-done((bf16[64,4096]{1,0:T(8,128)(2,1)S(1)}, bf16[64,4096]{1,0:T(8,128)(2,1)S(1)}, u32[]{:S(2)}, u32[]{:S(2)}) %collective-permute-start.22) | collective-permute-done | bytes 524320 | tf_op jit(solution)/shard_map/ppermute | solution.py:342
  93.2 1.3 collective-permute-done.23.refs_1_
  94.5 3.1 %cost_share.15 = (f32[512,128]{1,0:T(8,128)S(1)}, f32[512,128]{1,0:T(8,128)S(1)}) custom-call(s32[3]{0:T(128)S(1)} %pad_add_fusion.core_ref.ids_ref, bf16[1024,4096]{1,0:T(8,128)(2,1)S(1)} %bitcast.6, f32[1024,128]{1,0:T(8,128)S(1)} %norms.1.sq_ref, bf16[64,4096]{1,0:T(8,128)(2,1)S(1)} %collective-permute-done.22.refs_0_, ...), custom_call_target="tpu_custom_call" | custom-call | flops 1073741824 | bytes 8388608 | tf_op jit(solution)/shard_map/cost_share/pallas_call | solution.py:107
  97.7 1.6 collective-permute-start.17
  100.1 1.6 collective-permute-start.26
  102.1 4.8 %collective-permute-done.17 = f32[512,128]{1,0:T(8,128)S(1)} collective-permute-done((f32[512,128]{1,0:T(8,128)S(1)}, f32[512,128]{1,0:T(8,128)S(1)}, u32[]{:S(2)}, u32[]{:S(2)}) %collective-permute-start.17) | collective-permute-done | bytes 262176 | tf_op jit(solution)/shard_map/ppermute | solution.py:313
  107.0 5.5 %collective-permute-done.21 = f32[512,128]{1,0:T(8,128)S(1)} collective-permute-done((f32[512,128]{1,0:T(8,128)S(1)}, f32[512,128]{1,0:T(8,128)S(1)}, u32[]{:S(2)}, u32[]{:S(2)}) %collective-permute-start.21) | collective-permute-done | bytes 262176 | tf_op jit(solution)/shard_map/ppermute | solution.py:313
  112.6 5.1 %collective-permute-done.26 = f32[512,128]{1,0:T(8,128)S(1)} collective-permute-done((f32[512,128]{1,0:T(8,128)S(1)}, f32[512,128]{1,0:T(8,128)S(1)}, u32[]{:S(2)}, u32[]{:S(2)}) %collective-permute-start.26) | collective-permute-done | bytes 262176 | tf_op jit(solution)/shard_map/ppermute | solution.py:313
  117.9 1.5 collective-permute-done.31.refs_11_
  119.3 5.2 %first.1 = (f32[1024,1024]{1,0:T(8,128)S(1)}, f32[1024,128]{1,0:T(8,128)S(1)}, f32[8,8,128]{2,1,0:T(8,128)S(1)}) custom-call(s32[3]{0:T(128)S(1)} %pad_add_fusion.core_ref.ids_ref, f32[512,128]{1,0:T(8,128)S(1)} %add.116.refs_0_, f32[512,256]{1,0:T(8,128)S(1)} %add.128.refs_1_, f32[512,256]{1,0:T(8,128)S(1)} %add.130.refs_2_, f32[512,128]{1,0:T(8,128)S(1)} %add.132.refs_3_, ...), custom_call_target="tpu_custom_call" | custom-call | tf_op jit(solution)/shard_map/first/pallas_call | solution.py:393
  124.5 10.3 %all_to_all.15.got_ref = f32[8,8,128]{2,1,0:T(8,128)S(1)} all-to-all(f32[8,8,128]{2,1,0:T(8,128)S(1)} %get-tuple-element.97), channel_id=1, replica_groups=mesh['scen'=8,'rep'=4] {'scen'}, dimensions={0} | all-to-all | bytes 65536 | tf_op jit(solution)/shard_map/all_to_all | solution.py:388
  134.8 2.3 %step.1 = f32[8,8,128]{2,1,0:T(8,128)S(1)} custom-call(s32[3]{0:T(128)S(1)} %pad_add_fusion.core_ref.ids_ref, f32[8,8,128]{2,1,0:T(8,128)S(1)} %all_to_all.15.got_ref, f32[1024,1024]{1,0:T(8,128)S(1)} %get-tuple-element.98.e_ref), custom_call_target="tpu_custom_call" | custom-call | tf_op jit(solution)/shard_map/step/pallas_call | solution.py:403
  137.1 9.1 %all_to_all.16.got_ref = f32[8,8,128]{2,1,0:T(8,128)S(1)} all-to-all(f32[8,8,128]{2,1,0:T(8,128)S(1)} %step.1), channel_id=1, replica_groups=mesh['scen'=8,'rep'=4] {'scen'}, dimensions={0} | all-to-all | bytes 65536 | tf_op jit(solution)/shard_map/all_to_all | solution.py:388
  146.2 3.2 %last.1 = (f32[8,8,128]{2,1,0:T(8,128)S(1)}, f32[8,128]{1,0:T(8,128)}, f32[1024,1024]{1,0:T(8,128)S(1)}) custom-call(s32[3]{0:T(128)S(1)} %pad_add_fusion.core_ref.ids_ref, f32[8,8,128]{2,1,0:T(8,128)S(1)} %all_to_all.16.got_ref, f32[1024,1024]{1,0:T(8,128)S(1)} %get-tuple-element.98.e_ref, f32[1024,128]{1,0:T(8,128)S(1)} %get-tuple-element.99.peak_ref), custom_call_target="tpu_custom_call" | custom-call | tf_op jit(solution)/shard_map/last/pallas_call | solution.py:411
  149.4 9.0 %all_to_all.17.got_ref = f32[8,8,128]{2,1,0:T(8,128)S(1)} all-to-all(f32[8,8,128]{2,1,0:T(8,128)S(1)} %get-tuple-element.101), channel_id=1, replica_groups=mesh['scen'=8,'rep'=4] {'scen'}, dimensions={0} | all-to-all | bytes 65536 | tf_op jit(solution)/shard_map/all_to_all | solution.py:388
  158.4 2.2 %out.1 = (f32[1,256]{1,0:T(1,128)}, bf16[256,1024]{1,0:T(8,128)(2,1)}) custom-call(s32[3]{0:T(128)S(1)} %pad_add_fusion.core_ref.ids_ref, f32[8,8,128]{2,1,0:T(8,128)S(1)} %all_to_all.17.got_ref, f32[1024,1024]{1,0:T(8,128)S(1)} %get-tuple-element.102.scaled_ref, bf16[256,1024]{1,0:T(8,128)(2,1)S(1)} %fusion.1.perm_ref), custom_call_target="tpu_custom_call" | custom-call | tf_op jit(solution)/shard_map/out/pallas_call | solution.py:424
  (63 shorter events, 4.8 us)
Async XLA Ops:
  3.4 3.4 %copy-start = (bf16[1024,4096]{1,0:T(8,128)(2,1)S(1)}, bf16[1024,4096]{1,0:T(8,128)(2,1)}, u32[]{:S(2)}) copy-start(bf16[1024,4096]{1,0:T(8,128)(2,1)} %scen_ref.19) | copy-start | bytes 25165828
  8.1 16.4 %collective-permute-start.4 = (bf16[64,4096]{1,0:T(8,128)(2,1)S(1)}, bf16[64,4096]{1,0:T(8,128)(2,1)S(1)}, u32[]{:S(2)}, u32[]{:S(2)}) collective-permute-start(bf16[64,4096]{1,0:T(8,128)(2,1)S(1)} %get-tuple-element.63.refs_0_), channel_id=1, source_target_pairs={{0,8},{8,16},{16,24},{24,28},{28,20},{20,12},{12,4},{4,0},{1,9},{9... | collective-permute-start | bytes 1572872 | tf_op jit(solution)/shard_map/ppermute | solution.py:342
  11.2 29.8 %collective-permute-start.3 = (bf16[64,4096]{1,0:T(8,128)(2,1)S(1)}, bf16[64,4096]{1,0:T(8,128)(2,1)S(1)}, u32[]{:S(2)}, u32[]{:S(2)}) collective-permute-start(bf16[64,4096]{1,0:T(8,128)(2,1)S(1)} %get-tuple-element.63.refs_0_), channel_id=1, source_target_pairs={{8,0},{16,8},{24,16},{28,24},{20,28},{12,20},{4,12},{0,4},{9,1},{1... | collective-permute-start | bytes 1572872 | tf_op jit(solution)/shard_map/ppermute | solution.py:343
  11.2 24.6 %collective-permute-start.5 = (bf16[64,4096]{1,0:T(8,128)(2,1)S(1)}, bf16[64,4096]{1,0:T(8,128)(2,1)S(1)}, u32[]{:S(2)}, u32[]{:S(2)}) collective-permute-start(bf16[64,4096]{1,0:T(8,128)(2,1)S(1)} %get-tuple-element.64.refs_1_), channel_id=1, source_target_pairs={{8,0},{16,8},{24,16},{28,24},{20,28},{12,20},{4,12},{0,4},{9,1},{1... | collective-permute-start | bytes 1572872 | tf_op jit(solution)/shard_map/ppermute | solution.py:343
  13.1 27.9 %collective-permute-start.2 = (bf16[64,4096]{1,0:T(8,128)(2,1)S(1)}, bf16[64,4096]{1,0:T(8,128)(2,1)S(1)}, u32[]{:S(2)}, u32[]{:S(2)}) collective-permute-start(bf16[64,4096]{1,0:T(8,128)(2,1)S(1)} %get-tuple-element.64.refs_1_), channel_id=1, source_target_pairs={{0,8},{8,16},{16,24},{24,28},{28,20},{20,12},{12,4},{4,0},{1,9},{9... | collective-permute-start | bytes 1572872 | tf_op jit(solution)/shard_map/ppermute | solution.py:342
  13.2 24.6 %slice-start = ((s8[8388608]{0:T(1024)(128)(4,1)}), s8[4194304]{0:T(1024)(128)(4,1)S(1)}, s32[]{:S(2)}) async-start(s8[8388608]{0:T(1024)(128)(4,1)} %bitcast.5), calls=%async_computation.3 | async-start | bytes 8388608
  17.8 3.2 %copy-start.1 = (s32[1024]{0:T(1024)S(1)}, s32[1024]{0:T(1024)}, u32[]{:S(2)}) copy-start(s32[1024]{0:T(1024)} %param.3) | copy-start | bytes 12292
  17.8 20.1 %slice-start.1 = ((s8[8388608]{0:T(1024)(128)(4,1)}), s8[4194304]{0:T(1024)(128)(4,1)S(1)}, s32[]{:S(2)}) async-start(s8[8388608]{0:T(1024)(128)(4,1)} %bitcast.5), calls=%async_computation.4 | async-start | bytes 8388608
  20.9 1.6 collective-permute-start
  22.5 22.0 %collective-permute-start.1 = (f32[512,128]{1,0:T(8,128)S(1)}, f32[512,128]{1,0:T(8,128)S(1)}, u32[]{:S(2)}, u32[]{:S(2)}) collective-permute-start(f32[512,128]{1,0:T(8,128)S(1)} %add.115), channel_id=1, source_target_pairs={{0,2},{1,3},{2,0},{3,1},{4,6},{5,7},{6,4},{7,5},{8,10},{9,11},{10,... | collective-permute-start | bytes 786440 | tf_op jit(solution)/shard_map/ppermute | solution.py:313
  35.8 13.3 %collective-permute-start.10 = (bf16[64,4096]{1,0:T(8,128)(2,1)S(1)}, bf16[64,4096]{1,0:T(8,128)(2,1)S(1)}, u32[]{:S(2)}, u32[]{:S(2)}) collective-permute-start(bf16[64,4096]{1,0:T(8,128)(2,1)S(1)} %collective-permute-done.4.refs_0_), channel_id=1, source_target_pairs={{0,8},{8,16},{16,24},{24,28},{28,20},{20,12},{12,4},{4,0},{1,9},{9... | collective-permute-start | bytes 1572872 | tf_op jit(solution)/shard_map/ppermute | solution.py:342
  37.4 14.3 %collective-permute-start.11 = (bf16[64,4096]{1,0:T(8,128)(2,1)S(1)}, bf16[64,4096]{1,0:T(8,128)(2,1)S(1)}, u32[]{:S(2)}, u32[]{:S(2)}) collective-permute-start(bf16[64,4096]{1,0:T(8,128)(2,1)S(1)} %collective-permute-done.5.refs_1_), channel_id=1, source_target_pairs={{8,0},{16,8},{24,16},{28,24},{20,28},{12,20},{4,12},{0,4},{9,1},{1... | collective-permute-start | bytes 1572872 | tf_op jit(solution)/shard_map/ppermute | solution.py:343
  44.2 9.6 %collective-permute-start.6 = (f32[512,256]{1,0:T(8,128)S(1)}, f32[512,256]{1,0:T(8,128)S(1)}, u32[]{:S(2)}, u32[]{:S(2)}) collective-permute-start(f32[512,256]{1,0:T(8,128)S(1)} %get-tuple-element.76), channel_id=1, source_target_pairs={{0,1},{1,0},{2,3},{3,2},{4,5},{5,4},{6,7},{7,6},{8,9},{9,8},{10,11... | collective-permute-start | bytes 1572872 | tf_op jit(solution)/shard_map/ppermute | solution.py:313
  44.3 18.7 %collective-permute-start.9 = (bf16[64,4096]{1,0:T(8,128)(2,1)S(1)}, bf16[64,4096]{1,0:T(8,128)(2,1)S(1)}, u32[]{:S(2)}, u32[]{:S(2)}) collective-permute-start(bf16[64,4096]{1,0:T(8,128)(2,1)S(1)} %collective-permute-done.3.refs_0_), channel_id=1, source_target_pairs={{8,0},{16,8},{24,16},{28,24},{20,28},{12,20},{4,12},{0,4},{9,1},{1... | collective-permute-start | bytes 1572872 | tf_op jit(solution)/shard_map/ppermute | solution.py:343
  44.6 18.4 %collective-permute-start.8 = (bf16[64,4096]{1,0:T(8,128)(2,1)S(1)}, bf16[64,4096]{1,0:T(8,128)(2,1)S(1)}, u32[]{:S(2)}, u32[]{:S(2)}) collective-permute-start(bf16[64,4096]{1,0:T(8,128)(2,1)S(1)} %collective-permute-done.2.refs_1_), channel_id=1, source_target_pairs={{0,8},{8,16},{16,24},{24,28},{28,20},{20,12},{12,4},{4,0},{1,9},{9... | collective-permute-start | bytes 1572872 | tf_op jit(solution)/shard_map/ppermute | solution.py:342
  51.7 19.9 %collective-permute-start.14 = (bf16[64,4096]{1,0:T(8,128)(2,1)S(1)}, bf16[64,4096]{1,0:T(8,128)(2,1)S(1)}, u32[]{:S(2)}, u32[]{:S(2)}) collective-permute-start(bf16[64,4096]{1,0:T(8,128)(2,1)S(1)} %collective-permute-done.10.refs_0_), channel_id=1, source_target_pairs={{0,8},{8,16},{16,24},{24,28},{28,20},{20,12},{12,4},{4,0},{1,9},{9... | collective-permute-start | bytes 1572872 | tf_op jit(solution)/shard_map/ppermute | solution.py:342
  53.3 20.9 %collective-permute-start.15 = (bf16[64,4096]{1,0:T(8,128)(2,1)S(1)}, bf16[64,4096]{1,0:T(8,128)(2,1)S(1)}, u32[]{:S(2)}, u32[]{:S(2)}) collective-permute-start(bf16[64,4096]{1,0:T(8,128)(2,1)S(1)} %collective-permute-done.11.refs_1_), channel_id=1, source_target_pairs={{8,0},{16,8},{24,16},{28,24},{20,28},{12,20},{4,12},{0,4},{9,1},{1... | collective-permute-start | bytes 1572872 | tf_op jit(solution)/shard_map/ppermute | solution.py:343
  53.8 13.0 %collective-permute-start.7 = (f32[512,256]{1,0:T(8,128)S(1)}, f32[512,256]{1,0:T(8,128)S(1)}, u32[]{:S(2)}, u32[]{:S(2)}) collective-permute-start(f32[512,256]{1,0:T(8,128)S(1)} %add.127), channel_id=1, source_target_pairs={{0,2},{1,3},{2,0},{3,1},{4,6},{5,7},{6,4},{7,5},{8,10},{9,11},{10,... | collective-permute-start | bytes 1572872 | tf_op jit(solution)/shard_map/ppermute | solution.py:313
  66.1 9.7 %collective-permute-start.12 = (f32[512,256]{1,0:T(8,128)S(1)}, f32[512,256]{1,0:T(8,128)S(1)}, u32[]{:S(2)}, u32[]{:S(2)}) collective-permute-start(f32[512,256]{1,0:T(8,128)S(1)} %get-tuple-element.84), channel_id=1, source_target_pairs={{0,1},{1,0},{2,3},{3,2},{4,5},{5,4},{6,7},{7,6},{8,9},{9,8},{10,11... | collective-permute-start | bytes 1572872 | tf_op jit(solution)/shard_map/ppermute | solution.py:313
  66.2 19.2 %collective-permute-start.19 = (bf16[64,4096]{1,0:T(8,128)(2,1)S(1)}, bf16[64,4096]{1,0:T(8,128)(2,1)S(1)}, u32[]{:S(2)}, u32[]{:S(2)}) collective-permute-start(bf16[64,4096]{1,0:T(8,128)(2,1)S(1)} %collective-permute-done.9.refs_0_), channel_id=1, source_target_pairs={{8,0},{16,8},{24,16},{28,24},{20,28},{12,20},{4,12},{0,4},{9,1},{1... | collective-permute-start | bytes 1572872 | tf_op jit(solution)/shard_map/ppermute | solution.py:343
  66.9 18.6 %collective-permute-start.18 = (bf16[64,4096]{1,0:T(8,128)(2,1)S(1)}, bf16[64,4096]{1,0:T(8,128)(2,1)S(1)}, u32[]{:S(2)}, u32[]{:S(2)}) collective-permute-start(bf16[64,4096]{1,0:T(8,128)(2,1)S(1)} %collective-permute-done.8.refs_1_), channel_id=1, source_target_pairs={{0,8},{8,16},{16,24},{24,28},{28,20},{20,12},{12,4},{4,0},{1,9},{9... | collective-permute-start | bytes 1572872 | tf_op jit(solution)/shard_map/ppermute | solution.py:342
  71.6 19.0 %collective-permute-start.24 = (f32[512,256]{1,0:T(8,128)S(1)}, f32[512,256]{1,0:T(8,128)S(1)}, u32[]{:S(2)}, u32[]{:S(2)}) collective-permute-start(f32[512,256]{1,0:T(8,128)S(1)} %add.128.refs_1_), channel_id=1, source_target_pairs={{0,1},{1,0},{2,3},{3,2},{4,5},{5,4},{6,7},{7,6},{8,9},{9,8},{10,11... | collective-permute-start | bytes 1572872 | tf_op jit(solution)/shard_map/ppermute | solution.py:313
  74.2 19.0 %collective-permute-start.22 = (bf16[64,4096]{1,0:T(8,128)(2,1)S(1)}, bf16[64,4096]{1,0:T(8,128)(2,1)S(1)}, u32[]{:S(2)}, u32[]{:S(2)}) collective-permute-start(bf16[64,4096]{1,0:T(8,128)(2,1)S(1)} %collective-permute-done.14.refs_0_), channel_id=1, source_target_pairs={{0,8},{8,16},{16,24},{24,28},{28,20},{20,12},{12,4},{4,0},{1,9},{9... | collective-permute-start | bytes 1572872 | tf_op jit(solution)/shard_map/ppermute | solution.py:342
  75.8 18.7 %collective-permute-start.23 = (bf16[64,4096]{1,0:T(8,128)(2,1)S(1)}, bf16[64,4096]{1,0:T(8,128)(2,1)S(1)}, u32[]{:S(2)}, u32[]{:S(2)}) collective-permute-start(bf16[64,4096]{1,0:T(8,128)(2,1)S(1)} %collective-permute-done.15.refs_1_), channel_id=1, source_target_pairs={{8,0},{16,8},{24,16},{28,24},{20,28},{12,20},{4,12},{0,4},{9,1},{1... | collective-permute-start | bytes 1572872 | tf_op jit(solution)/shard_map/ppermute | solution.py:343
  85.4 4.8 %collective-permute-start.16 = (f32[512,128]{1,0:T(8,128)S(1)}, f32[512,128]{1,0:T(8,128)S(1)}, u32[]{:S(2)}, u32[]{:S(2)}) collective-permute-start(f32[512,128]{1,0:T(8,128)S(1)} %get-tuple-element.88), channel_id=1, source_target_pairs={{0,1},{1,0},{2,3},{3,2},{4,5},{5,4},{6,7},{7,6},{8,9},{9,8},{10,11... | collective-permute-start | bytes 786440 | tf_op jit(solution)/shard_map/ppermute | solution.py:313
  85.5 14.4 %collective-permute-start.13 = (f32[512,256]{1,0:T(8,128)S(1)}, f32[512,256]{1,0:T(8,128)S(1)}, u32[]{:S(2)}, u32[]{:S(2)}) collective-permute-start(f32[512,256]{1,0:T(8,128)S(1)} %add.129), channel_id=1, source_target_pairs={{0,2},{1,3},{2,0},{3,1},{4,6},{5,7},{6,4},{7,5},{8,10},{9,11},{10,... | collective-permute-start | bytes 1572872 | tf_op jit(solution)/shard_map/ppermute | solution.py:313
  90.2 9.1 %collective-permute-start.20 = (f32[512,128]{1,0:T(8,128)S(1)}, f32[512,128]{1,0:T(8,128)S(1)}, u32[]{:S(2)}, u32[]{:S(2)}) collective-permute-start(f32[512,128]{1,0:T(8,128)S(1)} %get-tuple-element.92), channel_id=1, source_target_pairs={{0,1},{1,0},{2,3},{3,2},{4,5},{5,4},{6,7},{7,6},{8,9},{9,8},{10,11... | collective-permute-start | bytes 786440 | tf_op jit(solution)/shard_map/ppermute | solution.py:313
  97.7 2.3 %collective-permute-start.25 = (f32[512,128]{1,0:T(8,128)S(1)}, f32[512,128]{1,0:T(8,128)S(1)}, u32[]{:S(2)}, u32[]{:S(2)}) collective-permute-start(f32[512,128]{1,0:T(8,128)S(1)} %get-tuple-element.96), channel_id=1, source_target_pairs={{0,1},{1,0},{2,3},{3,2},{4,5},{5,4},{6,7},{7,6},{8,9},{9,8},{10,11... | collective-permute-start | bytes 786440 | tf_op jit(solution)/shard_map/ppermute | solution.py:313
  97.7 9.2 %collective-permute-start.17 = (f32[512,128]{1,0:T(8,128)S(1)}, f32[512,128]{1,0:T(8,128)S(1)}, u32[]{:S(2)}, u32[]{:S(2)}) collective-permute-start(f32[512,128]{1,0:T(8,128)S(1)} %add.131), channel_id=1, source_target_pairs={{0,2},{1,3},{2,0},{3,1},{4,6},{5,7},{6,4},{7,5},{8,10},{9,11},{10,... | collective-permute-start | bytes 786440 | tf_op jit(solution)/shard_map/ppermute | solution.py:313
  99.4 13.2 %collective-permute-start.21 = (f32[512,128]{1,0:T(8,128)S(1)}, f32[512,128]{1,0:T(8,128)S(1)}, u32[]{:S(2)}, u32[]{:S(2)}) collective-permute-start(f32[512,128]{1,0:T(8,128)S(1)} %add.133), channel_id=1, source_target_pairs={{0,2},{1,3},{2,0},{3,1},{4,6},{5,7},{6,4},{7,5},{8,10},{9,11},{10,... | collective-permute-start | bytes 786440 | tf_op jit(solution)/shard_map/ppermute | solution.py:313
  100.1 17.6 %collective-permute-start.26 = (f32[512,128]{1,0:T(8,128)S(1)}, f32[512,128]{1,0:T(8,128)S(1)}, u32[]{:S(2)}, u32[]{:S(2)}) collective-permute-start(f32[512,128]{1,0:T(8,128)S(1)} %add.135), channel_id=1, source_target_pairs={{0,2},{1,3},{2,0},{3,1},{4,6},{5,7},{6,4},{7,5},{8,10},{9,11},{10,... | collective-permute-start | bytes 786440 | tf_op jit(solution)/shard_map/ppermute | solution.py:313
  101.6 16.2 %collective-permute-start.28 = (f32[512,256]{1,0:T(8,128)S(1)}, f32[512,256]{1,0:T(8,128)S(1)}, u32[]{:S(2)}, u32[]{:S(2)}) collective-permute-start(f32[512,256]{1,0:T(8,128)S(1)} %add.130.refs_2_), channel_id=1, source_target_pairs={{0,1},{1,0},{2,3},{3,2},{4,5},{5,4},{6,7},{7,6},{8,9},{9,8},{10,11... | collective-permute-start | bytes 1572872 | tf_op jit(solution)/shard_map/ppermute | solution.py:313
  101.6 16.2 %collective-permute-start.27 = (f32[512,128]{1,0:T(8,128)S(1)}, f32[512,128]{1,0:T(8,128)S(1)}, u32[]{:S(2)}, u32[]{:S(2)}) collective-permute-start(f32[512,128]{1,0:T(8,128)S(1)} %add.116.refs_0_), channel_id=1, source_target_pairs={{0,1},{1,0},{2,3},{3,2},{4,5},{5,4},{6,7},{7,6},{8,9},{9,8},{10,11... | collective-permute-start | bytes 786440 | tf_op jit(solution)/shard_map/ppermute | solution.py:313
  106.9 10.9 %collective-permute-start.29 = (f32[512,128]{1,0:T(8,128)S(1)}, f32[512,128]{1,0:T(8,128)S(1)}, u32[]{:S(2)}, u32[]{:S(2)}) collective-permute-start(f32[512,128]{1,0:T(8,128)S(1)} %add.132.refs_3_), channel_id=1, source_target_pairs={{0,1},{1,0},{2,3},{3,2},{4,5},{5,4},{6,7},{7,6},{8,9},{9,8},{10,11... | collective-permute-start | bytes 786440 | tf_op jit(solution)/shard_map/ppermute | solution.py:313
  112.6 5.3 %collective-permute-start.30 = (f32[512,128]{1,0:T(8,128)S(1)}, f32[512,128]{1,0:T(8,128)S(1)}, u32[]{:S(2)}, u32[]{:S(2)}) collective-permute-start(f32[512,128]{1,0:T(8,128)S(1)} %add.134.refs_4_), channel_id=1, source_target_pairs={{0,1},{1,0},{2,3},{3,2},{4,5},{5,4},{6,7},{7,6},{8,9},{9,8},{10,11... | collective-permute-start | bytes 786440 | tf_op jit(solution)/shard_map/ppermute | solution.py:313
  117.7 1.6 collective-permute-start.31

commit v3 on v2

--- a/solution.py
+++ b/solution.py
@@ -16,6 +16,8 @@
 NT = (((1,), (1,)), ((), ()))
 VMEM = pl.BlockSpec(memory_space=pltpu.VMEM)
 SMEM = pl.BlockSpec(memory_space=pltpu.SMEM)
+AFTER = {0: (2, 3, 4), 5: (2, 0, 4), 4: (1, 2, 3), 3: (1, 0, 0), 2: (1, 0, 0), 1: (0, 0, 0)}
+COST = pl.CostEstimate(flops=4 * 10**9, bytes_accessed=10**7, transcendentals=0)
 ROOM = pltpu.CompilerParams(vmem_limit_bytes=10 * 2**20)
 
 
@@ -30,28 +32,63 @@
     return jnp.sum(jnp.where(eye, gram, 0.0), axis=0, keepdims=True)
 
 
-def pick_kernel(sel_ref, scen_ref, low_ref, high_ref, *, step):
-    half = low_ref.shape[0]
-    for at in range(0, scen_ref.shape[1], step):
+def pick_kernel(index_ref, scen_ref, kept_ref, low_ref, high_ref, col_ref, sel_ref, sems, *, step):
+    rows_all, width = scen_ref.shape
+    copies = [
+        pltpu.make_async_copy(scen_ref.at[:, at : at + step], kept_ref.at[:, at : at + step], sems.at[i])
+        for i, at in enumerate(range(0, width, step))
+    ]
+    for copy in copies:
+        copy.start()
+    local = index_ref[...] - lax.axis_index("scen") * rows_all
+    local = jnp.where(local >= 0, local, 2 * rows_all)
+    tiles = [jnp.broadcast_to(local[i : i + 1, :], (SUB, LANES)) for i in range(local.shape[0])]
+    sub = lax.broadcasted_iota(jnp.int32, (SUB, LANES), 0)
+    lane = lax.broadcasted_iota(jnp.int32, (SUB, LANES), 1).astype(jnp.float32)
+
+    def body(i, carry):
+        keys = []
+        for g in range(16):
+            row = sub + (i * 16 + g) * SUB
+            hits = [jnp.where(t == row, 4096.0, jnp.where(t < row, 1.0, 0.0)) for t in tiles]
+            keys.append(tree(jnp.add, hits))
+        keys = [jnp.sum(x, axis=1, keepdims=True) for x in keys]
+        for g in range(16):
+            rows = pl.ds(pl.multiple_of((i * 16 + g) * SUB, SUB), SUB)
+            col_ref[rows, :] = jnp.where(lane == keys[g] - 4096.0, 1.0, 0.0)
+        return carry
+
+    lax.fori_loop(0, rows_all // LANES, body, 0)
+    per = 2 * low_ref.shape[0]
+    for at in range(0, rows_all, LANES):
+        block = jnp.transpose(col_ref[at : at + LANES, :])
+        sel_ref[:, at : at + LANES] = block[:per].astype(sel_ref.dtype)
+    for i, at in enumerate(range(0, width, step)):
+        copies[i].wait()
         cols = slice(at, at + step)
-        rows = jnp.dot(sel_ref[...], scen_ref[:, cols], preferred_element_type=jnp.float32)
-        low_ref[:, cols] = rows[:half].astype(low_ref.dtype)
-        high_ref[:, cols] = rows[half:].astype(high_ref.dtype)
-
-
-def pick(sel, scenarios):
-    rows, width = sel.shape[0], scenarios.shape[1]
+        rows = jnp.dot(sel_ref[...], kept_ref[:, cols], preferred_element_type=jnp.float32)
+        low_ref[:, cols] = rows[: per // 2].astype(low_ref.dtype)
+        high_ref[:, cols] = rows[per // 2 :].astype(high_ref.dtype)
+
+
+def pick(rep_index, scenarios, per):
+    rows, width = scenarios.shape
+    step = min(512, width)
+    some = pltpu.VMEM((per // 2, width), scenarios.dtype)
     return pl.pallas_call(
-        functools.partial(pick_kernel, step=min(512, width)),
-        out_shape=(pltpu.VMEM((rows // 2, width), scenarios.dtype),) * 2,
-        in_specs=[VMEM] * 2,
-        out_specs=(VMEM, VMEM),
-        cost_estimate=pl.CostEstimate(
-            flops=2 * rows * scenarios.size, bytes_accessed=2 * scenarios.size, transcendentals=0
-        ),
+        functools.partial(pick_kernel, step=step),
+        out_shape=(pltpu.VMEM((rows, width), scenarios.dtype), some, some),
+        in_specs=[VMEM, pl.BlockSpec(memory_space=pltpu.HBM)],
+        out_specs=(VMEM,) * 3,
+        scratch_shapes=[
+            pltpu.VMEM((rows, LANES), jnp.float32),
+            pltpu.VMEM((per, rows), scenarios.dtype),
+            pltpu.SemaphoreType.DMA((width // step,)),
+        ],
+        cost_estimate=COST,
         compiler_params=ROOM,
         name="pick",
-    )(*kept(sel, scenarios))
+    )(rep_index.reshape(-1, LANES), pltpu.with_memory_space_constraint(scenarios, pltpu.HBM))
 
 
 def norm_kernel(scen_ref, out_ref):
@@ -70,51 +107,37 @@
         out_shape=pltpu.VMEM((scenarios.shape[0], LANES), jnp.float32),
         in_specs=[VMEM],
         out_specs=VMEM,
-        cost_estimate=pl.CostEstimate(
-            flops=2 * scenarios.size, bytes_accessed=2 * scenarios.size, transcendentals=0
-        ),
+        cost_estimate=COST,
         compiler_params=ROOM,
         name="norms",
     )(*kept(scenarios))
 
 
-def cost_kernel(core_ref, scen_ref, sq_ref, *refs, tile, merge):
-    *refs, send_ref, keep_ref = refs
-    chunks, before = (refs[:-2], refs[-2:]) if merge else (refs, (None, None))
+def cost_kernel(core_ref, scen_ref, sq_ref, *refs, tile, parts):
+    chunks, outs = refs[: -len(parts)], refs[-len(parts) :]
     reps = jnp.concatenate([c[...] for c in chunks], axis=0)
     sq_rep = square_sums(reps)
-    half = send_ref.shape[0]
-    core = core_ref[0]
-    cols = reps.shape[0]
-    first = lax.broadcasted_iota(jnp.int32, (tile, cols), 1) < cols // 2
-    for out_ref, old_ref, which in ((send_ref, before[0], 1 - core), (keep_ref, before[1], core)):
+    half = outs[0].shape[0]
+    for flip, out_ref in zip(parts, outs, strict=True):
+        which = 1 - core_ref[0] if flip else core_ref[0]
         for at in range(0, half, tile):
             rows = pl.ds(pl.multiple_of(which * half + at, tile), tile)
             cross = lax.dot_general(scen_ref[rows, :], reps, NT, preferred_element_type=jnp.float32)
-            new = sq_rep + sq_ref[rows, 0:1] - 2.0 * cross
-            if merge:
-                old = old_ref[at : at + tile, :]
-                out_ref[at : at + tile, :cols] = jnp.where(first, old, new)
-                out_ref[at : at + tile, cols:] = jnp.where(first, new, old)
-            else:
-                out_ref[at : at + tile, :] = new
-
-
-def cost_share(core, scenarios, sq_scen, chunks, before=()):
+            out_ref[at : at + tile, :] = sq_rep + sq_ref[rows, 0:1] - 2.0 * cross
+
+
+def cost_share(core, scenarios, sq_scen, chunks, parts=(True, False)):
     rows, width = scenarios.shape
-    cols = sum(c.shape[0] for c in chunks)
-    half = pltpu.VMEM((rows // 2, cols * (2 if before else 1)), jnp.float32)
+    half = pltpu.VMEM((rows // 2, sum(c.shape[0] for c in chunks)), jnp.float32)
     return pl.pallas_call(
-        functools.partial(cost_kernel, tile=min(256, rows // 2), merge=bool(before)),
-        out_shape=(half, half),
-        in_specs=[SMEM] + [VMEM] * (2 + len(chunks) + len(before)),
-        out_specs=(VMEM, VMEM),
-        cost_estimate=pl.CostEstimate(
-            flops=2 * rows * cols * width, bytes_accessed=2 * rows * width, transcendentals=0
-        ),
+        functools.partial(cost_kernel, tile=min(256, rows // 2), parts=parts),
+        out_shape=(half,) * len(parts),
+        in_specs=[SMEM] + [VMEM] * (2 + len(chunks)),
+        out_specs=(VMEM,) * len(parts),
+        cost_estimate=COST,
         compiler_params=ROOM,
         name="cost_share",
-    )(core, *kept(scenarios, sq_scen, *chunks, *before))
+    )(core, *kept(scenarios, sq_scen, *chunks))
 
 
 def tree(op, xs):
@@ -145,7 +168,7 @@
     return [jnp.broadcast_to(w[i : i + 1, :], (SUB, LANES)) for i in range(w.shape[0])]
 
 
-GROUP = 8
+GROUP = 16
 
 
 def load(ref, rows):
@@ -161,26 +184,28 @@
     return pl.ds(pl.multiple_of(base + (i * GROUP + g) * SUB, SUB), SUB)
 
 
-def first_kernel(ids_ref, *refs, pieces, scale, rolled):
-    stages = len(refs) // 2 - 1
-    mine, other = refs[:stages], refs[stages : 2 * stages]
-    e_ref, peak_ref, out_ref = refs[2 * stages :]
-    half = mine[0].shape[0]
-    core = ids_ref[0]
+def cost_tiles(refs, pieces, src, here, left, scale):
+    mine, other = refs[: len(refs) // 2], refs[len(refs) // 2 :]
+    tiles = []
+    for piece in pieces:
+        part = [
+            jnp.where(here, mine[s][src, at : at + LANES], other[s][src, at : at + LANES])
+            for s, at in piece
+        ]
+        part = part[0] if len(part) == 1 else jnp.where(left, part[0], part[1])
+        tiles.append(part * scale)
+    return tiles
+
+
+def early_kernel(ids_ref, *refs, pieces, scale):
+    *refs, e_ref, peak_ref, sum_ref = refs
+    half = refs[0].shape[0]
     left = lax.broadcasted_iota(jnp.int32, (SUB, LANES), 1) < LANES // 2
 
-    def body(i, acc, h):
+    def body(i, carry, h):
         peaks, sums = [], []
         for g in range(GROUP):
-            src = group_rows(i, g)
-            z = []
-            for piece in pieces:
-                part = [
-                    jnp.where(core == h, mine[s][src, at : at + LANES], other[s][src, at : at + LANES])
-                    for s, at in piece
-                ]
-                part = part[0] if len(part) == 1 else jnp.where(left, part[0], part[1])
-                z.append(part * scale)
+            z = cost_tiles(refs, pieces, group_rows(i, g), ids_ref[0] == h, left, scale)
             store(e_ref, group_rows(i, g, h * half), z)
             peaks.append(tree(jnp.maximum, z))
         peaks = [jnp.max(p, axis=1, keepdims=True) for p in peaks]
@@ -190,14 +215,56 @@
             store(e_ref, dst, e)
             peak_ref[dst, :] = jnp.broadcast_to(peaks[g], (SUB, LANES))
             sums.append(tree(jnp.add, e))
-        sums = [1.0 / jnp.sum(x, axis=1, keepdims=True) for x in sums]
-        for g in range(GROUP):
-            acc = [a + x * sums[g] for a, x in zip(acc, load(e_ref, group_rows(i, g, h * half)))]
+        for g in range(GROUP):
+            total = jnp.sum(sums[g], axis=1, keepdims=True)
+            sum_ref[group_rows(i, g, h * half), :] = jnp.broadcast_to(total, (SUB, LANES))
+        return carry
+
+    for h in range(2):
+        lax.fori_loop(0, half // (GROUP * SUB), functools.partial(body, h=h), 0)
+
+
+def late_kernel(ids_ref, early_ref, old_peak_ref, old_sum_ref, *refs, pieces, order, scale, rolled):
+    *refs, e_ref, peak_ref, out_ref = refs
+    half = refs[0].shape[0]
+    left = lax.broadcasted_iota(jnp.int32, (SUB, LANES), 1) < LANES // 2
+    early = early_ref.shape[1] // LANES
+    at = [slice(k * LANES, (k + 1) * LANES) for k in order]
+
+    def body(i, acc, h):
+        peaks, sums, factors = [], [], []
+        for g in range(GROUP):
+            dst = group_rows(i, g, h * half)
+            z = cost_tiles(refs, pieces, group_rows(i, g), ids_ref[0] == h, left, scale)
+            for k, x in zip(at[early:], z, strict=True):
+                e_ref[dst, k] = x
+            peaks.append(tree(jnp.maximum, z))
+        peaks = [jnp.max(p, axis=1, keepdims=True) for p in peaks]
+        for g in range(GROUP):
+            dst = group_rows(i, g, h * half)
+            peak = jnp.maximum(old_peak_ref[dst, :], peaks[g])
+            factor = jnp.exp2(old_peak_ref[dst, :] - peak)
+            peak_ref[dst, :] = peak
+            factors.append(factor)
+            e = [jnp.exp2(e_ref[dst, k] - peak) for k in at[early:]]
+            for k, x in zip(at[early:], e, strict=True):
+                e_ref[dst, k] = x
+            sums.append(tree(jnp.add, e))
+        sums = [jnp.sum(x, axis=1, keepdims=True) for x in sums]
+        for g in range(GROUP):
+            dst = group_rows(i, g, h * half)
+            q = 1.0 / (old_sum_ref[dst, :] * factors[g] + sums[g])
+            e = [x * factors[g] for x in load(early_ref, dst)]
+            for k, x in zip(at[:early], e, strict=True):
+                e_ref[dst, k] = x
+            e += [e_ref[dst, k] for k in at[early:]]
+            acc = [a + x * q for a, x in zip(acc, e, strict=True)]
         return tuple(acc)
 
-    acc = tuple(jnp.zeros((SUB, LANES), jnp.float32) for _ in pieces)
+    acc = tuple(jnp.zeros((SUB, LANES), jnp.float32) for _ in order)
     for h in range(2):
         acc = lax.fori_loop(0, half // (GROUP * SUB), functools.partial(body, h=h), acc)
+    acc = [acc[order.index(k)] for k in range(len(order))]
     put_sums(acc, out_ref, ids_ref[1] if rolled else None)
 
 
@@ -237,9 +304,11 @@
     acc = tuple(jnp.zeros((SUB, LANES), jnp.float32) for _ in range(tiles))
     acc = lax.fori_loop(0, rows_all // (GROUP * SUB), body, acc)
     put_sums(acc, out_ref, ids_ref[1] if rolled else None)
+    shape = (LANES, LANES)
+    eye = lax.broadcasted_iota(jnp.int32, shape, 0) == lax.broadcasted_iota(jnp.int32, shape, 1)
     for i in range(rows_all // LANES):
         block = col_ref[i * LANES : (i + 1) * LANES, :]
-        pot_ref[i : i + 1, :] = jnp.transpose(block)[0:1, :]
+        pot_ref[i : i + 1, :] = jnp.sum(jnp.where(eye, block, 0.0), axis=0, keepdims=True)
 
 
 def out_kernel(ids_ref, got_ref, scaled_ref, perm_ref, pot_ref, member_ref, *, scale, rolled):
@@ -288,20 +357,12 @@
     rep = lax.axis_index("rep")
     place = jnp.where((d & 1) == 0, d >> 1, n - 1 - (d >> 1))
     back = jnp.where(place == 0, 0, n - place)
-    scalars = tuple(x.astype(jnp.int32) for x in (rep & 1, place, back, d * scen_rows, rep * rows_out))
-    rep_index, *scalars = tied([rep_index, *scalars])
-    core, place, back, scen_from, out_from = scalars
+    scalars = tuple(x.astype(jnp.int32) for x in (rep & 1, place, back, rep * rows_out))
+    rep_index, core, place, back, out_from = tied([rep_index, *scalars])
+
+    scenarios, *halves = pick(rep_index, scenarios, per)
     ids = jnp.stack([core, place, back])
-    wanted = lax.dynamic_slice_in_dim(rep_index, out_from, rows_out)
-    rep_index, ids, wanted, place, scen_from = tied([rep_index, ids, wanted, place, scen_from])
-
-    local = rep_index - scen_from
-    i_scen = jnp.arange(scen_rows, dtype=jnp.int32)
-    chosen = jnp.sum(as_int(local[:, None] == i_scen[None, :]), axis=0)
-    before = jnp.sum(as_int((local[:, None] >= 0) & (local[:, None] < i_scen[None, :])), axis=0)
-    key = jnp.where(chosen > 0, before, -1)
-    sel = (key[None, :] == jnp.arange(per, dtype=jnp.int32)[:, None]).astype(scenarios.dtype)
-    halves = list(pick(sel, scenarios))
+    wanted = lax.dynamic_slice(rep_index, (out_from,), (rows_out,), allow_negative_indices=False)
 
     rank = jnp.sum(as_int(rep_index[None, :] < wanted[:, None]), axis=1)
     block = rank // per
@@ -312,74 +373,101 @@
     def swap(x, bit):
         return lax.ppermute(x, "rep", [(i, i ^ bit) for i in range(n_rep)])
 
-    def rest(part):
+    def rest(part, *after):
         bit = 2
         while bit < n_rep:
-            part = part + swap(part, bit)
+            got = swap(part, bit)
+            if after:
+                (got,) = tied([got], *after)
+            part = part + got
             bit *= 2
         return part
 
     stages = []
     where = [None] * n
 
-    def finish(send, keep):
-        part = keep + swap(send, 1)
-        whole = rest(part)
+    def finish(part, *after):
+        whole = rest(part, *after)
         other = swap(whole, 1)
         stages.append((whole, other))
-        return part, whole, other
+        return whole, other
+
+    f32 = lambda *shape: pltpu.VMEM(shape, jnp.float32)
+    tiles = count_r // LANES
+    to_power = -1.0 / (features * eps_blur * math.log(2))
+
+    def start_early(pieces, stages):
+        given = [s[0] for s in stages] + [s[1] for s in stages]
+        return pl.pallas_call(
+            functools.partial(early_kernel, pieces=pieces, scale=to_power),
+            out_shape=(f32(scen_rows, len(pieces) * LANES), f32(scen_rows, LANES), f32(scen_rows, LANES)),
+            in_specs=[SMEM] + [VMEM] * len(given),
+            out_specs=(VMEM,) * 3,
+            cost_estimate=COST,
+            compiler_params=ROOM,
+            name="early",
+        )(ids, *kept(*given))
+
+    ties = {}
+
+    def tie(h, after, *xs):
+        if after:
+            ties.setdefault(h + after, []).extend(xs)
 
     sq_scen = norms(scenarios)
     shares = cost_share(ids, scenarios, sq_scen, halves)
-    ties = {1: [*shares, perm], 2: [], 3: [], 4: []}
-    part, whole, other = finish(*shares)
-    ties[2] += [part]
-    ties[4] += [whole]
-    where[0] = [(0, 0)]
+    tie(0, 1, perm)
     a, b = halves, halves[::-1]
-    for h in range(1, n):
+    a[1], b[1] = tied([a[1], b[1]], sq_scen)
+    begun = []
+    for h in range(n):
         i, k = (h + 1) % 2, (h + 1) // 2
-        x = lax.ppermute(a[i], "scen", up)
-        y = lax.ppermute(b[i], "scen", down)
-        x, y = tied([x, y], *ties.pop(h, []))
-        if i == 0:
-            a, b = [x, a[1]], [y, b[1]]
-            shares = cost_share(ids, scenarios, sq_scen, [x, y])
-        else:
-            a, b = [a[0], x], [b[0], y]
-            joined = h < n - 3
-            shares = cost_share(ids, scenarios, sq_scen, [y, x], shares if joined else ())
-        ties.setdefault(h + 1, []).extend(shares)
-        if i == 1 or h >= n - 3:
-            part, whole, other = finish(*shares)
-            ties.setdefault(h + 2, []).append(part)
-            ties.setdefault(h + 4, []).append(whole)
-            ties.setdefault(h + 5, []).append(other)
-            s = len(stages) - 1
-            if h == n - 1:
-                where[k] = [(s, 0)]
-            elif i == 1 and h < n - 3:
-                where[n - k], where[k] = [(s, 0)], [(s, per)]
-            elif i == 1:
-                where[n - k], where[k] = [(s - 1, 0), (s, 0)], [(s, 0), (s - 1, 0)]
+        if h:
+            a[i], b[i] = (lax.ppermute(x, "scen", way) for x, way in ((a[i], up), (b[i], down)))
+            a[i], b[i] = tied([a[i], b[i]], *ties.pop(h, []))
+            chunks = [b[i], a[i]] if i else [a[i], b[i]]
+        if h == n - 1:
+            sent = cost_share(ids, scenarios, sq_scen, chunks, parts=(True,))
+            finish(part, *sent, *begun)
+            shares = [*sent, *cost_share(ids, scenarios, sq_scen, chunks, parts=(False,))]
+        elif h:
+            shares = cost_share(ids, scenarios, sq_scen, chunks)
+        part = shares[1] + swap(shares[0], 1)
+        after = AFTER.get(n - h, AFTER[0])
+        tie(h, 1, *shares)
+        tie(h, after[0], part)
+        if h != n - 2:
+            whole, other = finish(part)
+            tie(h, after[1], whole)
+            tie(h, after[2], other)
+        if h in (0, n - 1):
+            where[k] = [(h, 0)]
+        elif i == 1:
+            where[n - k], where[k] = [(h - 1, 0), (h, 0)], [(h, 0), (h - 1, 0)]
+        if rolled and h == n - 4:
+            begun = start_early([w for w in where if w], stages)
 
     own, other = [s[0] for s in stages], [s[1] for s in stages]
-    if not rolled:
+    if rolled:
+        cut = len(stages) - 3
+        order = sorted(range(n), key=lambda q: where[q][0][0] >= cut)
+        pieces = [[(s - cut, at) for s, at in where[q]] for q in order if where[q][0][0] >= cut]
+        late = own[cut:] + other[cut:]
+    else:
 
         def join(xs):
             cols = []
             for piece in where:
                 part = [xs[s][:, at : at + per] for s, at in piece]
                 cols += part if len(part) == 1 else [part[0][:, : per // 2], part[1][:, per // 2 :]]
-            return [jnp.concatenate(cols, axis=1)]
-
-        own, other = join(own), join(other)
-        pieces = [[(0, i * LANES)] for i in range(count_r // LANES)]
-    else:
-        pieces = where
-
-    f32 = lambda *shape: pltpu.VMEM(shape, jnp.float32)
-    tiles = count_r // LANES
+            return jnp.concatenate(cols, axis=1)
+
+        order = list(range(tiles))
+        pieces = [[(0, i * LANES)] for i in order]
+        late = [join(own), join(other)]
+        begun = start_early(pieces[: tiles // 2], [late])
+        pieces = pieces[tiles // 2 :]
+
     sums = f32(n, tiles, LANES)
 
     def exchange(x):
@@ -391,13 +479,13 @@
         return x
 
     e, peak, x = pl.pallas_call(
-        functools.partial(first_kernel, pieces=pieces, scale=-1.0 / (features * eps_blur * math.log(2)), rolled=rolled),
+        functools.partial(late_kernel, pieces=pieces, order=order, scale=to_power, rolled=rolled),
         out_shape=(f32(scen_rows, count_r), f32(scen_rows, LANES), sums),
-        in_specs=[SMEM] + [VMEM] * (2 * len(own)),
+        in_specs=[SMEM] + [VMEM] * (3 + len(late)),
         out_specs=(VMEM,) * 3,
         compiler_params=ROOM,
-        name="first",
-    )(ids, *kept(*own, *other))
+        name="late",
+    )(ids, *kept(*begun, *late))
     scale = count_s / count_r
     for _ in range(ITERS - 2):
         x = pl.pallas_call(

time: 161 us -> 144 us (0.89)
  waiting for transfers between devices: 54.7 us -> 33.1 us
  starting transfers between devices: 25.6 us -> 30.5 us
  Pallas kernels: 43.9 us -> 48.1 us
  local copies, waits for them, and re-layouts: 4.15 us -> 0.76 us
  other arithmetic: 2.93 us -> 0.98 us
    ppermute x18 -> x24, waiting for transfers between devices: 17.9 us -> 6.04 us  [swap(): return lax.ppermute(x, 'rep', [(i, i ^ bit) for i in range(n_rep)])]
    ppermute x14, waiting for transfers between devices: 36.8 us -> 27.1 us  [on_device(): lax.ppermute(x, 'scen', way)]
    pallas_call x10 -> x12, Pallas kernels: 31.7 us -> 37.4 us  [the longest x9 26.2 us: cost_share(): pl.pallas_call(functools.partial(cost_kernel, tile=min(256, rows // 2), p...]
    ppermute x18 -> x24, starting transfers between devices: 10.2 us -> 14.7 us  [swap(): return lax.ppermute(x, 'rep', [(i, i ^ bit) for i in range(n_rep)])]
    unnamed x8 -> x4, local copies, waits for them, and re-layouts: 3.39 us -> 0.69 us
  transfers between devices with their start and end apart: 32 -> 38, of which waited for: 14 -> 16; matrix products, arithmetic and copies ran while one was open for 1% -> 1% of each run, Pallas kernels for 19% -> 24%
where the time goes in v3:
time: 144 us
  Pallas kernels  48.1 us (33%)
  waiting for transfers between devices  33.1 us (23%)
  starting transfers between devices  30.5 us (21%)
  blocking collectives  29.4 us (20%)
    all_to_all x3, blocking collectives, exchange(): x = lax.all_to_all(x, 'scen', 0, 0, tiled=False)  29.4 us
    ppermute x14, waiting for transfers between devices, on_device(): lax.ppermute(x, 'scen', way)  27.1 us
    pallas_call x9, Pallas kernels, cost_share(): pl.pallas_call(functools.partial(cost_kernel, tile=min(256, rows // 2), p...  26.2 us
    ppermute x14, starting transfers between devices, on_device(): lax.ppermute(x, 'scen', way)  15.7 us
    ppermute x24, starting transfers between devices, swap(): return lax.ppermute(x, 'rep', [(i, i ^ bit) for i in range(n_rep)])  14.7 us
    ppermute x24, waiting for transfers between devices, swap(): return lax.ppermute(x, 'rep', [(i, i ^ bit) for i in range(n_rep)])  6.04 us
    pallas_call x1, Pallas kernels, norms(): pl.pallas_call(norm_kernel, out_shape=pltpu.VMEM((scenarios.shape[0], LAN...  4.51 us
    pallas_call x1, Pallas kernels, pick(): pl.pallas_call(functools.partial(pick_kernel, step=step), out_shape=(pltp...  4.16 us
  transfers between devices with their start and end apart: 38, of which 16 were waited for; matrix products, arithmetic and copies ran while one was open for 1% of the time, Pallas kernels for 24%

profile of v3, /device:TPU:0, one launch (start us, length us, event | category | flops | bytes accessed | tf_op | source)
XLA Modules:
  0.0 143.8 jit_solution(11399172179428090017)
XLA Ops:
  1.3 4.2 %pick.1 = (bf16[1024,4096]{1,0:T(8,128)(2,1)S(1)}, bf16[64,4096]{1,0:T(8,128)(2,1)S(1)}, bf16[64,4096]{1,0:T(8,128)(2,1)S(1)}) custom-call(s32[8,128]{1,0:T(8,128)S(1)} %bitcast.6, bf16[1024,4096]{1,0:T(8,128)(2,1)} %scen_ref.1), custom_call_target="tpu_custom_call" | custom-call | flops 4000000000 | bytes 10000000 | tf_op jit(solution)/shard_map/pick/pallas_call | solution.py:78
  5.5 3.1 %collective-permute-start.2 = (bf16[64,4096]{1,0:T(8,128)(2,1)S(1)}, bf16[64,4096]{1,0:T(8,128)(2,1)S(1)}, u32[]{:S(2)}, u32[]{:S(2)}) collective-permute-start(bf16[64,4096]{1,0:T(8,128)(2,1)S(1)} %get-tuple-element.68.refs_0_), channel_id=1, source_target_pairs={{0,8},{8,16},{16,24},{24,28},{28,20},{20,12},{12,4},{4,0},{1,9},{9... | collective-permute-start | bytes 1572872 | tf_op jit(solution)/shard_map/ppermute | solution.py:426
  8.6 4.5 %norms.1.sq_ref = f32[1024,128]{1,0:T(8,128)S(1)} custom-call(bf16[1024,4096]{1,0:T(8,128)(2,1)S(1)} %get-tuple-element.57.scen_ref), custom_call_target="tpu_custom_call" | custom-call | flops 4000000000 | bytes 10000000 | tf_op jit(solution)/shard_map/norms/pallas_call | solution.py:105
  13.2 3.2 %cost_share.9 = (f32[512,128]{1,0:T(8,128)S(1)}, f32[512,128]{1,0:T(8,128)S(1)}) custom-call(s32[3]{0:T(128)S(1)} %pad_add_fusion.core_ref.ids_ref, bf16[1024,4096]{1,0:T(8,128)(2,1)S(1)} %get-tuple-element.57.scen_ref, f32[1024,128]{1,0:T(8,128)S(1)} %norms.1.sq_ref, bf16[64,4096]{1,0:T(8,128)(2,1)S(1)} %get-tuple-element.68.refs_0_, ...), custom_call_target="tpu_custom_call" | custom-call | flops 4000000000 | bytes 10000000 | tf_op jit(solution)/shard_map/cost_share/pallas_call | solution.py:132
  16.4 2.1 %collective-permute-start.6 = (bf16[64,4096]{1,0:T(8,128)(2,1)S(1)}, bf16[64,4096]{1,0:T(8,128)(2,1)S(1)}, u32[]{:S(2)}, u32[]{:S(2)}) collective-permute-start(bf16[64,4096]{1,0:T(8,128)(2,1)S(1)} %get-tuple-element.67.refs_1_), channel_id=1, source_target_pairs={{0,8},{8,16},{16,24},{24,28},{28,20},{20,12},{12,4},{4,0},{1,9},{9... | collective-permute-start | bytes 1572872 | tf_op jit(solution)/shard_map/ppermute | solution.py:426
  19.1 2.0 %collective-permute-start.1 = (f32[512,128]{1,0:T(8,128)S(1)}, f32[512,128]{1,0:T(8,128)S(1)}, u32[]{:S(2)}, u32[]{:S(2)}) collective-permute-start(f32[512,128]{1,0:T(8,128)S(1)} %add.123), channel_id=1, source_target_pairs={{0,2},{1,3},{2,0},{3,1},{4,6},{5,7},{6,4},{7,5},{8,10},{9,11},{10,... | collective-permute-start | bytes 786440 | tf_op jit(solution)/shard_map/ppermute | solution.py:374
  21.1 1.5 %collective-permute-done.3.refs_1_ = bf16[64,4096]{1,0:T(8,128)(2,1)S(1)} collective-permute-done((bf16[64,4096]{1,0:T(8,128)(2,1)S(1)}, bf16[64,4096]{1,0:T(8,128)(2,1)S(1)}, u32[]{:S(2)}, u32[]{:S(2)}) %collective-permute-start.3) | collective-permute-done | bytes 524320 | tf_op jit(solution)/shard_map/ppermute | solution.py:426
  22.6 1.6 %collective-permute-start.10 = (bf16[64,4096]{1,0:T(8,128)(2,1)S(1)}, bf16[64,4096]{1,0:T(8,128)(2,1)S(1)}, u32[]{:S(2)}, u32[]{:S(2)}) collective-permute-start(bf16[64,4096]{1,0:T(8,128)(2,1)S(1)} %collective-permute-done.2.refs_0_), channel_id=1, source_target_pairs={{0,8},{8,16},{16,24},{24,28},{28,20},{20,12},{12,4},{4,0},{1,9},{9... | collective-permute-start | bytes 1572872 | tf_op jit(solution)/shard_map/ppermute | solution.py:426
  24.6 3.2 %cost_share.10 = (f32[512,128]{1,0:T(8,128)S(1)}, f32[512,128]{1,0:T(8,128)S(1)}) custom-call(s32[3]{0:T(128)S(1)} %pad_add_fusion.core_ref.ids_ref, bf16[1024,4096]{1,0:T(8,128)(2,1)S(1)} %get-tuple-element.57.scen_ref, f32[1024,128]{1,0:T(8,128)S(1)} %norms.1.sq_ref, bf16[64,4096]{1,0:T(8,128)(2,1)S(1)} %collective-permute-done.2.refs_0_, ...), custom_call_target="tpu_custom_call" | custom-call | flops 4000000000 | bytes 10000000 | tf_op jit(solution)/shard_map/cost_share/pallas_call | solution.py:132
  27.8 4.5 %collective-permute-done.6.refs_1_ = bf16[64,4096]{1,0:T(8,128)(2,1)S(1)} collective-permute-done((bf16[64,4096]{1,0:T(8,128)(2,1)S(1)}, bf16[64,4096]{1,0:T(8,128)(2,1)S(1)}, u32[]{:S(2)}, u32[]{:S(2)}) %collective-permute-start.6) | collective-permute-done | bytes 524320 | tf_op jit(solution)/shard_map/ppermute | solution.py:426
  32.3 1.5 %collective-permute-done.7.refs_0_ = bf16[64,4096]{1,0:T(8,128)(2,1)S(1)} collective-permute-done((bf16[64,4096]{1,0:T(8,128)(2,1)S(1)}, bf16[64,4096]{1,0:T(8,128)(2,1)S(1)}, u32[]{:S(2)}, u32[]{:S(2)}) %collective-permute-start.7) | collective-permute-done | bytes 524320 | tf_op jit(solution)/shard_map/ppermute | solution.py:426
  33.8 3.2 %cost_share.11 = (f32[512,128]{1,0:T(8,128)S(1)}, f32[512,128]{1,0:T(8,128)S(1)}) custom-call(s32[3]{0:T(128)S(1)} %pad_add_fusion.core_ref.ids_ref, bf16[1024,4096]{1,0:T(8,128)(2,1)S(1)} %get-tuple-element.57.scen_ref, f32[1024,128]{1,0:T(8,128)S(1)} %norms.1.sq_ref, bf16[64,4096]{1,0:T(8,128)(2,1)S(1)} %collective-permute-done.7.refs_0_, ...), custom_call_target="tpu_custom_call" | custom-call | flops 4000000000 | bytes 10000000 | tf_op jit(solution)/shard_map/cost_share/pallas_call | solution.py:132
  37.1 1.6 %collective-permute-start.5 = (f32[512,128]{1,0:T(8,128)S(1)}, f32[512,128]{1,0:T(8,128)S(1)}, u32[]{:S(2)}, u32[]{:S(2)}) collective-permute-start(f32[512,128]{1,0:T(8,128)S(1)} %add.135), channel_id=1, source_target_pairs={{0,2},{1,3},{2,0},{3,1},{4,6},{5,7},{6,4},{7,5},{8,10},{9,11},{10,... | collective-permute-start | bytes 786440 | tf_op jit(solution)/shard_map/ppermute | solution.py:374
  38.7 1.6 %collective-permute-start.14 = (bf16[64,4096]{1,0:T(8,128)(2,1)S(1)}, bf16[64,4096]{1,0:T(8,128)(2,1)S(1)}, u32[]{:S(2)}, u32[]{:S(2)}) collective-permute-start(bf16[64,4096]{1,0:T(8,128)(2,1)S(1)} %collective-permute-done.6.refs_1_), channel_id=1, source_target_pairs={{0,8},{8,16},{16,24},{24,28},{28,20},{20,12},{12,4},{4,0},{1,9},{9... | collective-permute-start | bytes 1572872 | tf_op jit(solution)/shard_map/ppermute | solution.py:426
  40.8 2.7 %collective-permute-done.10.refs_0_ = bf16[64,4096]{1,0:T(8,128)(2,1)S(1)} collective-permute-done((bf16[64,4096]{1,0:T(8,128)(2,1)S(1)}, bf16[64,4096]{1,0:T(8,128)(2,1)S(1)}, u32[]{:S(2)}, u32[]{:S(2)}) %collective-permute-start.10) | collective-permute-done | bytes 524320 | tf_op jit(solution)/shard_map/ppermute | solution.py:426
  43.5 1.5 %collective-permute-done.11.refs_1_ = bf16[64,4096]{1,0:T(8,128)(2,1)S(1)} collective-permute-done((bf16[64,4096]{1,0:T(8,128)(2,1)S(1)}, bf16[64,4096]{1,0:T(8,128)(2,1)S(1)}, u32[]{:S(2)}, u32[]{:S(2)}) %collective-permute-start.11) | collective-permute-done | bytes 524320 | tf_op jit(solution)/shard_map/ppermute | solution.py:426
  45.1 1.5 %collective-permute-start.9 = (f32[512,128]{1,0:T(8,128)S(1)}, f32[512,128]{1,0:T(8,128)S(1)}, u32[]{:S(2)}, u32[]{:S(2)}) collective-permute-start(f32[512,128]{1,0:T(8,128)S(1)} %add.137), channel_id=1, source_target_pairs={{0,2},{1,3},{2,0},{3,1},{4,6},{5,7},{6,4},{7,5},{8,10},{9,11},{10,... | collective-permute-start | bytes 786440 | tf_op jit(solution)/shard_map/ppermute | solution.py:374
  46.6 1.6 %collective-permute-start.23 = (bf16[64,4096]{1,0:T(8,128)(2,1)S(1)}, bf16[64,4096]{1,0:T(8,128)(2,1)S(1)}, u32[]{:S(2)}, u32[]{:S(2)}) collective-permute-start(bf16[64,4096]{1,0:T(8,128)(2,1)S(1)} %collective-permute-done.10.refs_0_), channel_id=1, source_target_pairs={{0,8},{8,16},{16,24},{24,28},{28,20},{20,12},{12,4},{4,0},{1,9},{9... | collective-permute-start | bytes 1572872 | tf_op jit(solution)/shard_map/ppermute | solution.py:426
  48.2 3.2 %cost_share.12 = (f32[512,128]{1,0:T(8,128)S(1)}, f32[512,128]{1,0:T(8,128)S(1)}) custom-call(s32[3]{0:T(128)S(1)} %pad_add_fusion.core_ref.ids_ref, bf16[1024,4096]{1,0:T(8,128)(2,1)S(1)} %get-tuple-element.57.scen_ref, f32[1024,128]{1,0:T(8,128)S(1)} %norms.1.sq_ref, bf16[64,4096]{1,0:T(8,128)(2,1)S(1)} %collective-permute-done.10.refs_0_, ...), custom_call_target="tpu_custom_call" | custom-call | flops 4000000000 | bytes 10000000 | tf_op jit(solution)/shard_map/cost_share/pallas_call | solution.py:132
  52.1 2.7 %collective-permute-done.14.refs_1_ = bf16[64,4096]{1,0:T(8,128)(2,1)S(1)} collective-permute-done((bf16[64,4096]{1,0:T(8,128)(2,1)S(1)}, bf16[64,4096]{1,0:T(8,128)(2,1)S(1)}, u32[]{:S(2)}, u32[]{:S(2)}) %collective-permute-start.14) | collective-permute-done | bytes 524320 | tf_op jit(solution)/shard_map/ppermute | solution.py:426
  54.8 1.5 %collective-permute-done.15.refs_0_ = bf16[64,4096]{1,0:T(8,128)(2,1)S(1)} collective-permute-done((bf16[64,4096]{1,0:T(8,128)(2,1)S(1)}, bf16[64,4096]{1,0:T(8,128)(2,1)S(1)}, u32[]{:S(2)}, u32[]{:S(2)}) %collective-permute-start.15) | collective-permute-done | bytes 524320 | tf_op jit(solution)/shard_map/ppermute | solution.py:426
  56.3 3.2 %cost_share.13 = (f32[512,128]{1,0:T(8,128)S(1)}, f32[512,128]{1,0:T(8,128)S(1)}) custom-call(s32[3]{0:T(128)S(1)} %pad_add_fusion.core_ref.ids_ref, bf16[1024,4096]{1,0:T(8,128)(2,1)S(1)} %get-tuple-element.57.scen_ref, f32[1024,128]{1,0:T(8,128)S(1)} %norms.1.sq_ref, bf16[64,4096]{1,0:T(8,128)(2,1)S(1)} %collective-permute-done.15.refs_0_, ...), custom_call_target="tpu_custom_call" | custom-call | flops 4000000000 | bytes 10000000 | tf_op jit(solution)/shard_map/cost_share/pallas_call | solution.py:132
  60.1 1.6 %collective-permute-start.27 = (bf16[64,4096]{1,0:T(8,128)(2,1)S(1)}, bf16[64,4096]{1,0:T(8,128)(2,1)S(1)}, u32[]{:S(2)}, u32[]{:S(2)}) collective-permute-start(bf16[64,4096]{1,0:T(8,128)(2,1)S(1)} %collective-permute-done.14.refs_1_), channel_id=1, source_target_pairs={{0,8},{8,16},{16,24},{24,28},{28,20},{20,12},{12,4},{4,0},{1,9},{9... | collective-permute-start | bytes 1572872 | tf_op jit(solution)/shard_map/ppermute | solution.py:426
  62.3 1.6 %collective-permute-start.18 = (f32[512,128]{1,0:T(8,128)S(1)}, f32[512,128]{1,0:T(8,128)S(1)}, u32[]{:S(2)}, u32[]{:S(2)}) collective-permute-start(f32[512,128]{1,0:T(8,128)S(1)} %add.141), channel_id=1, source_target_pairs={{0,2},{1,3},{2,0},{3,1},{4,6},{5,7},{6,4},{7,5},{8,10},{9,11},{10,... | collective-permute-start | bytes 786440 | tf_op jit(solution)/shard_map/ppermute | solution.py:374
  63.9 2.1 %collective-permute-done.23.refs_0_ = bf16[64,4096]{1,0:T(8,128)(2,1)S(1)} collective-permute-done((bf16[64,4096]{1,0:T(8,128)(2,1)S(1)}, bf16[64,4096]{1,0:T(8,128)(2,1)S(1)}, u32[]{:S(2)}, u32[]{:S(2)}) %collective-permute-start.23) | collective-permute-done | bytes 524320 | tf_op jit(solution)/shard_map/ppermute | solution.py:426
  66.0 1.5 %collective-permute-done.24.refs_1_ = bf16[64,4096]{1,0:T(8,128)(2,1)S(1)} collective-permute-done((bf16[64,4096]{1,0:T(8,128)(2,1)S(1)}, bf16[64,4096]{1,0:T(8,128)(2,1)S(1)}, u32[]{:S(2)}, u32[]{:S(2)}) %collective-permute-start.24) | collective-permute-done | bytes 524320 | tf_op jit(solution)/shard_map/ppermute | solution.py:426
  67.6 3.2 %cost_share.14 = (f32[512,128]{1,0:T(8,128)S(1)}, f32[512,128]{1,0:T(8,128)S(1)}) custom-call(s32[3]{0:T(128)S(1)} %pad_add_fusion.core_ref.ids_ref, bf16[1024,4096]{1,0:T(8,128)(2,1)S(1)} %get-tuple-element.57.scen_ref, f32[1024,128]{1,0:T(8,128)S(1)} %norms.1.sq_ref, bf16[64,4096]{1,0:T(8,128)(2,1)S(1)} %collective-permute-done.23.refs_0_, ...), custom_call_target="tpu_custom_call" | custom-call | flops 4000000000 | bytes 10000000 | tf_op jit(solution)/shard_map/cost_share/pallas_call | solution.py:132
  71.3 1.5 %collective-permute-start.13 = (f32[512,128]{1,0:T(8,128)S(1)}, f32[512,128]{1,0:T(8,128)S(1)}, u32[]{:S(2)}, u32[]{:S(2)}) collective-permute-start(f32[512,128]{1,0:T(8,128)S(1)} %add.139), channel_id=1, source_target_pairs={{0,2},{1,3},{2,0},{3,1},{4,6},{5,7},{6,4},{7,5},{8,10},{9,11},{10,... | collective-permute-start | bytes 786440 | tf_op jit(solution)/shard_map/ppermute | solution.py:374
  72.9 1.6 %collective-permute-start.31 = (bf16[64,4096]{1,0:T(8,128)(2,1)S(1)}, bf16[64,4096]{1,0:T(8,128)(2,1)S(1)}, u32[]{:S(2)}, u32[]{:S(2)}) collective-permute-start(bf16[64,4096]{1,0:T(8,128)(2,1)S(1)} %collective-permute-done.23.refs_0_), channel_id=1, source_target_pairs={{0,8},{8,16},{16,24},{24,28},{28,20},{20,12},{12,4},{4,0},{1,9},{9... | collective-permute-start | bytes 1572872 | tf_op jit(solution)/shard_map/ppermute | solution.py:426
  75.0 2.2 %collective-permute-done.27.refs_1_ = bf16[64,4096]{1,0:T(8,128)(2,1)S(1)} collective-permute-done((bf16[64,4096]{1,0:T(8,128)(2,1)S(1)}, bf16[64,4096]{1,0:T(8,128)(2,1)S(1)}, u32[]{:S(2)}, u32[]{:S(2)}) %collective-permute-start.27) | collective-permute-done | bytes 524320 | tf_op jit(solution)/shard_map/ppermute | solution.py:426
  77.2 1.5 %collective-permute-done.28.refs_0_ = bf16[64,4096]{1,0:T(8,128)(2,1)S(1)} collective-permute-done((bf16[64,4096]{1,0:T(8,128)(2,1)S(1)}, bf16[64,4096]{1,0:T(8,128)(2,1)S(1)}, u32[]{:S(2)}, u32[]{:S(2)}) %collective-permute-start.28) | collective-permute-done | bytes 524320 | tf_op jit(solution)/shard_map/ppermute | solution.py:426
  78.8 3.2 %cost_share.15 = (f32[512,128]{1,0:T(8,128)S(1)}, f32[512,128]{1,0:T(8,128)S(1)}) custom-call(s32[3]{0:T(128)S(1)} %pad_add_fusion.core_ref.ids_ref, bf16[1024,4096]{1,0:T(8,128)(2,1)S(1)} %get-tuple-element.57.scen_ref, f32[1024,128]{1,0:T(8,128)S(1)} %norms.1.sq_ref, bf16[64,4096]{1,0:T(8,128)(2,1)S(1)} %collective-permute-done.28.refs_0_, ...), custom_call_target="tpu_custom_call" | custom-call | flops 4000000000 | bytes 10000000 | tf_op jit(solution)/shard_map/cost_share/pallas_call | solution.py:132
  83.6 1.5 %collective-permute-start.26 = (f32[512,128]{1,0:T(8,128)S(1)}, f32[512,128]{1,0:T(8,128)S(1)}, u32[]{:S(2)}, u32[]{:S(2)}) collective-permute-start(f32[512,128]{1,0:T(8,128)S(1)} %add.143), channel_id=1, source_target_pairs={{0,2},{1,3},{2,0},{3,1},{4,6},{5,7},{6,4},{7,5},{8,10},{9,11},{10,... | collective-permute-start | bytes 786440 | tf_op jit(solution)/shard_map/ppermute | solution.py:374
  85.7 2.1 %collective-permute-done.31.refs_0_ = bf16[64,4096]{1,0:T(8,128)(2,1)S(1)} collective-permute-done((bf16[64,4096]{1,0:T(8,128)(2,1)S(1)}, bf16[64,4096]{1,0:T(8,128)(2,1)S(1)}, u32[]{:S(2)}, u32[]{:S(2)}) %collective-permute-start.31) | collective-permute-done | bytes 524320 | tf_op jit(solution)/shard_map/ppermute | solution.py:426
  87.8 1.5 %collective-permute-done.32.refs_1_ = bf16[64,4096]{1,0:T(8,128)(2,1)S(1)} collective-permute-done((bf16[64,4096]{1,0:T(8,128)(2,1)S(1)}, bf16[64,4096]{1,0:T(8,128)(2,1)S(1)}, u32[]{:S(2)}, u32[]{:S(2)}) %collective-permute-start.32) | collective-permute-done | bytes 524320 | tf_op jit(solution)/shard_map/ppermute | solution.py:426
  89.4 2.1 %cost_share.16 = f32[512,128]{1,0:T(8,128)S(1)} custom-call(s32[3]{0:T(128)S(1)} %pad_add_fusion.core_ref.ids_ref, bf16[1024,4096]{1,0:T(8,128)(2,1)S(1)} %get-tuple-element.57.scen_ref, f32[1024,128]{1,0:T(8,128)S(1)} %norms.1.sq_ref, bf16[64,4096]{1,0:T(8,128)(2,1)S(1)} %collective-permute-done.31.refs_0_, bf16[64,4096]{1,0:T(8,128)(2,1)S(1)} %collective-permute-done.32.refs_1_), custom_call_target="tpu_custom_call" | custom-call | flops 4000000000 | bytes 10000000 | tf_op jit(solution)/shard_map/cost_share/pallas_call | solution.py:132
  91.5 2.1 %cost_share.17 = f32[512,128]{1,0:T(8,128)S(1)} custom-call(s32[3]{0:T(128)S(1)} %pad_add_fusion.core_ref.ids_ref, bf16[1024,4096]{1,0:T(8,128)(2,1)S(1)} %get-tuple-element.57.scen_ref, f32[1024,128]{1,0:T(8,128)S(1)} %norms.1.sq_ref, bf16[64,4096]{1,0:T(8,128)(2,1)S(1)} %collective-permute-done.31.refs_0_, bf16[64,4096]{1,0:T(8,128)(2,1)S(1)} %collective-permute-done.32.refs_1_), custom_call_target="tpu_custom_call" | custom-call | flops 4000000000 | bytes 10000000 | tf_op jit(solution)/shard_map/cost_share/pallas_call | solution.py:132
  93.7 1.6 %collective-permute-start.34 = (f32[512,128]{1,0:T(8,128)S(1)}, f32[512,128]{1,0:T(8,128)S(1)}, u32[]{:S(2)}, u32[]{:S(2)}) collective-permute-start(f32[512,128]{1,0:T(8,128)S(1)} %add.147), channel_id=1, source_target_pairs={{0,2},{1,3},{2,0},{3,1},{4,6},{5,7},{6,4},{7,5},{8,10},{9,11},{10,... | collective-permute-start | bytes 786440 | tf_op jit(solution)/shard_map/ppermute | solution.py:374
  95.2 3.5 %early.1 = (f32[1024,640]{1,0:T(8,128)S(1)}, f32[1024,128]{1,0:T(8,128)S(1)}, f32[1024,128]{1,0:T(8,128)S(1)}) custom-call(s32[3]{0:T(128)S(1)} %pad_add_fusion.core_ref.ids_ref, f32[512,128]{1,0:T(8,128)S(1)} %add.124.refs_0_, f32[512,128]{1,0:T(8,128)S(1)} %add.136.refs_1_, f32[512,128]{1,0:T(8,128)S(1)} %add.138.refs_2_, f32[512,128]{1,0:T(8,128)S(1)} %add.140.refs_3_, ...), custom_call_target="tpu_custom_call" | custom-call | flops 4000000000 | bytes 10000000 | tf_op jit(solution)/shard_map/early/pallas_call | solution.py:401
  99.5 3.6 %collective-permute-done.34 = f32[512,128]{1,0:T(8,128)S(1)} collective-permute-done((f32[512,128]{1,0:T(8,128)S(1)}, f32[512,128]{1,0:T(8,128)S(1)}, u32[]{:S(2)}, u32[]{:S(2)}) %collective-permute-start.34) | collective-permute-done | bytes 262176 | tf_op jit(solution)/shard_map/ppermute | solution.py:374
  103.3 1.5 %collective-permute-done.37.refs_5_ = f32[512,128]{1,0:T(8,128)S(1)} collective-permute-done((f32[512,128]{1,0:T(8,128)S(1)}, f32[512,128]{1,0:T(8,128)S(1)}, u32[]{:S(2)}, u32[]{:S(2)}) %collective-permute-start.37) | collective-permute-done | bytes 262176 | tf_op jit(solution)/shard_map/ppermute | solution.py:374
  104.8 3.5 %late.1 = (f32[1024,1024]{1,0:T(8,128)S(1)}, f32[1024,128]{1,0:T(8,128)S(1)}, f32[8,8,128]{2,1,0:T(8,128)S(1)}) custom-call(s32[3]{0:T(128)S(1)} %pad_add_fusion.core_ref.ids_ref, f32[1024,640]{1,0:T(8,128)S(1)} %get-tuple-element.81.early_ref, f32[1024,128]{1,0:T(8,128)S(1)} %get-tuple-element.82.old_peak_ref, ...), custom_call_target="tpu_custom_call" | custom-call | tf_op jit(solution)/shard_map/late/pallas_call | solution.py:481
  108.2 11.3 %all_to_all.15.got_ref = f32[8,8,128]{2,1,0:T(8,128)S(1)} all-to-all(f32[8,8,128]{2,1,0:T(8,128)S(1)} %get-tuple-element.95), channel_id=1, replica_groups=mesh['scen'=8,'rep'=4] {'scen'}, dimensions={0} | all-to-all | bytes 65536 | tf_op jit(solution)/shard_map/all_to_all | solution.py:476
  119.5 1.6 %step.1 = f32[8,8,128]{2,1,0:T(8,128)S(1)} custom-call(s32[3]{0:T(128)S(1)} %pad_add_fusion.core_ref.ids_ref, f32[8,8,128]{2,1,0:T(8,128)S(1)} %all_to_all.15.got_ref, f32[1024,1024]{1,0:T(8,128)S(1)} %get-tuple-element.96.e_ref), custom_call_target="tpu_custom_call" | custom-call | tf_op jit(solution)/shard_map/step/pallas_call | solution.py:491
  121.1 9.1 %all_to_all.16.got_ref = f32[8,8,128]{2,1,0:T(8,128)S(1)} all-to-all(f32[8,8,128]{2,1,0:T(8,128)S(1)} %step.1), channel_id=1, replica_groups=mesh['scen'=8,'rep'=4] {'scen'}, dimensions={0} | all-to-all | bytes 65536 | tf_op jit(solution)/shard_map/all_to_all | solution.py:476
  130.2 2.4 %last.1 = (f32[8,8,128]{2,1,0:T(8,128)S(1)}, f32[8,128]{1,0:T(8,128)}, f32[1024,1024]{1,0:T(8,128)S(1)}) custom-call(s32[3]{0:T(128)S(1)} %pad_add_fusion.core_ref.ids_ref, f32[8,8,128]{2,1,0:T(8,128)S(1)} %all_to_all.16.got_ref, f32[1024,1024]{1,0:T(8,128)S(1)} %get-tuple-element.96.e_ref, f32[1024,128]{1,0:T(8,128)S(1)} %get-tuple-element.97.peak_ref), custom_call_target="tpu_custom_call" | custom-call | tf_op jit(solution)/shard_map/last/pallas_call | solution.py:499
  132.6 9.0 %all_to_all.17.got_ref = f32[8,8,128]{2,1,0:T(8,128)S(1)} all-to-all(f32[8,8,128]{2,1,0:T(8,128)S(1)} %get-tuple-element.99), channel_id=1, replica_groups=mesh['scen'=8,'rep'=4] {'scen'}, dimensions={0} | all-to-all | bytes 65536 | tf_op jit(solution)/shard_map/all_to_all | solution.py:476
  141.6 2.2 %out.1 = (f32[1,256]{1,0:T(1,128)}, bf16[256,1024]{1,0:T(8,128)(2,1)}) custom-call(s32[3]{0:T(128)S(1)} %pad_add_fusion.core_ref.ids_ref, f32[8,8,128]{2,1,0:T(8,128)S(1)} %all_to_all.17.got_ref, f32[1024,1024]{1,0:T(8,128)S(1)} %get-tuple-element.100.scaled_ref, bf16[256,1024]{1,0:T(8,128)(2,1)S(1)} %fusion.perm_ref), custom_call_target="tpu_custom_call" | custom-call | tf_op jit(solution)/shard_map/out/pallas_call | solution.py:512
  (72 shorter events, 8.6 us)
Async XLA Ops:
  0.6 0.7 copy-start
  5.5 15.6 %collective-permute-start.2 = (bf16[64,4096]{1,0:T(8,128)(2,1)S(1)}, bf16[64,4096]{1,0:T(8,128)(2,1)S(1)}, u32[]{:S(2)}, u32[]{:S(2)}) collective-permute-start(bf16[64,4096]{1,0:T(8,128)(2,1)S(1)} %get-tuple-element.68.refs_0_), channel_id=1, source_target_pairs={{0,8},{8,16},{16,24},{24,28},{28,20},{20,12},{12,4},{4,0},{1,9},{9... | collective-permute-start | bytes 1572872 | tf_op jit(solution)/shard_map/ppermute | solution.py:426
  8.6 14.0 %collective-permute-start.3 = (bf16[64,4096]{1,0:T(8,128)(2,1)S(1)}, bf16[64,4096]{1,0:T(8,128)(2,1)S(1)}, u32[]{:S(2)}, u32[]{:S(2)}) collective-permute-start(bf16[64,4096]{1,0:T(8,128)(2,1)S(1)} %get-tuple-element.67.refs_1_), channel_id=1, source_target_pairs={{8,0},{16,8},{24,16},{28,24},{20,28},{12,20},{4,12},{0,4},{9,1},{1... | collective-permute-start | bytes 1572872 | tf_op jit(solution)/shard_map/ppermute | solution.py:426
  13.2 5.3 %copy-start.1 = (s32[1024]{0:T(1024)S(1)}, s32[1024]{0:T(1024)}, u32[]{:S(2)}) copy-start(s32[1024]{0:T(1024)} %param.3) | copy-start | bytes 12292
  16.3 2.7 %collective-permute-start = (f32[512,128]{1,0:T(8,128)S(1)}, f32[512,128]{1,0:T(8,128)S(1)}, u32[]{:S(2)}, u32[]{:S(2)}) collective-permute-start(f32[512,128]{1,0:T(8,128)S(1)} %get-tuple-element.61), channel_id=1, source_target_pairs={{0,1},{1,0},{2,3},{3,2},{4,5},{5,4},{6,7},{7,6},{8,9},{9,8},{10,11... | collective-permute-start | bytes 786440 | tf_op jit(solution)/shard_map/ppermute | solution.py:374
  16.4 15.9 %collective-permute-start.6 = (bf16[64,4096]{1,0:T(8,128)(2,1)S(1)}, bf16[64,4096]{1,0:T(8,128)(2,1)S(1)}, u32[]{:S(2)}, u32[]{:S(2)}) collective-permute-start(bf16[64,4096]{1,0:T(8,128)(2,1)S(1)} %get-tuple-element.67.refs_1_), channel_id=1, source_target_pairs={{0,8},{8,16},{16,24},{24,28},{28,20},{20,12},{12,4},{4,0},{1,9},{9... | collective-permute-start | bytes 1572872 | tf_op jit(solution)/shard_map/ppermute | solution.py:426
  18.5 15.3 %collective-permute-start.7 = (bf16[64,4096]{1,0:T(8,128)(2,1)S(1)}, bf16[64,4096]{1,0:T(8,128)(2,1)S(1)}, u32[]{:S(2)}, u32[]{:S(2)}) collective-permute-start(bf16[64,4096]{1,0:T(8,128)(2,1)S(1)} %get-tuple-element.68.refs_0_), channel_id=1, source_target_pairs={{8,0},{16,8},{24,16},{28,24},{20,28},{12,20},{4,12},{0,4},{9,1},{1... | collective-permute-start | bytes 1572872 | tf_op jit(solution)/shard_map/ppermute | solution.py:426
  19.1 19.7 %collective-permute-start.1 = (f32[512,128]{1,0:T(8,128)S(1)}, f32[512,128]{1,0:T(8,128)S(1)}, u32[]{:S(2)}, u32[]{:S(2)}) collective-permute-start(f32[512,128]{1,0:T(8,128)S(1)} %add.123), channel_id=1, source_target_pairs={{0,2},{1,3},{2,0},{3,1},{4,6},{5,7},{6,4},{7,5},{8,10},{9,11},{10,... | collective-permute-start | bytes 786440 | tf_op jit(solution)/shard_map/ppermute | solution.py:374
  22.6 20.9 %collective-permute-start.10 = (bf16[64,4096]{1,0:T(8,128)(2,1)S(1)}, bf16[64,4096]{1,0:T(8,128)(2,1)S(1)}, u32[]{:S(2)}, u32[]{:S(2)}) collective-permute-start(bf16[64,4096]{1,0:T(8,128)(2,1)S(1)} %collective-permute-done.2.refs_0_), channel_id=1, source_target_pairs={{0,8},{8,16},{16,24},{24,28},{28,20},{20,12},{12,4},{4,0},{1,9},{9... | collective-permute-start | bytes 1572872 | tf_op jit(solution)/shard_map/ppermute | solution.py:426
  24.2 20.9 %collective-permute-start.11 = (bf16[64,4096]{1,0:T(8,128)(2,1)S(1)}, bf16[64,4096]{1,0:T(8,128)(2,1)S(1)}, u32[]{:S(2)}, u32[]{:S(2)}) collective-permute-start(bf16[64,4096]{1,0:T(8,128)(2,1)S(1)} %collective-permute-done.3.refs_1_), channel_id=1, source_target_pairs={{8,0},{16,8},{24,16},{28,24},{20,28},{12,20},{4,12},{0,4},{9,1},{1... | collective-permute-start | bytes 1572872 | tf_op jit(solution)/shard_map/ppermute | solution.py:426
  32.3 4.8 %collective-permute-start.4 = (f32[512,128]{1,0:T(8,128)S(1)}, f32[512,128]{1,0:T(8,128)S(1)}, u32[]{:S(2)}, u32[]{:S(2)}) collective-permute-start(f32[512,128]{1,0:T(8,128)S(1)} %get-tuple-element.66), channel_id=1, source_target_pairs={{0,1},{1,0},{2,3},{3,2},{4,5},{5,4},{6,7},{7,6},{8,9},{9,8},{10,11... | collective-permute-start | bytes 786440 | tf_op jit(solution)/shard_map/ppermute | solution.py:374
  37.0 3.3 %collective-permute-start.8 = (f32[512,128]{1,0:T(8,128)S(1)}, f32[512,128]{1,0:T(8,128)S(1)}, u32[]{:S(2)}, u32[]{:S(2)}) collective-permute-start(f32[512,128]{1,0:T(8,128)S(1)} %get-tuple-element.72), channel_id=1, source_target_pairs={{0,1},{1,0},{2,3},{3,2},{4,5},{5,4},{6,7},{7,6},{8,9},{9,8},{10,11... | collective-permute-start | bytes 786440 | tf_op jit(solution)/shard_map/ppermute | solution.py:374
  37.1 9.5 %collective-permute-start.5 = (f32[512,128]{1,0:T(8,128)S(1)}, f32[512,128]{1,0:T(8,128)S(1)}, u32[]{:S(2)}, u32[]{:S(2)}) collective-permute-start(f32[512,128]{1,0:T(8,128)S(1)} %add.135), channel_id=1, source_target_pairs={{0,2},{1,3},{2,0},{3,1},{4,6},{5,7},{6,4},{7,5},{8,10},{9,11},{10,... | collective-permute-start | bytes 786440 | tf_op jit(solution)/shard_map/ppermute | solution.py:374
  38.7 16.0 %collective-permute-start.14 = (bf16[64,4096]{1,0:T(8,128)(2,1)S(1)}, bf16[64,4096]{1,0:T(8,128)(2,1)S(1)}, u32[]{:S(2)}, u32[]{:S(2)}) collective-permute-start(bf16[64,4096]{1,0:T(8,128)(2,1)S(1)} %collective-permute-done.6.refs_1_), channel_id=1, source_target_pairs={{0,8},{8,16},{16,24},{24,28},{28,20},{20,12},{12,4},{4,0},{1,9},{9... | collective-permute-start | bytes 1572872 | tf_op jit(solution)/shard_map/ppermute | solution.py:426
  40.3 16.0 %collective-permute-start.15 = (bf16[64,4096]{1,0:T(8,128)(2,1)S(1)}, bf16[64,4096]{1,0:T(8,128)(2,1)S(1)}, u32[]{:S(2)}, u32[]{:S(2)}) collective-permute-start(bf16[64,4096]{1,0:T(8,128)(2,1)S(1)} %collective-permute-done.7.refs_0_), channel_id=1, source_target_pairs={{8,0},{16,8},{24,16},{28,24},{20,28},{12,20},{4,12},{0,4},{9,1},{1... | collective-permute-start | bytes 1572872 | tf_op jit(solution)/shard_map/ppermute | solution.py:426
  43.5 7.8 %collective-permute-start.16 = (f32[512,128]{1,0:T(8,128)S(1)}, f32[512,128]{1,0:T(8,128)S(1)}, u32[]{:S(2)}, u32[]{:S(2)}) collective-permute-start(f32[512,128]{1,0:T(8,128)S(1)} %add.124.refs_0_), channel_id=1, source_target_pairs={{0,1},{1,0},{2,3},{3,2},{4,5},{5,4},{6,7},{7,6},{8,9},{9,8},{10,11... | collective-permute-start | bytes 786440 | tf_op jit(solution)/shard_map/ppermute | solution.py:374
  45.1 14.5 %collective-permute-start.9 = (f32[512,128]{1,0:T(8,128)S(1)}, f32[512,128]{1,0:T(8,128)S(1)}, u32[]{:S(2)}, u32[]{:S(2)}) collective-permute-start(f32[512,128]{1,0:T(8,128)S(1)} %add.137), channel_id=1, source_target_pairs={{0,2},{1,3},{2,0},{3,1},{4,6},{5,7},{6,4},{7,5},{8,10},{9,11},{10,... | collective-permute-start | bytes 786440 | tf_op jit(solution)/shard_map/ppermute | solution.py:374
  46.6 19.4 %collective-permute-start.23 = (bf16[64,4096]{1,0:T(8,128)(2,1)S(1)}, bf16[64,4096]{1,0:T(8,128)(2,1)S(1)}, u32[]{:S(2)}, u32[]{:S(2)}) collective-permute-start(bf16[64,4096]{1,0:T(8,128)(2,1)S(1)} %collective-permute-done.10.refs_0_), channel_id=1, source_target_pairs={{0,8},{8,16},{16,24},{24,28},{28,20},{20,12},{12,4},{4,0},{1,9},{9... | collective-permute-start | bytes 1572872 | tf_op jit(solution)/shard_map/ppermute | solution.py:426
  51.4 16.2 %collective-permute-start.24 = (bf16[64,4096]{1,0:T(8,128)(2,1)S(1)}, bf16[64,4096]{1,0:T(8,128)(2,1)S(1)}, u32[]{:S(2)}, u32[]{:S(2)}) collective-permute-start(bf16[64,4096]{1,0:T(8,128)(2,1)S(1)} %collective-permute-done.11.refs_1_), channel_id=1, source_target_pairs={{8,0},{16,8},{24,16},{28,24},{20,28},{12,20},{4,12},{0,4},{9,1},{1... | collective-permute-start | bytes 1572872 | tf_op jit(solution)/shard_map/ppermute | solution.py:426
  54.8 5.3 %collective-permute-start.12 = (f32[512,128]{1,0:T(8,128)S(1)}, f32[512,128]{1,0:T(8,128)S(1)}, u32[]{:S(2)}, u32[]{:S(2)}) collective-permute-start(f32[512,128]{1,0:T(8,128)S(1)} %get-tuple-element.76), channel_id=1, source_target_pairs={{0,1},{1,0},{2,3},{3,2},{4,5},{5,4},{6,7},{7,6},{8,9},{9,8},{10,11... | collective-permute-start | bytes 786440 | tf_op jit(solution)/shard_map/ppermute | solution.py:374
  59.5 2.3 %collective-permute-start.17 = (f32[512,128]{1,0:T(8,128)S(1)}, f32[512,128]{1,0:T(8,128)S(1)}, u32[]{:S(2)}, u32[]{:S(2)}) collective-permute-start(f32[512,128]{1,0:T(8,128)S(1)} %get-tuple-element.80), channel_id=1, source_target_pairs={{0,1},{1,0},{2,3},{3,2},{4,5},{5,4},{6,7},{7,6},{8,9},{9,8},{10,11... | collective-permute-start | bytes 786440 | tf_op jit(solution)/shard_map/ppermute | solution.py:374
  59.6 2.7 %collective-permute-start.19 = (f32[512,128]{1,0:T(8,128)S(1)}, f32[512,128]{1,0:T(8,128)S(1)}, u32[]{:S(2)}, u32[]{:S(2)}) collective-permute-start(f32[512,128]{1,0:T(8,128)S(1)} %add.136.refs_1_), channel_id=1, source_target_pairs={{0,1},{1,0},{2,3},{3,2},{4,5},{5,4},{6,7},{7,6},{8,9},{9,8},{10,11... | collective-permute-start | bytes 786440 | tf_op jit(solution)/shard_map/ppermute | solution.py:374
  60.1 17.1 %collective-permute-start.27 = (bf16[64,4096]{1,0:T(8,128)(2,1)S(1)}, bf16[64,4096]{1,0:T(8,128)(2,1)S(1)}, u32[]{:S(2)}, u32[]{:S(2)}) collective-permute-start(bf16[64,4096]{1,0:T(8,128)(2,1)S(1)} %collective-permute-done.14.refs_1_), channel_id=1, source_target_pairs={{0,8},{8,16},{16,24},{24,28},{28,20},{20,12},{12,4},{4,0},{1,9},{9... | collective-permute-start | bytes 1572872 | tf_op jit(solution)/shard_map/ppermute | solution.py:426
  61.8 17.0 %collective-permute-start.28 = (bf16[64,4096]{1,0:T(8,128)(2,1)S(1)}, bf16[64,4096]{1,0:T(8,128)(2,1)S(1)}, u32[]{:S(2)}, u32[]{:S(2)}) collective-permute-start(bf16[64,4096]{1,0:T(8,128)(2,1)S(1)} %collective-permute-done.15.refs_0_), channel_id=1, source_target_pairs={{8,0},{16,8},{24,16},{28,24},{20,28},{12,20},{4,12},{0,4},{9,1},{1... | collective-permute-start | bytes 1572872 | tf_op jit(solution)/shard_map/ppermute | solution.py:426
  62.3 9.0 %collective-permute-start.18 = (f32[512,128]{1,0:T(8,128)S(1)}, f32[512,128]{1,0:T(8,128)S(1)}, u32[]{:S(2)}, u32[]{:S(2)}) collective-permute-start(f32[512,128]{1,0:T(8,128)S(1)} %add.141), channel_id=1, source_target_pairs={{0,2},{1,3},{2,0},{3,1},{4,6},{5,7},{6,4},{7,5},{8,10},{9,11},{10,... | collective-permute-start | bytes 786440 | tf_op jit(solution)/shard_map/ppermute | solution.py:374
  70.7 2.1 %collective-permute-start.25 = (f32[512,128]{1,0:T(8,128)S(1)}, f32[512,128]{1,0:T(8,128)S(1)}, u32[]{:S(2)}, u32[]{:S(2)}) collective-permute-start(f32[512,128]{1,0:T(8,128)S(1)} %get-tuple-element.87), channel_id=1, source_target_pairs={{0,1},{1,0},{2,3},{3,2},{4,5},{5,4},{6,7},{7,6},{8,9},{9,8},{10,11... | collective-permute-start | bytes 786440 | tf_op jit(solution)/shard_map/ppermute | solution.py:374
  70.8 3.7 %collective-permute-start.20 = (f32[512,128]{1,0:T(8,128)S(1)}, f32[512,128]{1,0:T(8,128)S(1)}, u32[]{:S(2)}, u32[]{:S(2)}) collective-permute-start(f32[512,128]{1,0:T(8,128)S(1)} %add.138.refs_2_), channel_id=1, source_target_pairs={{0,1},{1,0},{2,3},{3,2},{4,5},{5,4},{6,7},{7,6},{8,9},{9,8},{10,11... | collective-permute-start | bytes 786440 | tf_op jit(solution)/shard_map/ppermute | solution.py:374
  71.3 11.2 %collective-permute-start.13 = (f32[512,128]{1,0:T(8,128)S(1)}, f32[512,128]{1,0:T(8,128)S(1)}, u32[]{:S(2)}, u32[]{:S(2)}) collective-permute-start(f32[512,128]{1,0:T(8,128)S(1)} %add.139), channel_id=1, source_target_pairs={{0,2},{1,3},{2,0},{3,1},{4,6},{5,7},{6,4},{7,5},{8,10},{9,11},{10,... | collective-permute-start | bytes 786440 | tf_op jit(solution)/shard_map/ppermute | solution.py:374
  72.9 15.0 %collective-permute-start.31 = (bf16[64,4096]{1,0:T(8,128)(2,1)S(1)}, bf16[64,4096]{1,0:T(8,128)(2,1)S(1)}, u32[]{:S(2)}, u32[]{:S(2)}) collective-permute-start(bf16[64,4096]{1,0:T(8,128)(2,1)S(1)} %collective-permute-done.23.refs_0_), channel_id=1, source_target_pairs={{0,8},{8,16},{16,24},{24,28},{28,20},{20,12},{12,4},{4,0},{1,9},{9... | collective-permute-start | bytes 1572872 | tf_op jit(solution)/shard_map/ppermute | solution.py:426
  74.5 14.9 %collective-permute-start.32 = (bf16[64,4096]{1,0:T(8,128)(2,1)S(1)}, bf16[64,4096]{1,0:T(8,128)(2,1)S(1)}, u32[]{:S(2)}, u32[]{:S(2)}) collective-permute-start(bf16[64,4096]{1,0:T(8,128)(2,1)S(1)} %collective-permute-done.24.refs_1_), channel_id=1, source_target_pairs={{8,0},{16,8},{24,16},{28,24},{20,28},{12,20},{4,12},{0,4},{9,1},{1... | collective-permute-start | bytes 1572872 | tf_op jit(solution)/shard_map/ppermute | solution.py:426
  81.9 1.6 %collective-permute-start.29 = (f32[512,128]{1,0:T(8,128)S(1)}, f32[512,128]{1,0:T(8,128)S(1)}, u32[]{:S(2)}, u32[]{:S(2)}) collective-permute-start(f32[512,128]{1,0:T(8,128)S(1)} %get-tuple-element.91), channel_id=1, source_target_pairs={{0,1},{1,0},{2,3},{3,2},{4,5},{5,4},{6,7},{7,6},{8,9},{9,8},{10,11... | collective-permute-start | bytes 786440 | tf_op jit(solution)/shard_map/ppermute | solution.py:374
  82.0 3.1 %collective-permute-start.22 = (f32[512,128]{1,0:T(8,128)S(1)}, f32[512,128]{1,0:T(8,128)S(1)}, u32[]{:S(2)}, u32[]{:S(2)}) collective-permute-start(f32[512,128]{1,0:T(8,128)S(1)} %add.142.refs_4_), channel_id=1, source_target_pairs={{0,1},{1,0},{2,3},{3,2},{4,5},{5,4},{6,7},{7,6},{8,9},{9,8},{10,11... | collective-permute-start | bytes 786440 | tf_op jit(solution)/shard_map/ppermute | solution.py:374
  82.6 3.1 %collective-permute-start.21 = (f32[512,128]{1,0:T(8,128)S(1)}, f32[512,128]{1,0:T(8,128)S(1)}, u32[]{:S(2)}, u32[]{:S(2)}) collective-permute-start(f32[512,128]{1,0:T(8,128)S(1)} %add.140.refs_3_), channel_id=1, source_target_pairs={{0,1},{1,0},{2,3},{3,2},{4,5},{5,4},{6,7},{7,6},{8,9},{9,8},{10,11... | collective-permute-start | bytes 786440 | tf_op jit(solution)/shard_map/ppermute | solution.py:374
  83.6 15.2 %collective-permute-start.26 = (f32[512,128]{1,0:T(8,128)S(1)}, f32[512,128]{1,0:T(8,128)S(1)}, u32[]{:S(2)}, u32[]{:S(2)}) collective-permute-start(f32[512,128]{1,0:T(8,128)S(1)} %add.143), channel_id=1, source_target_pairs={{0,2},{1,3},{2,0},{3,1},{4,6},{5,7},{6,4},{7,5},{8,10},{9,11},{10,... | collective-permute-start | bytes 786440 | tf_op jit(solution)/shard_map/ppermute | solution.py:374
  85.1 14.0 %collective-permute-start.30 = (f32[512,128]{1,0:T(8,128)S(1)}, f32[512,128]{1,0:T(8,128)S(1)}, u32[]{:S(2)}, u32[]{:S(2)}) collective-permute-start(f32[512,128]{1,0:T(8,128)S(1)} %add.145), channel_id=1, source_target_pairs={{0,2},{1,3},{2,0},{3,1},{4,6},{5,7},{6,4},{7,5},{8,10},{9,11},{10,... | collective-permute-start | bytes 786440 | tf_op jit(solution)/shard_map/ppermute | solution.py:374
  91.5 2.2 %collective-permute-start.33 = (f32[512,128]{1,0:T(8,128)S(1)}, f32[512,128]{1,0:T(8,128)S(1)}, u32[]{:S(2)}, u32[]{:S(2)}) collective-permute-start(f32[512,128]{1,0:T(8,128)S(1)} %cost_share.16), channel_id=1, source_target_pairs={{0,1},{1,0},{2,3},{3,2},{4,5},{5,4},{6,7},{7,6},{8,9},{9,8},{10,11... | collective-permute-start | bytes 786440 | tf_op jit(solution)/shard_map/ppermute | solution.py:374
  93.7 9.5 %collective-permute-start.34 = (f32[512,128]{1,0:T(8,128)S(1)}, f32[512,128]{1,0:T(8,128)S(1)}, u32[]{:S(2)}, u32[]{:S(2)}) collective-permute-start(f32[512,128]{1,0:T(8,128)S(1)} %add.147), channel_id=1, source_target_pairs={{0,2},{1,3},{2,0},{3,1},{4,6},{5,7},{6,4},{7,5},{8,10},{9,11},{10,... | collective-permute-start | bytes 786440 | tf_op jit(solution)/shard_map/ppermute | solution.py:374
  98.8 4.4 %collective-permute-start.35 = (f32[512,128]{1,0:T(8,128)S(1)}, f32[512,128]{1,0:T(8,128)S(1)}, u32[]{:S(2)}, u32[]{:S(2)}) collective-permute-start(f32[512,128]{1,0:T(8,128)S(1)} %add.144.refs_0_), channel_id=1, source_target_pairs={{0,1},{1,0},{2,3},{3,2},{4,5},{5,4},{6,7},{7,6},{8,9},{9,8},{10,11... | collective-permute-start | bytes 786440 | tf_op jit(solution)/shard_map/ppermute | solution.py:374
  99.1 4.1 %collective-permute-start.36 = (f32[512,128]{1,0:T(8,128)S(1)}, f32[512,128]{1,0:T(8,128)S(1)}, u32[]{:S(2)}, u32[]{:S(2)}) collective-permute-start(f32[512,128]{1,0:T(8,128)S(1)} %add.146.refs_1_), channel_id=1, source_target_pairs={{0,1},{1,0},{2,3},{3,2},{4,5},{5,4},{6,7},{7,6},{8,9},{9,8},{10,11... | collective-permute-start | bytes 786440 | tf_op jit(solution)/shard_map/ppermute | solution.py:374
  103.2 1.6 %collective-permute-start.37 = (f32[512,128]{1,0:T(8,128)S(1)}, f32[512,128]{1,0:T(8,128)S(1)}, u32[]{:S(2)}, u32[]{:S(2)}) collective-permute-start(f32[512,128]{1,0:T(8,128)S(1)} %add.148.refs_2_), channel_id=1, source_target_pairs={{0,1},{1,0},{2,3},{3,2},{4,5},{5,4},{6,7},{7,6},{8,9},{9,8},{10,11... | collective-permute-start | bytes 786440 | tf_op jit(solution)/shard_map/ppermute | solution.py:374

commit v4 on v3

--- a/solution.py
+++ b/solution.py
@@ -16,7 +16,7 @@
 NT = (((1,), (1,)), ((), ()))
 VMEM = pl.BlockSpec(memory_space=pltpu.VMEM)
 SMEM = pl.BlockSpec(memory_space=pltpu.SMEM)
-AFTER = {0: (2, 3, 4), 5: (2, 0, 4), 4: (1, 2, 3), 3: (1, 0, 0), 2: (1, 0, 0), 1: (0, 0, 0)}
+AFTER = {0: (2, 3, 4), 5: (2, 0, 4), 4: (1, 2, 3), 3: (1, 2, 0), 2: (1, 0, 0), 1: (0, 0, 0)}
 COST = pl.CostEstimate(flops=4 * 10**9, bytes_accessed=10**7, transcendentals=0)
 ROOM = pltpu.CompilerParams(vmem_limit_bytes=10 * 2**20)
 
@@ -25,21 +25,28 @@
     return [pltpu.with_memory_space_constraint(x, pltpu.VMEM) for x in xs]
 
 
-def square_sums(x):
-    gram = lax.dot_general(x, x, NT, preferred_element_type=jnp.float32)
-    n = x.shape[0]
+def square_sums(chunks):
+    sums = []
+    for c in chunks:
+        x = c[...].astype(jnp.float32)
+        sums.append(jnp.sum(x * x, axis=1, keepdims=True))
+    column = jnp.concatenate(sums, axis=0)
+    n = column.shape[0]
     eye = lax.broadcasted_iota(jnp.int32, (n, n), 0) == lax.broadcasted_iota(jnp.int32, (n, n), 1)
-    return jnp.sum(jnp.where(eye, gram, 0.0), axis=0, keepdims=True)
-
-
-def pick_kernel(index_ref, scen_ref, kept_ref, low_ref, high_ref, col_ref, sel_ref, sems, *, step):
+    return jnp.sum(jnp.where(eye, column, 0.0), axis=0, keepdims=True)
+
+
+def pick_kernel(index_hbm, scen_ref, kept_ref, low_ref, high_ref, index_ref, col_ref, sel_ref, sems, *, step):
     rows_all, width = scen_ref.shape
     copies = [
         pltpu.make_async_copy(scen_ref.at[:, at : at + step], kept_ref.at[:, at : at + step], sems.at[i])
         for i, at in enumerate(range(0, width, step))
     ]
+    fetch = pltpu.make_async_copy(index_hbm, index_ref, sems.at[len(copies)])
+    fetch.start()
     for copy in copies:
         copy.start()
+    fetch.wait()
     local = index_ref[...] - lax.axis_index("scen") * rows_all
     local = jnp.where(local >= 0, local, 2 * rows_all)
     tiles = [jnp.broadcast_to(local[i : i + 1, :], (SUB, LANES)) for i in range(local.shape[0])]
@@ -73,22 +80,23 @@
 
 def pick(rep_index, scenarios, per):
     rows, width = scenarios.shape
-    step = min(512, width)
+    step = min(1024, width)
     some = pltpu.VMEM((per // 2, width), scenarios.dtype)
     return pl.pallas_call(
         functools.partial(pick_kernel, step=step),
         out_shape=(pltpu.VMEM((rows, width), scenarios.dtype), some, some),
-        in_specs=[VMEM, pl.BlockSpec(memory_space=pltpu.HBM)],
+        in_specs=[pl.BlockSpec(memory_space=pltpu.HBM)] * 2,
         out_specs=(VMEM,) * 3,
         scratch_shapes=[
+            pltpu.VMEM((rep_index.size // LANES, LANES), rep_index.dtype),
             pltpu.VMEM((rows, LANES), jnp.float32),
             pltpu.VMEM((per, rows), scenarios.dtype),
-            pltpu.SemaphoreType.DMA((width // step,)),
+            pltpu.SemaphoreType.DMA((width // step + 1,)),
         ],
         cost_estimate=COST,
         compiler_params=ROOM,
         name="pick",
-    )(rep_index.reshape(-1, LANES), pltpu.with_memory_space_constraint(scenarios, pltpu.HBM))
+    )(*(pltpu.with_memory_space_constraint(x, pltpu.HBM) for x in (rep_index.reshape(-1, LANES), scenarios)))
 
 
 def norm_kernel(scen_ref, out_ref):
@@ -116,7 +124,7 @@
 def cost_kernel(core_ref, scen_ref, sq_ref, *refs, tile, parts):
     chunks, outs = refs[: -len(parts)], refs[-len(parts) :]
     reps = jnp.concatenate([c[...] for c in chunks], axis=0)
-    sq_rep = square_sums(reps)
+    sq_rep = square_sums(chunks)
     half = outs[0].shape[0]
     for flip, out_ref in zip(parts, outs, strict=True):
         which = 1 - core_ref[0] if flip else core_ref[0]
@@ -168,7 +176,8 @@
     return [jnp.broadcast_to(w[i : i + 1, :], (SUB, LANES)) for i in range(w.shape[0])]
 
 
-GROUP = 16
+def group_of(rows):
+    return math.gcd(64, rows // SUB)
 
 
 def load(ref, rows):
@@ -180,8 +189,8 @@
         ref[rows, k * LANES : (k + 1) * LANES] = x
 
 
-def group_rows(i, g, base=0):
-    return pl.ds(pl.multiple_of(base + (i * GROUP + g) * SUB, SUB), SUB)
+def group_rows(i, g, group, base=0):
+    return pl.ds(pl.multiple_of(base + (i * group + g) * SUB, SUB), SUB)
 
 
 def cost_tiles(refs, pieces, src, here, left, scale):
@@ -201,47 +210,49 @@
     *refs, e_ref, peak_ref, sum_ref = refs
     half = refs[0].shape[0]
     left = lax.broadcasted_iota(jnp.int32, (SUB, LANES), 1) < LANES // 2
+    group = group_of(half)
 
     def body(i, carry, h):
         peaks, sums = [], []
-        for g in range(GROUP):
-            z = cost_tiles(refs, pieces, group_rows(i, g), ids_ref[0] == h, left, scale)
-            store(e_ref, group_rows(i, g, h * half), z)
+        for g in range(group):
+            z = cost_tiles(refs, pieces, group_rows(i, g, group), ids_ref[0] == h, left, scale)
+            store(e_ref, group_rows(i, g, group, h * half), z)
             peaks.append(tree(jnp.maximum, z))
         peaks = [jnp.max(p, axis=1, keepdims=True) for p in peaks]
-        for g in range(GROUP):
-            dst = group_rows(i, g, h * half)
+        for g in range(group):
+            dst = group_rows(i, g, group, h * half)
             e = [jnp.exp2(x - peaks[g]) for x in load(e_ref, dst)]
             store(e_ref, dst, e)
             peak_ref[dst, :] = jnp.broadcast_to(peaks[g], (SUB, LANES))
             sums.append(tree(jnp.add, e))
-        for g in range(GROUP):
+        for g in range(group):
             total = jnp.sum(sums[g], axis=1, keepdims=True)
-            sum_ref[group_rows(i, g, h * half), :] = jnp.broadcast_to(total, (SUB, LANES))
+            sum_ref[group_rows(i, g, group, h * half), :] = jnp.broadcast_to(total, (SUB, LANES))
         return carry
 
     for h in range(2):
-        lax.fori_loop(0, half // (GROUP * SUB), functools.partial(body, h=h), 0)
+        lax.fori_loop(0, half // (group * SUB), functools.partial(body, h=h), 0)
 
 
 def late_kernel(ids_ref, early_ref, old_peak_ref, old_sum_ref, *refs, pieces, order, scale, rolled):
     *refs, e_ref, peak_ref, out_ref = refs
     half = refs[0].shape[0]
     left = lax.broadcasted_iota(jnp.int32, (SUB, LANES), 1) < LANES // 2
+    group = group_of(half)
     early = early_ref.shape[1] // LANES
     at = [slice(k * LANES, (k + 1) * LANES) for k in order]
 
     def body(i, acc, h):
         peaks, sums, factors = [], [], []
-        for g in range(GROUP):
-            dst = group_rows(i, g, h * half)
-            z = cost_tiles(refs, pieces, group_rows(i, g), ids_ref[0] == h, left, scale)
+        for g in range(group):
+            dst = group_rows(i, g, group, h * half)
+            z = cost_tiles(refs, pieces, group_rows(i, g, group), ids_ref[0] == h, left, scale)
             for k, x in zip(at[early:], z, strict=True):
                 e_ref[dst, k] = x
             peaks.append(tree(jnp.maximum, z))
         peaks = [jnp.max(p, axis=1, keepdims=True) for p in peaks]
-        for g in range(GROUP):
-            dst = group_rows(i, g, h * half)
+        for g in range(group):
+            dst = group_rows(i, g, group, h * half)
             peak = jnp.maximum(old_peak_ref[dst, :], peaks[g])
             factor = jnp.exp2(old_peak_ref[dst, :] - peak)
             peak_ref[dst, :] = peak
@@ -251,8 +262,8 @@
                 e_ref[dst, k] = x
             sums.append(tree(jnp.add, e))
         sums = [jnp.sum(x, axis=1, keepdims=True) for x in sums]
-        for g in range(GROUP):
-            dst = group_rows(i, g, h * half)
+        for g in range(group):
+            dst = group_rows(i, g, group, h * half)
             q = 1.0 / (old_sum_ref[dst, :] * factors[g] + sums[g])
             e = [x * factors[g] for x in load(early_ref, dst)]
             for k, x in zip(at[:early], e, strict=True):
@@ -263,37 +274,39 @@
 
     acc = tuple(jnp.zeros((SUB, LANES), jnp.float32) for _ in order)
     for h in range(2):
-        acc = lax.fori_loop(0, half // (GROUP * SUB), functools.partial(body, h=h), acc)
+        acc = lax.fori_loop(0, half // (group * SUB), functools.partial(body, h=h), acc)
     acc = [acc[order.index(k)] for k in range(len(order))]
     put_sums(acc, out_ref, ids_ref[1] if rolled else None)
 
 
 def step_kernel(ids_ref, got_ref, e_ref, out_ref, *, scale, rolled):
     tiles = e_ref.shape[1] // LANES
+    group = group_of(e_ref.shape[0])
     w = spread(get_factors(got_ref, scale, ids_ref[2] if rolled else None))
 
     def body(i, acc):
-        sums = [tree(jnp.add, [x * f for x, f in zip(load(e_ref, group_rows(i, g)), w)]) for g in range(GROUP)]
+        sums = [tree(jnp.add, [x * f for x, f in zip(load(e_ref, group_rows(i, g, group)), w)]) for g in range(group)]
         sums = [1.0 / jnp.sum(x, axis=1, keepdims=True) for x in sums]
-        for g in range(GROUP):
-            acc = [a + x * sums[g] for a, x in zip(acc, load(e_ref, group_rows(i, g)))]
+        for g in range(group):
+            acc = [a + x * sums[g] for a, x in zip(acc, load(e_ref, group_rows(i, g, group)))]
         return tuple(acc)
 
     acc = tuple(jnp.zeros((SUB, LANES), jnp.float32) for _ in range(tiles))
-    acc = lax.fori_loop(0, e_ref.shape[0] // (GROUP * SUB), body, acc)
+    acc = lax.fori_loop(0, e_ref.shape[0] // (group * SUB), body, acc)
     put_sums(acc, out_ref, ids_ref[1] if rolled else None)
 
 
 def last_kernel(ids_ref, got_ref, e_ref, peak_ref, out_ref, pot_ref, scaled_ref, col_ref, *, scale, rolled, log_count):
     rows_all = e_ref.shape[0]
     tiles = e_ref.shape[1] // LANES
+    group = group_of(e_ref.shape[0])
     w = spread(get_factors(got_ref, scale, ids_ref[2] if rolled else None))
 
     def body(i, acc):
-        sums = [tree(jnp.add, [x * f for x, f in zip(load(e_ref, group_rows(i, g)), w)]) for g in range(GROUP)]
+        sums = [tree(jnp.add, [x * f for x, f in zip(load(e_ref, group_rows(i, g, group)), w)]) for g in range(group)]
         sums = [jnp.sum(x, axis=1, keepdims=True) for x in sums]
-        for g in range(GROUP):
-            rows = group_rows(i, g)
+        for g in range(group):
+            rows = group_rows(i, g, group)
             col_ref[rows, :] = -eps_blur * (log_count + math.log(2) * peak_ref[rows, :] + jnp.log(sums[g]))
             q = 1.0 / sums[g]
             e = [x * q for x in load(e_ref, rows)]
@@ -302,7 +315,7 @@
         return tuple(acc)
 
     acc = tuple(jnp.zeros((SUB, LANES), jnp.float32) for _ in range(tiles))
-    acc = lax.fori_loop(0, rows_all // (GROUP * SUB), body, acc)
+    acc = lax.fori_loop(0, rows_all // (group * SUB), body, acc)
     put_sums(acc, out_ref, ids_ref[1] if rolled else None)
     shape = (LANES, LANES)
     eye = lax.broadcasted_iota(jnp.int32, shape, 0) == lax.broadcasted_iota(jnp.int32, shape, 1)
@@ -419,7 +432,7 @@
     tie(0, 1, perm)
     a, b = halves, halves[::-1]
     a[1], b[1] = tied([a[1], b[1]], sq_scen)
-    begun = []
+    waiting = []
     for h in range(n):
         i, k = (h + 1) % 2, (h + 1) // 2
         if h:
@@ -428,15 +441,21 @@
             chunks = [b[i], a[i]] if i else [a[i], b[i]]
         if h == n - 1:
             sent = cost_share(ids, scenarios, sq_scen, chunks, parts=(True,))
-            finish(part, *sent, *begun)
             shares = [*sent, *cost_share(ids, scenarios, sq_scen, chunks, parts=(False,))]
         elif h:
-            shares = cost_share(ids, scenarios, sq_scen, chunks)
+            sent = shares = cost_share(ids, scenarios, sq_scen, chunks)
+        for g, part in waiting:
+            whole, other = finish(part, *sent, *(begun if g == n - 2 else ()))
+            tie(g, AFTER[n - g][1], whole)
+            tie(g, AFTER[n - g][2], other)
+        waiting = []
         part = shares[1] + swap(shares[0], 1)
         after = AFTER.get(n - h, AFTER[0])
         tie(h, 1, *shares)
         tie(h, after[0], part)
-        if h != n - 2:
+        if h in (n - 3, n - 2):
+            waiting.append((h, part))
+        else:
             whole, other = finish(part)
             tie(h, after[1], whole)
             tie(h, after[2], other)
@@ -444,8 +463,8 @@
             where[k] = [(h, 0)]
         elif i == 1:
             where[n - k], where[k] = [(h - 1, 0), (h, 0)], [(h, 0), (h - 1, 0)]
-        if rolled and h == n - 4:
-            begun = start_early([w for w in where if w], stages)
+        if h == n - 4:
+            begun = start_early([w for w in where if w], stages) if rolled else ()
 
     own, other = [s[0] for s in stages], [s[1] for s in stages]
     if rolled:

time: 144 us -> 139 us (0.965)
  Pallas kernels: 48.1 us -> 40.5 us
  waiting for transfers between devices: 33.1 us -> 35.2 us
    ppermute x24, waiting for transfers between devices: 6.04 us -> 9.19 us  [swap(): return lax.ppermute(x, 'rep', [(i, i ^ bit) for i in range(n_rep)])]
    pallas_call x9, Pallas kernels: 26.2 us -> 23.9 us  [cost_share(): pl.pallas_call(functools.partial(cost_kernel, tile=min(256, rows // 2), p...]
    pallas_call x1, Pallas kernels: 3.52 us -> 1.32 us  [start_early(): pl.pallas_call(functools.partial(early_kernel, pieces=pieces, scale=to_po...]
    pallas_call x1, Pallas kernels: 3.45 us -> 1.46 us  [on_device(): pl.pallas_call(functools.partial(late_kernel, pieces=pieces, order=order,...]
  transfers between devices with their start and end apart: 38 -> 38, of which waited for: 16 -> 16; matrix products, arithmetic and copies ran while one was open for 1% -> 1% of each run, Pallas kernels for 24% -> 21%
where the time goes in v4:
time: 139 us
  Pallas kernels  40.5 us (29%)
  waiting for transfers between devices  35.2 us (25%)
  starting transfers between devices  31.6 us (23%)
  blocking collectives  29.4 us (21%)
    all_to_all x3, blocking collectives, exchange(): x = lax.all_to_all(x, 'scen', 0, 0, tiled=False)  29.4 us
    ppermute x14, waiting for transfers between devices, on_device(): lax.ppermute(x, 'scen', way)  26 us
    pallas_call x9, Pallas kernels, cost_share(): pl.pallas_call(functools.partial(cost_kernel, tile=min(256, rows // 2), p...  23.9 us
    ppermute x24, starting transfers between devices, swap(): return lax.ppermute(x, 'rep', [(i, i ^ bit) for i in range(n_rep)])  15.9 us
    ppermute x14, starting transfers between devices, on_device(): lax.ppermute(x, 'scen', way)  15.7 us
    ppermute x24, waiting for transfers between devices, swap(): return lax.ppermute(x, 'rep', [(i, i ^ bit) for i in range(n_rep)])  9.19 us
    pallas_call x1, Pallas kernels, norms(): pl.pallas_call(norm_kernel, out_shape=pltpu.VMEM((scenarios.shape[0], LAN...  4.51 us
    pallas_call x1, Pallas kernels, pick(): pl.pallas_call(functools.partial(pick_kernel, step=step), out_shape=(pltp...  4.09 us
  transfers between devices with their start and end apart: 38, of which 16 were waited for; matrix products, arithmetic and copies ran while one was open for 1% of the time, Pallas kernels for 21%

profile of v4, /device:TPU:0, one launch (start us, length us, event | category | flops | bytes accessed | tf_op | source)
XLA Modules:
  0.0 138.9 jit_solution(17000372456695394800)
XLA Ops:
  0.6 4.1 %pick.1 = (bf16[1024,4096]{1,0:T(8,128)(2,1)S(1)}, bf16[64,4096]{1,0:T(8,128)(2,1)S(1)}, bf16[64,4096]{1,0:T(8,128)(2,1)S(1)}) custom-call(s32[8,128]{1,0:T(8,128)} %bitcast.6, bf16[1024,4096]{1,0:T(8,128)(2,1)} %scen_ref.1), custom_call_target="tpu_custom_call" | custom-call | flops 4000000000 | bytes 10000000 | tf_op jit(solution)/shard_map/pick/pallas_call | solution.py:85
  4.7 3.1 %collective-permute-start.2 = (bf16[64,4096]{1,0:T(8,128)(2,1)S(1)}, bf16[64,4096]{1,0:T(8,128)(2,1)S(1)}, u32[]{:S(2)}, u32[]{:S(2)}) collective-permute-start(bf16[64,4096]{1,0:T(8,128)(2,1)S(1)} %get-tuple-element.69.refs_0_), channel_id=1, source_target_pairs={{0,8},{8,16},{16,24},{24,28},{28,20},{20,12},{12,4},{4,0},{1,9},{9... | collective-permute-start | bytes 1572872 | tf_op jit(solution)/shard_map/ppermute | solution.py:439
  7.8 4.5 %norms.1.sq_ref = f32[1024,128]{1,0:T(8,128)S(1)} custom-call(bf16[1024,4096]{1,0:T(8,128)(2,1)S(1)} %get-tuple-element.58.scen_ref), custom_call_target="tpu_custom_call" | custom-call | flops 4000000000 | bytes 10000000 | tf_op jit(solution)/shard_map/norms/pallas_call | solution.py:113
  12.4 2.9 %cost_share.9 = (f32[512,128]{1,0:T(8,128)S(1)}, f32[512,128]{1,0:T(8,128)S(1)}) custom-call(s32[3]{0:T(128)S(1)} %pad_add_fusion.core_ref.ids_ref, bf16[1024,4096]{1,0:T(8,128)(2,1)S(1)} %get-tuple-element.58.scen_ref, f32[1024,128]{1,0:T(8,128)S(1)} %norms.1.sq_ref, bf16[64,4096]{1,0:T(8,128)(2,1)S(1)} %get-tuple-element.69.refs_0_, ...), custom_call_target="tpu_custom_call" | custom-call | flops 4000000000 | bytes 10000000 | tf_op jit(solution)/shard_map/cost_share/pallas_call | solution.py:140
  15.4 2.1 %collective-permute-start.6 = (bf16[64,4096]{1,0:T(8,128)(2,1)S(1)}, bf16[64,4096]{1,0:T(8,128)(2,1)S(1)}, u32[]{:S(2)}, u32[]{:S(2)}) collective-permute-start(bf16[64,4096]{1,0:T(8,128)(2,1)S(1)} %get-tuple-element.68.refs_1_), channel_id=1, source_target_pairs={{0,8},{8,16},{16,24},{24,28},{28,20},{20,12},{12,4},{4,0},{1,9},{9... | collective-permute-start | bytes 1572872 | tf_op jit(solution)/shard_map/ppermute | solution.py:439
  18.0 2.1 %collective-permute-start.1 = (f32[512,128]{1,0:T(8,128)S(1)}, f32[512,128]{1,0:T(8,128)S(1)}, u32[]{:S(2)}, u32[]{:S(2)}) collective-permute-start(f32[512,128]{1,0:T(8,128)S(1)} %add.123), channel_id=1, source_target_pairs={{0,2},{1,3},{2,0},{3,1},{4,6},{5,7},{6,4},{7,5},{8,10},{9,11},{10,... | collective-permute-start | bytes 786440 | tf_op jit(solution)/shard_map/ppermute | solution.py:387
  20.5 1.6 %collective-permute-done.3.refs_1_ = bf16[64,4096]{1,0:T(8,128)(2,1)S(1)} collective-permute-done((bf16[64,4096]{1,0:T(8,128)(2,1)S(1)}, bf16[64,4096]{1,0:T(8,128)(2,1)S(1)}, u32[]{:S(2)}, u32[]{:S(2)}) %collective-permute-start.3) | collective-permute-done | bytes 524320 | tf_op jit(solution)/shard_map/ppermute | solution.py:439
  22.1 1.6 %collective-permute-start.10 = (bf16[64,4096]{1,0:T(8,128)(2,1)S(1)}, bf16[64,4096]{1,0:T(8,128)(2,1)S(1)}, u32[]{:S(2)}, u32[]{:S(2)}) collective-permute-start(bf16[64,4096]{1,0:T(8,128)(2,1)S(1)} %collective-permute-done.2.refs_0_), channel_id=1, source_target_pairs={{0,8},{8,16},{16,24},{24,28},{28,20},{20,12},{12,4},{4,0},{1,9},{9... | collective-permute-start | bytes 1572872 | tf_op jit(solution)/shard_map/ppermute | solution.py:439
  24.1 2.9 %cost_share.10 = (f32[512,128]{1,0:T(8,128)S(1)}, f32[512,128]{1,0:T(8,128)S(1)}) custom-call(s32[3]{0:T(128)S(1)} %pad_add_fusion.core_ref.ids_ref, bf16[1024,4096]{1,0:T(8,128)(2,1)S(1)} %get-tuple-element.58.scen_ref, f32[1024,128]{1,0:T(8,128)S(1)} %norms.1.sq_ref, bf16[64,4096]{1,0:T(8,128)(2,1)S(1)} %collective-permute-done.2.refs_0_, ...), custom_call_target="tpu_custom_call" | custom-call | flops 4000000000 | bytes 10000000 | tf_op jit(solution)/shard_map/cost_share/pallas_call | solution.py:140
  27.0 4.7 %collective-permute-done.6.refs_1_ = bf16[64,4096]{1,0:T(8,128)(2,1)S(1)} collective-permute-done((bf16[64,4096]{1,0:T(8,128)(2,1)S(1)}, bf16[64,4096]{1,0:T(8,128)(2,1)S(1)}, u32[]{:S(2)}, u32[]{:S(2)}) %collective-permute-start.6) | collective-permute-done | bytes 524320 | tf_op jit(solution)/shard_map/ppermute | solution.py:439
  31.7 1.6 %collective-permute-done.7.refs_0_ = bf16[64,4096]{1,0:T(8,128)(2,1)S(1)} collective-permute-done((bf16[64,4096]{1,0:T(8,128)(2,1)S(1)}, bf16[64,4096]{1,0:T(8,128)(2,1)S(1)}, u32[]{:S(2)}, u32[]{:S(2)}) %collective-permute-start.7) | collective-permute-done | bytes 524320 | tf_op jit(solution)/shard_map/ppermute | solution.py:439
  33.3 2.9 %cost_share.11 = (f32[512,128]{1,0:T(8,128)S(1)}, f32[512,128]{1,0:T(8,128)S(1)}) custom-call(s32[3]{0:T(128)S(1)} %pad_add_fusion.core_ref.ids_ref, bf16[1024,4096]{1,0:T(8,128)(2,1)S(1)} %get-tuple-element.58.scen_ref, f32[1024,128]{1,0:T(8,128)S(1)} %norms.1.sq_ref, bf16[64,4096]{1,0:T(8,128)(2,1)S(1)} %collective-permute-done.7.refs_0_, ...), custom_call_target="tpu_custom_call" | custom-call | flops 4000000000 | bytes 10000000 | tf_op jit(solution)/shard_map/cost_share/pallas_call | solution.py:140
  36.3 1.6 %collective-permute-start.5 = (f32[512,128]{1,0:T(8,128)S(1)}, f32[512,128]{1,0:T(8,128)S(1)}, u32[]{:S(2)}, u32[]{:S(2)}) collective-permute-start(f32[512,128]{1,0:T(8,128)S(1)} %add.135), channel_id=1, source_target_pairs={{0,2},{1,3},{2,0},{3,1},{4,6},{5,7},{6,4},{7,5},{8,10},{9,11},{10,... | collective-permute-start | bytes 786440 | tf_op jit(solution)/shard_map/ppermute | solution.py:387
  38.0 1.6 %collective-permute-start.14 = (bf16[64,4096]{1,0:T(8,128)(2,1)S(1)}, bf16[64,4096]{1,0:T(8,128)(2,1)S(1)}, u32[]{:S(2)}, u32[]{:S(2)}) collective-permute-start(bf16[64,4096]{1,0:T(8,128)(2,1)S(1)} %collective-permute-done.6.refs_1_), channel_id=1, source_target_pairs={{0,8},{8,16},{16,24},{24,28},{28,20},{20,12},{12,4},{4,0},{1,9},{9... | collective-permute-start | bytes 1572872 | tf_op jit(solution)/shard_map/ppermute | solution.py:439
  40.1 2.9 %collective-permute-done.10.refs_0_ = bf16[64,4096]{1,0:T(8,128)(2,1)S(1)} collective-permute-done((bf16[64,4096]{1,0:T(8,128)(2,1)S(1)}, bf16[64,4096]{1,0:T(8,128)(2,1)S(1)}, u32[]{:S(2)}, u32[]{:S(2)}) %collective-permute-start.10) | collective-permute-done | bytes 524320 | tf_op jit(solution)/shard_map/ppermute | solution.py:439
  42.9 1.6 %collective-permute-done.11.refs_1_ = bf16[64,4096]{1,0:T(8,128)(2,1)S(1)} collective-permute-done((bf16[64,4096]{1,0:T(8,128)(2,1)S(1)}, bf16[64,4096]{1,0:T(8,128)(2,1)S(1)}, u32[]{:S(2)}, u32[]{:S(2)}) %collective-permute-start.11) | collective-permute-done | bytes 524320 | tf_op jit(solution)/shard_map/ppermute | solution.py:439
  44.6 1.5 %collective-permute-start.9 = (f32[512,128]{1,0:T(8,128)S(1)}, f32[512,128]{1,0:T(8,128)S(1)}, u32[]{:S(2)}, u32[]{:S(2)}) collective-permute-start(f32[512,128]{1,0:T(8,128)S(1)} %add.137), channel_id=1, source_target_pairs={{0,2},{1,3},{2,0},{3,1},{4,6},{5,7},{6,4},{7,5},{8,10},{9,11},{10,... | collective-permute-start | bytes 786440 | tf_op jit(solution)/shard_map/ppermute | solution.py:387
  46.1 1.6 %collective-permute-start.23 = (bf16[64,4096]{1,0:T(8,128)(2,1)S(1)}, bf16[64,4096]{1,0:T(8,128)(2,1)S(1)}, u32[]{:S(2)}, u32[]{:S(2)}) collective-permute-start(bf16[64,4096]{1,0:T(8,128)(2,1)S(1)} %collective-permute-done.10.refs_0_), channel_id=1, source_target_pairs={{0,8},{8,16},{16,24},{24,28},{28,20},{20,12},{12,4},{4,0},{1,9},{9... | collective-permute-start | bytes 1572872 | tf_op jit(solution)/shard_map/ppermute | solution.py:439
  47.7 2.9 %cost_share.12 = (f32[512,128]{1,0:T(8,128)S(1)}, f32[512,128]{1,0:T(8,128)S(1)}) custom-call(s32[3]{0:T(128)S(1)} %pad_add_fusion.core_ref.ids_ref, bf16[1024,4096]{1,0:T(8,128)(2,1)S(1)} %get-tuple-element.58.scen_ref, f32[1024,128]{1,0:T(8,128)S(1)} %norms.1.sq_ref, bf16[64,4096]{1,0:T(8,128)(2,1)S(1)} %collective-permute-done.10.refs_0_, ...), custom_call_target="tpu_custom_call" | custom-call | flops 4000000000 | bytes 10000000 | tf_op jit(solution)/shard_map/cost_share/pallas_call | solution.py:140
  51.3 2.9 %collective-permute-done.14.refs_1_ = bf16[64,4096]{1,0:T(8,128)(2,1)S(1)} collective-permute-done((bf16[64,4096]{1,0:T(8,128)(2,1)S(1)}, bf16[64,4096]{1,0:T(8,128)(2,1)S(1)}, u32[]{:S(2)}, u32[]{:S(2)}) %collective-permute-start.14) | collective-permute-done | bytes 524320 | tf_op jit(solution)/shard_map/ppermute | solution.py:439
  54.2 1.6 %collective-permute-done.15.refs_0_ = bf16[64,4096]{1,0:T(8,128)(2,1)S(1)} collective-permute-done((bf16[64,4096]{1,0:T(8,128)(2,1)S(1)}, bf16[64,4096]{1,0:T(8,128)(2,1)S(1)}, u32[]{:S(2)}, u32[]{:S(2)}) %collective-permute-start.15) | collective-permute-done | bytes 524320 | tf_op jit(solution)/shard_map/ppermute | solution.py:439
  55.8 2.9 %cost_share.13 = (f32[512,128]{1,0:T(8,128)S(1)}, f32[512,128]{1,0:T(8,128)S(1)}) custom-call(s32[3]{0:T(128)S(1)} %pad_add_fusion.core_ref.ids_ref, bf16[1024,4096]{1,0:T(8,128)(2,1)S(1)} %get-tuple-element.58.scen_ref, f32[1024,128]{1,0:T(8,128)S(1)} %norms.1.sq_ref, bf16[64,4096]{1,0:T(8,128)(2,1)S(1)} %collective-permute-done.15.refs_0_, ...), custom_call_target="tpu_custom_call" | custom-call | flops 4000000000 | bytes 10000000 | tf_op jit(solution)/shard_map/cost_share/pallas_call | solution.py:140
  59.3 1.7 %collective-permute-start.27 = (bf16[64,4096]{1,0:T(8,128)(2,1)S(1)}, bf16[64,4096]{1,0:T(8,128)(2,1)S(1)}, u32[]{:S(2)}, u32[]{:S(2)}) collective-permute-start(bf16[64,4096]{1,0:T(8,128)(2,1)S(1)} %collective-permute-done.14.refs_1_), channel_id=1, source_target_pairs={{0,8},{8,16},{16,24},{24,28},{28,20},{20,12},{12,4},{4,0},{1,9},{9... | collective-permute-start | bytes 1572872 | tf_op jit(solution)/shard_map/ppermute | solution.py:439
  61.5 1.6 %collective-permute-start.18 = (f32[512,128]{1,0:T(8,128)S(1)}, f32[512,128]{1,0:T(8,128)S(1)}, u32[]{:S(2)}, u32[]{:S(2)}) collective-permute-start(f32[512,128]{1,0:T(8,128)S(1)} %add.141), channel_id=1, source_target_pairs={{0,2},{1,3},{2,0},{3,1},{4,6},{5,7},{6,4},{7,5},{8,10},{9,11},{10,... | collective-permute-start | bytes 786440 | tf_op jit(solution)/shard_map/ppermute | solution.py:387
  63.1 2.3 %collective-permute-done.23.refs_0_ = bf16[64,4096]{1,0:T(8,128)(2,1)S(1)} collective-permute-done((bf16[64,4096]{1,0:T(8,128)(2,1)S(1)}, bf16[64,4096]{1,0:T(8,128)(2,1)S(1)}, u32[]{:S(2)}, u32[]{:S(2)}) %collective-permute-start.23) | collective-permute-done | bytes 524320 | tf_op jit(solution)/shard_map/ppermute | solution.py:439
  65.4 1.6 %collective-permute-done.24.refs_1_ = bf16[64,4096]{1,0:T(8,128)(2,1)S(1)} collective-permute-done((bf16[64,4096]{1,0:T(8,128)(2,1)S(1)}, bf16[64,4096]{1,0:T(8,128)(2,1)S(1)}, u32[]{:S(2)}, u32[]{:S(2)}) %collective-permute-start.24) | collective-permute-done | bytes 524320 | tf_op jit(solution)/shard_map/ppermute | solution.py:439
  67.0 2.9 %cost_share.14 = (f32[512,128]{1,0:T(8,128)S(1)}, f32[512,128]{1,0:T(8,128)S(1)}) custom-call(s32[3]{0:T(128)S(1)} %pad_add_fusion.core_ref.ids_ref, bf16[1024,4096]{1,0:T(8,128)(2,1)S(1)} %get-tuple-element.58.scen_ref, f32[1024,128]{1,0:T(8,128)S(1)} %norms.1.sq_ref, bf16[64,4096]{1,0:T(8,128)(2,1)S(1)} %collective-permute-done.23.refs_0_, ...), custom_call_target="tpu_custom_call" | custom-call | flops 4000000000 | bytes 10000000 | tf_op jit(solution)/shard_map/cost_share/pallas_call | solution.py:140
  70.5 1.5 %collective-permute-start.13 = (f32[512,128]{1,0:T(8,128)S(1)}, f32[512,128]{1,0:T(8,128)S(1)}, u32[]{:S(2)}, u32[]{:S(2)}) collective-permute-start(f32[512,128]{1,0:T(8,128)S(1)} %add.139), channel_id=1, source_target_pairs={{0,2},{1,3},{2,0},{3,1},{4,6},{5,7},{6,4},{7,5},{8,10},{9,11},{10,... | collective-permute-start | bytes 786440 | tf_op jit(solution)/shard_map/ppermute | solution.py:387
  72.1 1.6 %collective-permute-start.31 = (bf16[64,4096]{1,0:T(8,128)(2,1)S(1)}, bf16[64,4096]{1,0:T(8,128)(2,1)S(1)}, u32[]{:S(2)}, u32[]{:S(2)}) collective-permute-start(bf16[64,4096]{1,0:T(8,128)(2,1)S(1)} %collective-permute-done.23.refs_0_), channel_id=1, source_target_pairs={{0,8},{8,16},{16,24},{24,28},{28,20},{20,12},{12,4},{4,0},{1,9},{9... | collective-permute-start | bytes 1572872 | tf_op jit(solution)/shard_map/ppermute | solution.py:439
  74.3 2.4 %collective-permute-done.27.refs_1_ = bf16[64,4096]{1,0:T(8,128)(2,1)S(1)} collective-permute-done((bf16[64,4096]{1,0:T(8,128)(2,1)S(1)}, bf16[64,4096]{1,0:T(8,128)(2,1)S(1)}, u32[]{:S(2)}, u32[]{:S(2)}) %collective-permute-start.27) | collective-permute-done | bytes 524320 | tf_op jit(solution)/shard_map/ppermute | solution.py:439
  76.7 1.8 %collective-permute-start.26 = (f32[512,128]{1,0:T(8,128)S(1)}, f32[512,128]{1,0:T(8,128)S(1)}, u32[]{:S(2)}, u32[]{:S(2)}) collective-permute-start(f32[512,128]{1,0:T(8,128)S(1)} %add.143), channel_id=1, source_target_pairs={{0,2},{1,3},{2,0},{3,1},{4,6},{5,7},{6,4},{7,5},{8,10},{9,11},{10,... | collective-permute-start | bytes 786440 | tf_op jit(solution)/shard_map/ppermute | solution.py:387
  78.5 2.9 %cost_share.15 = (f32[512,128]{1,0:T(8,128)S(1)}, f32[512,128]{1,0:T(8,128)S(1)}) custom-call(s32[3]{0:T(128)S(1)} %pad_add_fusion.core_ref.ids_ref, bf16[1024,4096]{1,0:T(8,128)(2,1)S(1)} %get-tuple-element.58.scen_ref, f32[1024,128]{1,0:T(8,128)S(1)} %norms.1.sq_ref, bf16[64,4096]{1,0:T(8,128)(2,1)S(1)} %collective-permute-done.28.refs_0_, ...), custom_call_target="tpu_custom_call" | custom-call | flops 4000000000 | bytes 10000000 | tf_op jit(solution)/shard_map/cost_share/pallas_call | solution.py:140
  82.0 2.4 %collective-permute-done.26 = f32[512,128]{1,0:T(8,128)S(1)} collective-permute-done((f32[512,128]{1,0:T(8,128)S(1)}, f32[512,128]{1,0:T(8,128)S(1)}, u32[]{:S(2)}, u32[]{:S(2)}) %collective-permute-start.26) | collective-permute-done | bytes 262176 | tf_op jit(solution)/shard_map/ppermute | solution.py:387
  84.5 1.6 %collective-permute-start.30 = (f32[512,128]{1,0:T(8,128)S(1)}, f32[512,128]{1,0:T(8,128)S(1)}, u32[]{:S(2)}, u32[]{:S(2)}) collective-permute-start(f32[512,128]{1,0:T(8,128)S(1)} %add.145), channel_id=1, source_target_pairs={{0,2},{1,3},{2,0},{3,1},{4,6},{5,7},{6,4},{7,5},{8,10},{9,11},{10,... | collective-permute-start | bytes 786440 | tf_op jit(solution)/shard_map/ppermute | solution.py:387
  87.1 1.5 %collective-permute-done.32.refs_1_ = bf16[64,4096]{1,0:T(8,128)(2,1)S(1)} collective-permute-done((bf16[64,4096]{1,0:T(8,128)(2,1)S(1)}, bf16[64,4096]{1,0:T(8,128)(2,1)S(1)}, u32[]{:S(2)}, u32[]{:S(2)}) %collective-permute-start.32) | collective-permute-done | bytes 524320 | tf_op jit(solution)/shard_map/ppermute | solution.py:439
  88.6 1.8 %cost_share.16 = f32[512,128]{1,0:T(8,128)S(1)} custom-call(s32[3]{0:T(128)S(1)} %pad_add_fusion.core_ref.ids_ref, bf16[1024,4096]{1,0:T(8,128)(2,1)S(1)} %get-tuple-element.58.scen_ref, f32[1024,128]{1,0:T(8,128)S(1)} %norms.1.sq_ref, bf16[64,4096]{1,0:T(8,128)(2,1)S(1)} %collective-permute-done.31.refs_0_, bf16[64,4096]{1,0:T(8,128)(2,1)S(1)} %collective-permute-done.32.refs_1_), custom_call_target="tpu_custom_call" | custom-call | flops 4000000000 | bytes 10000000 | tf_op jit(solution)/shard_map/cost_share/pallas_call | solution.py:140
  90.5 1.8 %cost_share.17 = f32[512,128]{1,0:T(8,128)S(1)} custom-call(s32[3]{0:T(128)S(1)} %pad_add_fusion.core_ref.ids_ref, bf16[1024,4096]{1,0:T(8,128)(2,1)S(1)} %get-tuple-element.58.scen_ref, f32[1024,128]{1,0:T(8,128)S(1)} %norms.1.sq_ref, bf16[64,4096]{1,0:T(8,128)(2,1)S(1)} %collective-permute-done.31.refs_0_, bf16[64,4096]{1,0:T(8,128)(2,1)S(1)} %collective-permute-done.32.refs_1_), custom_call_target="tpu_custom_call" | custom-call | flops 4000000000 | bytes 10000000 | tf_op jit(solution)/shard_map/cost_share/pallas_call | solution.py:140
  92.4 1.6 %collective-permute-start.34 = (f32[512,128]{1,0:T(8,128)S(1)}, f32[512,128]{1,0:T(8,128)S(1)}, u32[]{:S(2)}, u32[]{:S(2)}) collective-permute-start(f32[512,128]{1,0:T(8,128)S(1)} %add.147), channel_id=1, source_target_pairs={{0,2},{1,3},{2,0},{3,1},{4,6},{5,7},{6,4},{7,5},{8,10},{9,11},{10,... | collective-permute-start | bytes 786440 | tf_op jit(solution)/shard_map/ppermute | solution.py:387
  93.9 1.3 early.1
  95.9 5.2 %collective-permute-done.34 = f32[512,128]{1,0:T(8,128)S(1)} collective-permute-done((f32[512,128]{1,0:T(8,128)S(1)}, f32[512,128]{1,0:T(8,128)S(1)}, u32[]{:S(2)}, u32[]{:S(2)}) %collective-permute-start.34) | collective-permute-done | bytes 262176 | tf_op jit(solution)/shard_map/ppermute | solution.py:387
  101.3 1.5 %collective-permute-done.37.refs_5_ = f32[512,128]{1,0:T(8,128)S(1)} collective-permute-done((f32[512,128]{1,0:T(8,128)S(1)}, f32[512,128]{1,0:T(8,128)S(1)}, u32[]{:S(2)}, u32[]{:S(2)}) %collective-permute-start.37) | collective-permute-done | bytes 262176 | tf_op jit(solution)/shard_map/ppermute | solution.py:387
  102.8 1.5 %late.1 = (f32[1024,1024]{1,0:T(8,128)S(1)}, f32[1024,128]{1,0:T(8,128)S(1)}, f32[8,8,128]{2,1,0:T(8,128)S(1)}) custom-call(s32[3]{0:T(128)S(1)} %pad_add_fusion.core_ref.ids_ref, f32[1024,640]{1,0:T(8,128)S(1)} %get-tuple-element.82.early_ref, f32[1024,128]{1,0:T(8,128)S(1)} %get-tuple-element.83.old_peak_ref, ...), custom_call_target="tpu_custom_call" | custom-call | tf_op jit(solution)/shard_map/late/pallas_call | solution.py:500
  104.2 11.3 %all_to_all.15.got_ref = f32[8,8,128]{2,1,0:T(8,128)S(1)} all-to-all(f32[8,8,128]{2,1,0:T(8,128)S(1)} %get-tuple-element.97), channel_id=1, replica_groups=mesh['scen'=8,'rep'=4] {'scen'}, dimensions={0} | all-to-all | bytes 65536 | tf_op jit(solution)/shard_map/all_to_all | solution.py:495
  115.5 1.1 step.1
  116.6 9.1 %all_to_all.16.got_ref = f32[8,8,128]{2,1,0:T(8,128)S(1)} all-to-all(f32[8,8,128]{2,1,0:T(8,128)S(1)} %step.1), channel_id=1, replica_groups=mesh['scen'=8,'rep'=4] {'scen'}, dimensions={0} | all-to-all | bytes 65536 | tf_op jit(solution)/shard_map/all_to_all | solution.py:495
  125.7 1.9 %last.1 = (f32[8,8,128]{2,1,0:T(8,128)S(1)}, f32[8,128]{1,0:T(8,128)}, f32[1024,1024]{1,0:T(8,128)S(1)}) custom-call(s32[3]{0:T(128)S(1)} %pad_add_fusion.core_ref.ids_ref, f32[8,8,128]{2,1,0:T(8,128)S(1)} %all_to_all.16.got_ref, f32[1024,1024]{1,0:T(8,128)S(1)} %get-tuple-element.98.e_ref, f32[1024,128]{1,0:T(8,128)S(1)} %get-tuple-element.99.peak_ref), custom_call_target="tpu_custom_call" | custom-call | tf_op jit(solution)/shard_map/last/pallas_call | solution.py:518
  127.6 9.0 %all_to_all.17.got_ref = f32[8,8,128]{2,1,0:T(8,128)S(1)} all-to-all(f32[8,8,128]{2,1,0:T(8,128)S(1)} %get-tuple-element.101), channel_id=1, replica_groups=mesh['scen'=8,'rep'=4] {'scen'}, dimensions={0} | all-to-all | bytes 65536 | tf_op jit(solution)/shard_map/all_to_all | solution.py:495
  136.6 2.2 %out.1 = (f32[1,256]{1,0:T(1,128)}, bf16[256,1024]{1,0:T(8,128)(2,1)}) custom-call(s32[3]{0:T(128)S(1)} %pad_add_fusion.core_ref.ids_ref, f32[8,8,128]{2,1,0:T(8,128)S(1)} %all_to_all.17.got_ref, f32[1024,1024]{1,0:T(8,128)S(1)} %get-tuple-element.102.scaled_ref, bf16[256,1024]{1,0:T(8,128)(2,1)S(1)} %fusion.perm_ref), custom_call_target="tpu_custom_call" | custom-call | tf_op jit(solution)/shard_map/out/pallas_call | solution.py:531
  (70 shorter events, 7.7 us)
Async XLA Ops:
  4.7 15.7 %collective-permute-start.2 = (bf16[64,4096]{1,0:T(8,128)(2,1)S(1)}, bf16[64,4096]{1,0:T(8,128)(2,1)S(1)}, u32[]{:S(2)}, u32[]{:S(2)}) collective-permute-start(bf16[64,4096]{1,0:T(8,128)(2,1)S(1)} %get-tuple-element.69.refs_0_), channel_id=1, source_target_pairs={{0,8},{8,16},{16,24},{24,28},{28,20},{20,12},{12,4},{4,0},{1,9},{9... | collective-permute-start | bytes 1572872 | tf_op jit(solution)/shard_map/ppermute | solution.py:439
  7.8 14.3 %collective-permute-start.3 = (bf16[64,4096]{1,0:T(8,128)(2,1)S(1)}, bf16[64,4096]{1,0:T(8,128)(2,1)S(1)}, u32[]{:S(2)}, u32[]{:S(2)}) collective-permute-start(bf16[64,4096]{1,0:T(8,128)(2,1)S(1)} %get-tuple-element.68.refs_1_), channel_id=1, source_target_pairs={{8,0},{16,8},{24,16},{28,24},{20,28},{12,20},{4,12},{0,4},{9,1},{1... | collective-permute-start | bytes 1572872 | tf_op jit(solution)/shard_map/ppermute | solution.py:439
  12.4 5.1 %copy-start = (s32[1024]{0:T(1024)S(1)}, s32[1024]{0:T(1024)}, u32[]{:S(2)}) copy-start(s32[1024]{0:T(1024)} %param.3) | copy-start | bytes 12292
  15.3 2.7 %collective-permute-start = (f32[512,128]{1,0:T(8,128)S(1)}, f32[512,128]{1,0:T(8,128)S(1)}, u32[]{:S(2)}, u32[]{:S(2)}) collective-permute-start(f32[512,128]{1,0:T(8,128)S(1)} %get-tuple-element.62), channel_id=1, source_target_pairs={{0,1},{1,0},{2,3},{3,2},{4,5},{5,4},{6,7},{7,6},{8,9},{9,8},{10,11... | collective-permute-start | bytes 786440 | tf_op jit(solution)/shard_map/ppermute | solution.py:387
  15.4 16.3 %collective-permute-start.6 = (bf16[64,4096]{1,0:T(8,128)(2,1)S(1)}, bf16[64,4096]{1,0:T(8,128)(2,1)S(1)}, u32[]{:S(2)}, u32[]{:S(2)}) collective-permute-start(bf16[64,4096]{1,0:T(8,128)(2,1)S(1)} %get-tuple-element.68.refs_1_), channel_id=1, source_target_pairs={{0,8},{8,16},{16,24},{24,28},{28,20},{20,12},{12,4},{4,0},{1,9},{9... | collective-permute-start | bytes 1572872 | tf_op jit(solution)/shard_map/ppermute | solution.py:439
  17.5 15.9 %collective-permute-start.7 = (bf16[64,4096]{1,0:T(8,128)(2,1)S(1)}, bf16[64,4096]{1,0:T(8,128)(2,1)S(1)}, u32[]{:S(2)}, u32[]{:S(2)}) collective-permute-start(bf16[64,4096]{1,0:T(8,128)(2,1)S(1)} %get-tuple-element.69.refs_0_), channel_id=1, source_target_pairs={{8,0},{16,8},{24,16},{28,24},{20,28},{12,20},{4,12},{0,4},{9,1},{1... | collective-permute-start | bytes 1572872 | tf_op jit(solution)/shard_map/ppermute | solution.py:439
  18.0 19.9 %collective-permute-start.1 = (f32[512,128]{1,0:T(8,128)S(1)}, f32[512,128]{1,0:T(8,128)S(1)}, u32[]{:S(2)}, u32[]{:S(2)}) collective-permute-start(f32[512,128]{1,0:T(8,128)S(1)} %add.123), channel_id=1, source_target_pairs={{0,2},{1,3},{2,0},{3,1},{4,6},{5,7},{6,4},{7,5},{8,10},{9,11},{10,... | collective-permute-start | bytes 786440 | tf_op jit(solution)/shard_map/ppermute | solution.py:387
  22.1 20.9 %collective-permute-start.10 = (bf16[64,4096]{1,0:T(8,128)(2,1)S(1)}, bf16[64,4096]{1,0:T(8,128)(2,1)S(1)}, u32[]{:S(2)}, u32[]{:S(2)}) collective-permute-start(bf16[64,4096]{1,0:T(8,128)(2,1)S(1)} %collective-permute-done.2.refs_0_), channel_id=1, source_target_pairs={{0,8},{8,16},{16,24},{24,28},{28,20},{20,12},{12,4},{4,0},{1,9},{9... | collective-permute-start | bytes 1572872 | tf_op jit(solution)/shard_map/ppermute | solution.py:439
  23.7 20.9 %collective-permute-start.11 = (bf16[64,4096]{1,0:T(8,128)(2,1)S(1)}, bf16[64,4096]{1,0:T(8,128)(2,1)S(1)}, u32[]{:S(2)}, u32[]{:S(2)}) collective-permute-start(bf16[64,4096]{1,0:T(8,128)(2,1)S(1)} %collective-permute-done.3.refs_1_), channel_id=1, source_target_pairs={{8,0},{16,8},{24,16},{28,24},{20,28},{12,20},{4,12},{0,4},{9,1},{1... | collective-permute-start | bytes 1572872 | tf_op jit(solution)/shard_map/ppermute | solution.py:439
  31.7 4.6 %collective-permute-start.4 = (f32[512,128]{1,0:T(8,128)S(1)}, f32[512,128]{1,0:T(8,128)S(1)}, u32[]{:S(2)}, u32[]{:S(2)}) collective-permute-start(f32[512,128]{1,0:T(8,128)S(1)} %get-tuple-element.67), channel_id=1, source_target_pairs={{0,1},{1,0},{2,3},{3,2},{4,5},{5,4},{6,7},{7,6},{8,9},{9,8},{10,11... | collective-permute-start | bytes 786440 | tf_op jit(solution)/shard_map/ppermute | solution.py:387
  36.2 3.3 %collective-permute-start.8 = (f32[512,128]{1,0:T(8,128)S(1)}, f32[512,128]{1,0:T(8,128)S(1)}, u32[]{:S(2)}, u32[]{:S(2)}) collective-permute-start(f32[512,128]{1,0:T(8,128)S(1)} %get-tuple-element.73), channel_id=1, source_target_pairs={{0,1},{1,0},{2,3},{3,2},{4,5},{5,4},{6,7},{7,6},{8,9},{9,8},{10,11... | collective-permute-start | bytes 786440 | tf_op jit(solution)/shard_map/ppermute | solution.py:387
  36.3 9.8 %collective-permute-start.5 = (f32[512,128]{1,0:T(8,128)S(1)}, f32[512,128]{1,0:T(8,128)S(1)}, u32[]{:S(2)}, u32[]{:S(2)}) collective-permute-start(f32[512,128]{1,0:T(8,128)S(1)} %add.135), channel_id=1, source_target_pairs={{0,2},{1,3},{2,0},{3,1},{4,6},{5,7},{6,4},{7,5},{8,10},{9,11},{10,... | collective-permute-start | bytes 786440 | tf_op jit(solution)/shard_map/ppermute | solution.py:387
  38.0 16.2 %collective-permute-start.14 = (bf16[64,4096]{1,0:T(8,128)(2,1)S(1)}, bf16[64,4096]{1,0:T(8,128)(2,1)S(1)}, u32[]{:S(2)}, u32[]{:S(2)}) collective-permute-start(bf16[64,4096]{1,0:T(8,128)(2,1)S(1)} %collective-permute-done.6.refs_1_), channel_id=1, source_target_pairs={{0,8},{8,16},{16,24},{24,28},{28,20},{20,12},{12,4},{4,0},{1,9},{9... | collective-permute-start | bytes 1572872 | tf_op jit(solution)/shard_map/ppermute | solution.py:439
  39.5 16.3 %collective-permute-start.15 = (bf16[64,4096]{1,0:T(8,128)(2,1)S(1)}, bf16[64,4096]{1,0:T(8,128)(2,1)S(1)}, u32[]{:S(2)}, u32[]{:S(2)}) collective-permute-start(bf16[64,4096]{1,0:T(8,128)(2,1)S(1)} %collective-permute-done.7.refs_0_), channel_id=1, source_target_pairs={{8,0},{16,8},{24,16},{28,24},{20,28},{12,20},{4,12},{0,4},{9,1},{1... | collective-permute-start | bytes 1572872 | tf_op jit(solution)/shard_map/ppermute | solution.py:439
  42.9 7.6 %collective-permute-start.16 = (f32[512,128]{1,0:T(8,128)S(1)}, f32[512,128]{1,0:T(8,128)S(1)}, u32[]{:S(2)}, u32[]{:S(2)}) collective-permute-start(f32[512,128]{1,0:T(8,128)S(1)} %add.124.refs_0_), channel_id=1, source_target_pairs={{0,1},{1,0},{2,3},{3,2},{4,5},{5,4},{6,7},{7,6},{8,9},{9,8},{10,11... | collective-permute-start | bytes 786440 | tf_op jit(solution)/shard_map/ppermute | solution.py:387
  44.6 14.2 %collective-permute-start.9 = (f32[512,128]{1,0:T(8,128)S(1)}, f32[512,128]{1,0:T(8,128)S(1)}, u32[]{:S(2)}, u32[]{:S(2)}) collective-permute-start(f32[512,128]{1,0:T(8,128)S(1)} %add.137), channel_id=1, source_target_pairs={{0,2},{1,3},{2,0},{3,1},{4,6},{5,7},{6,4},{7,5},{8,10},{9,11},{10,... | collective-permute-start | bytes 786440 | tf_op jit(solution)/shard_map/ppermute | solution.py:387
  46.1 19.3 %collective-permute-start.23 = (bf16[64,4096]{1,0:T(8,128)(2,1)S(1)}, bf16[64,4096]{1,0:T(8,128)(2,1)S(1)}, u32[]{:S(2)}, u32[]{:S(2)}) collective-permute-start(bf16[64,4096]{1,0:T(8,128)(2,1)S(1)} %collective-permute-done.10.refs_0_), channel_id=1, source_target_pairs={{0,8},{8,16},{16,24},{24,28},{28,20},{20,12},{12,4},{4,0},{1,9},{9... | collective-permute-start | bytes 1572872 | tf_op jit(solution)/shard_map/ppermute | solution.py:439
  50.6 16.4 %collective-permute-start.24 = (bf16[64,4096]{1,0:T(8,128)(2,1)S(1)}, bf16[64,4096]{1,0:T(8,128)(2,1)S(1)}, u32[]{:S(2)}, u32[]{:S(2)}) collective-permute-start(bf16[64,4096]{1,0:T(8,128)(2,1)S(1)} %collective-permute-done.11.refs_1_), channel_id=1, source_target_pairs={{8,0},{16,8},{24,16},{28,24},{20,28},{12,20},{4,12},{0,4},{9,1},{1... | collective-permute-start | bytes 1572872 | tf_op jit(solution)/shard_map/ppermute | solution.py:439
  54.2 5.1 %collective-permute-start.12 = (f32[512,128]{1,0:T(8,128)S(1)}, f32[512,128]{1,0:T(8,128)S(1)}, u32[]{:S(2)}, u32[]{:S(2)}) collective-permute-start(f32[512,128]{1,0:T(8,128)S(1)} %get-tuple-element.77), channel_id=1, source_target_pairs={{0,1},{1,0},{2,3},{3,2},{4,5},{5,4},{6,7},{7,6},{8,9},{9,8},{10,11... | collective-permute-start | bytes 786440 | tf_op jit(solution)/shard_map/ppermute | solution.py:387
  58.7 2.3 %collective-permute-start.17 = (f32[512,128]{1,0:T(8,128)S(1)}, f32[512,128]{1,0:T(8,128)S(1)}, u32[]{:S(2)}, u32[]{:S(2)}) collective-permute-start(f32[512,128]{1,0:T(8,128)S(1)} %get-tuple-element.81), channel_id=1, source_target_pairs={{0,1},{1,0},{2,3},{3,2},{4,5},{5,4},{6,7},{7,6},{8,9},{9,8},{10,11... | collective-permute-start | bytes 786440 | tf_op jit(solution)/shard_map/ppermute | solution.py:387
  58.8 2.7 %collective-permute-start.19 = (f32[512,128]{1,0:T(8,128)S(1)}, f32[512,128]{1,0:T(8,128)S(1)}, u32[]{:S(2)}, u32[]{:S(2)}) collective-permute-start(f32[512,128]{1,0:T(8,128)S(1)} %add.136.refs_1_), channel_id=1, source_target_pairs={{0,1},{1,0},{2,3},{3,2},{4,5},{5,4},{6,7},{7,6},{8,9},{9,8},{10,11... | collective-permute-start | bytes 786440 | tf_op jit(solution)/shard_map/ppermute | solution.py:387
  59.3 17.3 %collective-permute-start.27 = (bf16[64,4096]{1,0:T(8,128)(2,1)S(1)}, bf16[64,4096]{1,0:T(8,128)(2,1)S(1)}, u32[]{:S(2)}, u32[]{:S(2)}) collective-permute-start(bf16[64,4096]{1,0:T(8,128)(2,1)S(1)} %collective-permute-done.14.refs_1_), channel_id=1, source_target_pairs={{0,8},{8,16},{16,24},{24,28},{28,20},{20,12},{12,4},{4,0},{1,9},{9... | collective-permute-start | bytes 1572872 | tf_op jit(solution)/shard_map/ppermute | solution.py:439
  61.0 17.5 %collective-permute-start.28 = (bf16[64,4096]{1,0:T(8,128)(2,1)S(1)}, bf16[64,4096]{1,0:T(8,128)(2,1)S(1)}, u32[]{:S(2)}, u32[]{:S(2)}) collective-permute-start(bf16[64,4096]{1,0:T(8,128)(2,1)S(1)} %collective-permute-done.15.refs_0_), channel_id=1, source_target_pairs={{8,0},{16,8},{24,16},{28,24},{20,28},{12,20},{4,12},{0,4},{9,1},{1... | collective-permute-start | bytes 1572872 | tf_op jit(solution)/shard_map/ppermute | solution.py:439
  61.5 9.0 %collective-permute-start.18 = (f32[512,128]{1,0:T(8,128)S(1)}, f32[512,128]{1,0:T(8,128)S(1)}, u32[]{:S(2)}, u32[]{:S(2)}) collective-permute-start(f32[512,128]{1,0:T(8,128)S(1)} %add.141), channel_id=1, source_target_pairs={{0,2},{1,3},{2,0},{3,1},{4,6},{5,7},{6,4},{7,5},{8,10},{9,11},{10,... | collective-permute-start | bytes 786440 | tf_op jit(solution)/shard_map/ppermute | solution.py:387
  70.0 2.1 %collective-permute-start.25 = (f32[512,128]{1,0:T(8,128)S(1)}, f32[512,128]{1,0:T(8,128)S(1)}, u32[]{:S(2)}, u32[]{:S(2)}) collective-permute-start(f32[512,128]{1,0:T(8,128)S(1)} %get-tuple-element.88), channel_id=1, source_target_pairs={{0,1},{1,0},{2,3},{3,2},{4,5},{5,4},{6,7},{7,6},{8,9},{9,8},{10,11... | collective-permute-start | bytes 786440 | tf_op jit(solution)/shard_map/ppermute | solution.py:387
  70.0 3.7 %collective-permute-start.20 = (f32[512,128]{1,0:T(8,128)S(1)}, f32[512,128]{1,0:T(8,128)S(1)}, u32[]{:S(2)}, u32[]{:S(2)}) collective-permute-start(f32[512,128]{1,0:T(8,128)S(1)} %add.138.refs_2_), channel_id=1, source_target_pairs={{0,1},{1,0},{2,3},{3,2},{4,5},{5,4},{6,7},{7,6},{8,9},{9,8},{10,11... | collective-permute-start | bytes 786440 | tf_op jit(solution)/shard_map/ppermute | solution.py:387
  70.5 10.9 %collective-permute-start.13 = (f32[512,128]{1,0:T(8,128)S(1)}, f32[512,128]{1,0:T(8,128)S(1)}, u32[]{:S(2)}, u32[]{:S(2)}) collective-permute-start(f32[512,128]{1,0:T(8,128)S(1)} %add.139), channel_id=1, source_target_pairs={{0,2},{1,3},{2,0},{3,1},{4,6},{5,7},{6,4},{7,5},{8,10},{9,11},{10,... | collective-permute-start | bytes 786440 | tf_op jit(solution)/shard_map/ppermute | solution.py:387
  72.1 15.0 %collective-permute-start.31 = (bf16[64,4096]{1,0:T(8,128)(2,1)S(1)}, bf16[64,4096]{1,0:T(8,128)(2,1)S(1)}, u32[]{:S(2)}, u32[]{:S(2)}) collective-permute-start(bf16[64,4096]{1,0:T(8,128)(2,1)S(1)} %collective-permute-done.23.refs_0_), channel_id=1, source_target_pairs={{0,8},{8,16},{16,24},{24,28},{28,20},{20,12},{12,4},{4,0},{1,9},{9... | collective-permute-start | bytes 1572872 | tf_op jit(solution)/shard_map/ppermute | solution.py:439
  73.7 14.9 %collective-permute-start.32 = (bf16[64,4096]{1,0:T(8,128)(2,1)S(1)}, bf16[64,4096]{1,0:T(8,128)(2,1)S(1)}, u32[]{:S(2)}, u32[]{:S(2)}) collective-permute-start(bf16[64,4096]{1,0:T(8,128)(2,1)S(1)} %collective-permute-done.24.refs_1_), channel_id=1, source_target_pairs={{8,0},{16,8},{24,16},{28,24},{20,28},{12,20},{4,12},{0,4},{9,1},{1... | collective-permute-start | bytes 1572872 | tf_op jit(solution)/shard_map/ppermute | solution.py:439
  76.7 7.8 %collective-permute-start.26 = (f32[512,128]{1,0:T(8,128)S(1)}, f32[512,128]{1,0:T(8,128)S(1)}, u32[]{:S(2)}, u32[]{:S(2)}) collective-permute-start(f32[512,128]{1,0:T(8,128)S(1)} %add.143), channel_id=1, source_target_pairs={{0,2},{1,3},{2,0},{3,1},{4,6},{5,7},{6,4},{7,5},{8,10},{9,11},{10,... | collective-permute-start | bytes 786440 | tf_op jit(solution)/shard_map/ppermute | solution.py:387
  81.4 3.1 %collective-permute-start.29 = (f32[512,128]{1,0:T(8,128)S(1)}, f32[512,128]{1,0:T(8,128)S(1)}, u32[]{:S(2)}, u32[]{:S(2)}) collective-permute-start(f32[512,128]{1,0:T(8,128)S(1)} %get-tuple-element.91), channel_id=1, source_target_pairs={{0,1},{1,0},{2,3},{3,2},{4,5},{5,4},{6,7},{7,6},{8,9},{9,8},{10,11... | collective-permute-start | bytes 786440 | tf_op jit(solution)/shard_map/ppermute | solution.py:387
  81.5 4.6 %collective-permute-start.22 = (f32[512,128]{1,0:T(8,128)S(1)}, f32[512,128]{1,0:T(8,128)S(1)}, u32[]{:S(2)}, u32[]{:S(2)}) collective-permute-start(f32[512,128]{1,0:T(8,128)S(1)} %add.142.refs_4_), channel_id=1, source_target_pairs={{0,1},{1,0},{2,3},{3,2},{4,5},{5,4},{6,7},{7,6},{8,9},{9,8},{10,11... | collective-permute-start | bytes 786440 | tf_op jit(solution)/shard_map/ppermute | solution.py:387
  84.4 1.7 %collective-permute-start.21 = (f32[512,128]{1,0:T(8,128)S(1)}, f32[512,128]{1,0:T(8,128)S(1)}, u32[]{:S(2)}, u32[]{:S(2)}) collective-permute-start(f32[512,128]{1,0:T(8,128)S(1)} %add.140.refs_3_), channel_id=1, source_target_pairs={{0,1},{1,0},{2,3},{3,2},{4,5},{5,4},{6,7},{7,6},{8,9},{9,8},{10,11... | collective-permute-start | bytes 786440 | tf_op jit(solution)/shard_map/ppermute | solution.py:387
  84.5 11.0 %collective-permute-start.30 = (f32[512,128]{1,0:T(8,128)S(1)}, f32[512,128]{1,0:T(8,128)S(1)}, u32[]{:S(2)}, u32[]{:S(2)}) collective-permute-start(f32[512,128]{1,0:T(8,128)S(1)} %add.145), channel_id=1, source_target_pairs={{0,2},{1,3},{2,0},{3,1},{4,6},{5,7},{6,4},{7,5},{8,10},{9,11},{10,... | collective-permute-start | bytes 786440 | tf_op jit(solution)/shard_map/ppermute | solution.py:387
  90.4 1.9 %collective-permute-start.33 = (f32[512,128]{1,0:T(8,128)S(1)}, f32[512,128]{1,0:T(8,128)S(1)}, u32[]{:S(2)}, u32[]{:S(2)}) collective-permute-start(f32[512,128]{1,0:T(8,128)S(1)} %cost_share.16), channel_id=1, source_target_pairs={{0,1},{1,0},{2,3},{3,2},{4,5},{5,4},{6,7},{7,6},{8,9},{9,8},{10,11... | collective-permute-start | bytes 786440 | tf_op jit(solution)/shard_map/ppermute | solution.py:387
  92.4 8.8 %collective-permute-start.34 = (f32[512,128]{1,0:T(8,128)S(1)}, f32[512,128]{1,0:T(8,128)S(1)}, u32[]{:S(2)}, u32[]{:S(2)}) collective-permute-start(f32[512,128]{1,0:T(8,128)S(1)} %add.147), channel_id=1, source_target_pairs={{0,2},{1,3},{2,0},{3,1},{4,6},{5,7},{6,4},{7,5},{8,10},{9,11},{10,... | collective-permute-start | bytes 786440 | tf_op jit(solution)/shard_map/ppermute | solution.py:387
  95.3 6.0 %collective-permute-start.35 = (f32[512,128]{1,0:T(8,128)S(1)}, f32[512,128]{1,0:T(8,128)S(1)}, u32[]{:S(2)}, u32[]{:S(2)}) collective-permute-start(f32[512,128]{1,0:T(8,128)S(1)} %add.144.refs_0_), channel_id=1, source_target_pairs={{0,1},{1,0},{2,3},{3,2},{4,5},{5,4},{6,7},{7,6},{8,9},{9,8},{10,11... | collective-permute-start | bytes 786440 | tf_op jit(solution)/shard_map/ppermute | solution.py:387
  95.6 5.7 %collective-permute-start.36 = (f32[512,128]{1,0:T(8,128)S(1)}, f32[512,128]{1,0:T(8,128)S(1)}, u32[]{:S(2)}, u32[]{:S(2)}) collective-permute-start(f32[512,128]{1,0:T(8,128)S(1)} %add.146.refs_1_), channel_id=1, source_target_pairs={{0,1},{1,0},{2,3},{3,2},{4,5},{5,4},{6,7},{7,6},{8,9},{9,8},{10,11... | collective-permute-start | bytes 786440 | tf_op jit(solution)/shard_map/ppermute | solution.py:387
  101.2 1.6 %collective-permute-start.37 = (f32[512,128]{1,0:T(8,128)S(1)}, f32[512,128]{1,0:T(8,128)S(1)}, u32[]{:S(2)}, u32[]{:S(2)}) collective-permute-start(f32[512,128]{1,0:T(8,128)S(1)} %add.148.refs_2_), channel_id=1, source_target_pairs={{0,1},{1,0},{2,3},{3,2},{4,5},{5,4},{6,7},{7,6},{8,9},{9,8},{10,11... | collective-permute-start | bytes 786440 | tf_op jit(solution)/shard_map/ppermute | solution.py:387

commit v5 on v4

--- a/solution.py
+++ b/solution.py
@@ -296,22 +296,19 @@
     put_sums(acc, out_ref, ids_ref[1] if rolled else None)
 
 
-def last_kernel(ids_ref, got_ref, e_ref, peak_ref, out_ref, pot_ref, scaled_ref, col_ref, *, scale, rolled, log_count):
+def last_kernel(ids_ref, got_ref, e_ref, peak_ref, out_ref, pot_ref, factor_ref, *, scale, rolled, log_count):
     rows_all = e_ref.shape[0]
     tiles = e_ref.shape[1] // LANES
-    group = group_of(e_ref.shape[0])
+    group = group_of(rows_all)
     w = spread(get_factors(got_ref, scale, ids_ref[2] if rolled else None))
 
     def body(i, acc):
         sums = [tree(jnp.add, [x * f for x, f in zip(load(e_ref, group_rows(i, g, group)), w)]) for g in range(group)]
-        sums = [jnp.sum(x, axis=1, keepdims=True) for x in sums]
+        sums = [1.0 / jnp.sum(x, axis=1, keepdims=True) for x in sums]
         for g in range(group):
             rows = group_rows(i, g, group)
-            col_ref[rows, :] = -eps_blur * (log_count + math.log(2) * peak_ref[rows, :] + jnp.log(sums[g]))
-            q = 1.0 / sums[g]
-            e = [x * q for x in load(e_ref, rows)]
-            store(scaled_ref, rows, e)
-            acc = [a + x for a, x in zip(acc, e)]
+            factor_ref[rows, :] = jnp.broadcast_to(sums[g], (SUB, LANES))
+            acc = [a + x * sums[g] for a, x in zip(acc, load(e_ref, rows))]
         return tuple(acc)
 
     acc = tuple(jnp.zeros((SUB, LANES), jnp.float32) for _ in range(tiles))
@@ -320,12 +317,15 @@
     shape = (LANES, LANES)
     eye = lax.broadcasted_iota(jnp.int32, shape, 0) == lax.broadcasted_iota(jnp.int32, shape, 1)
     for i in range(rows_all // LANES):
-        block = col_ref[i * LANES : (i + 1) * LANES, :]
-        pot_ref[i : i + 1, :] = jnp.sum(jnp.where(eye, block, 0.0), axis=0, keepdims=True)
-
-
-def out_kernel(ids_ref, got_ref, scaled_ref, perm_ref, pot_ref, member_ref, *, scale, rolled):
-    tiles = scaled_ref.shape[1] // LANES
+        rows = slice(i * LANES, (i + 1) * LANES)
+        peak, factor = (
+            jnp.sum(jnp.where(eye, ref[rows, :], 0.0), axis=0, keepdims=True) for ref in (peak_ref, factor_ref)
+        )
+        pot_ref[i : i + 1, :] = -eps_blur * (log_count + math.log(2) * peak - jnp.log(factor))
+
+
+def out_kernel(ids_ref, got_ref, e_ref, factor_ref, perm_ref, pot_ref, member_ref, *, scale, rolled):
+    tiles = e_ref.shape[1] // LANES
     factors = get_factors(got_ref, scale, ids_ref[2] if rolled else None)
     w = jnp.concatenate([factors[i : i + 1, :] for i in range(tiles)], axis=1)
     v = eps_blur * jnp.log(w)
@@ -338,11 +338,12 @@
         parts.astype(jnp.bfloat16), perm_ref[...], NT, preferred_element_type=jnp.float32
     )
     pot_ref[...] = moved[0:1, :] + moved[1:2, :] + moved[2:3, :]
-    step = min(256, scaled_ref.shape[0])
-    for i in range(0, scaled_ref.shape[0], step):
-        plan = (scaled_ref[i : i + step, :] * w).astype(jnp.bfloat16)
+    step = min(256, e_ref.shape[0])
+    for i in range(0, e_ref.shape[0], step):
+        tile = load(e_ref, slice(i, i + step))
+        plan = jnp.concatenate([x * factor_ref[i : i + step, :] for x in tile], axis=1) * w
         member_ref[:, i : i + step] = lax.dot_general(
-            perm_ref[...], plan, NT, preferred_element_type=jnp.float32
+            perm_ref[...], plan.astype(jnp.bfloat16), NT, preferred_element_type=jnp.float32
         ).astype(member_ref.dtype)
 
 
@@ -515,16 +516,15 @@
             compiler_params=ROOM,
             name="step",
         )(ids, *kept(exchange(x), e))
-    x, scen_pot, scaled = pl.pallas_call(
+    x, scen_pot, factor = pl.pallas_call(
         functools.partial(last_kernel, scale=scale, rolled=rolled, log_count=math.log(count_s)),
         out_shape=(
             sums,
             jax.ShapeDtypeStruct((scen_rows // LANES, LANES), jnp.float32),
-            f32(scen_rows, count_r),
+            f32(scen_rows, LANES),
         ),
         in_specs=[SMEM] + [VMEM] * 3,
         out_specs=(VMEM,) * 3,
-        scratch_shapes=[pltpu.VMEM((scen_rows, LANES), jnp.float32)],
         compiler_params=ROOM,
         name="last",
     )(ids, *kept(exchange(x), e, peak))
@@ -534,11 +534,11 @@
             jax.ShapeDtypeStruct((1, rows_out), jnp.float32),
             jax.ShapeDtypeStruct((rows_out, scen_rows), jnp.bfloat16),
         ),
-        in_specs=[SMEM] + [VMEM] * 3,
+        in_specs=[SMEM] + [VMEM] * 4,
         out_specs=(VMEM, VMEM),
         compiler_params=ROOM,
         name="out",
-    )(ids, *kept(exchange(x), scaled, perm))
+    )(ids, *kept(exchange(x), e, factor, perm))
     return scen_pot.reshape(scen_rows), rep_pot.reshape(rows_out), member
 
 

time: 139 us -> 139 us (level)
  no operation moved by 1% of the time
where the time goes in v5:
time: 139 us
  Pallas kernels  40.5 us (29%)
  waiting for transfers between devices  35.2 us (25%)
  starting transfers between devices  31.6 us (23%)
  blocking collectives  29.4 us (21%)
    all_to_all x3, blocking collectives, exchange(): x = lax.all_to_all(x, 'scen', 0, 0, tiled=False)  29.4 us
    ppermute x14, waiting for transfers between devices, on_device(): lax.ppermute(x, 'scen', way)  26 us
    pallas_call x9, Pallas kernels, cost_share(): pl.pallas_call(functools.partial(cost_kernel, tile=min(256, rows // 2), p...  23.9 us
    ppermute x24, starting transfers between devices, swap(): return lax.ppermute(x, 'rep', [(i, i ^ bit) for i in range(n_rep)])  15.9 us
    ppermute x14, starting transfers between devices, on_device(): lax.ppermute(x, 'scen', way)  15.7 us
    ppermute x24, waiting for transfers between devices, swap(): return lax.ppermute(x, 'rep', [(i, i ^ bit) for i in range(n_rep)])  9.19 us
    pallas_call x1, Pallas kernels, norms(): pl.pallas_call(norm_kernel, out_shape=pltpu.VMEM((scenarios.shape[0], LAN...  4.51 us
    pallas_call x1, Pallas kernels, pick(): pl.pallas_call(functools.partial(pick_kernel, step=step), out_shape=(pltp...  4.09 us
  transfers between devices with their start and end apart: 38, of which 16 were waited for; matrix products, arithmetic and copies ran while one was open for 1% of the time, Pallas kernels for 21%

profile of v5, /device:TPU:0, one launch (start us, length us, event | category | flops | bytes accessed | tf_op | source)
XLA Modules:
  0.0 138.8 jit_solution(3960459226992126250)
XLA Ops:
  0.6 4.1 %pick.1 = (bf16[1024,4096]{1,0:T(8,128)(2,1)S(1)}, bf16[64,4096]{1,0:T(8,128)(2,1)S(1)}, bf16[64,4096]{1,0:T(8,128)(2,1)S(1)}) custom-call(s32[8,128]{1,0:T(8,128)} %bitcast.6, bf16[1024,4096]{1,0:T(8,128)(2,1)} %scen_ref.1), custom_call_target="tpu_custom_call" | custom-call | flops 4000000000 | bytes 10000000 | tf_op jit(solution)/shard_map/pick/pallas_call | solution.py:85
  4.7 3.1 %collective-permute-start.2 = (bf16[64,4096]{1,0:T(8,128)(2,1)S(1)}, bf16[64,4096]{1,0:T(8,128)(2,1)S(1)}, u32[]{:S(2)}, u32[]{:S(2)}) collective-permute-start(bf16[64,4096]{1,0:T(8,128)(2,1)S(1)} %get-tuple-element.69.refs_0_), channel_id=1, source_target_pairs={{0,8},{8,16},{16,24},{24,28},{28,20},{20,12},{12,4},{4,0},{1,9},{9... | collective-permute-start | bytes 1572872 | tf_op jit(solution)/shard_map/ppermute | solution.py:440
  7.8 4.5 %norms.1.sq_ref = f32[1024,128]{1,0:T(8,128)S(1)} custom-call(bf16[1024,4096]{1,0:T(8,128)(2,1)S(1)} %get-tuple-element.58.scen_ref), custom_call_target="tpu_custom_call" | custom-call | flops 4000000000 | bytes 10000000 | tf_op jit(solution)/shard_map/norms/pallas_call | solution.py:113
  12.4 2.9 %cost_share.9 = (f32[512,128]{1,0:T(8,128)S(1)}, f32[512,128]{1,0:T(8,128)S(1)}) custom-call(s32[3]{0:T(128)S(1)} %pad_add_fusion.core_ref.ids_ref, bf16[1024,4096]{1,0:T(8,128)(2,1)S(1)} %get-tuple-element.58.scen_ref, f32[1024,128]{1,0:T(8,128)S(1)} %norms.1.sq_ref, bf16[64,4096]{1,0:T(8,128)(2,1)S(1)} %get-tuple-element.69.refs_0_, ...), custom_call_target="tpu_custom_call" | custom-call | flops 4000000000 | bytes 10000000 | tf_op jit(solution)/shard_map/cost_share/pallas_call | solution.py:140
  15.4 2.1 %collective-permute-start.6 = (bf16[64,4096]{1,0:T(8,128)(2,1)S(1)}, bf16[64,4096]{1,0:T(8,128)(2,1)S(1)}, u32[]{:S(2)}, u32[]{:S(2)}) collective-permute-start(bf16[64,4096]{1,0:T(8,128)(2,1)S(1)} %get-tuple-element.68.refs_1_), channel_id=1, source_target_pairs={{0,8},{8,16},{16,24},{24,28},{28,20},{20,12},{12,4},{4,0},{1,9},{9... | collective-permute-start | bytes 1572872 | tf_op jit(solution)/shard_map/ppermute | solution.py:440
  18.0 2.1 %collective-permute-start.1 = (f32[512,128]{1,0:T(8,128)S(1)}, f32[512,128]{1,0:T(8,128)S(1)}, u32[]{:S(2)}, u32[]{:S(2)}) collective-permute-start(f32[512,128]{1,0:T(8,128)S(1)} %add.123), channel_id=1, source_target_pairs={{0,2},{1,3},{2,0},{3,1},{4,6},{5,7},{6,4},{7,5},{8,10},{9,11},{10,... | collective-permute-start | bytes 786440 | tf_op jit(solution)/shard_map/ppermute | solution.py:388
  20.5 1.6 %collective-permute-done.3.refs_1_ = bf16[64,4096]{1,0:T(8,128)(2,1)S(1)} collective-permute-done((bf16[64,4096]{1,0:T(8,128)(2,1)S(1)}, bf16[64,4096]{1,0:T(8,128)(2,1)S(1)}, u32[]{:S(2)}, u32[]{:S(2)}) %collective-permute-start.3) | collective-permute-done | bytes 524320 | tf_op jit(solution)/shard_map/ppermute | solution.py:440
  22.1 1.6 %collective-permute-start.10 = (bf16[64,4096]{1,0:T(8,128)(2,1)S(1)}, bf16[64,4096]{1,0:T(8,128)(2,1)S(1)}, u32[]{:S(2)}, u32[]{:S(2)}) collective-permute-start(bf16[64,4096]{1,0:T(8,128)(2,1)S(1)} %collective-permute-done.2.refs_0_), channel_id=1, source_target_pairs={{0,8},{8,16},{16,24},{24,28},{28,20},{20,12},{12,4},{4,0},{1,9},{9... | collective-permute-start | bytes 1572872 | tf_op jit(solution)/shard_map/ppermute | solution.py:440
  24.1 2.9 %cost_share.10 = (f32[512,128]{1,0:T(8,128)S(1)}, f32[512,128]{1,0:T(8,128)S(1)}) custom-call(s32[3]{0:T(128)S(1)} %pad_add_fusion.core_ref.ids_ref, bf16[1024,4096]{1,0:T(8,128)(2,1)S(1)} %get-tuple-element.58.scen_ref, f32[1024,128]{1,0:T(8,128)S(1)} %norms.1.sq_ref, bf16[64,4096]{1,0:T(8,128)(2,1)S(1)} %collective-permute-done.2.refs_0_, ...), custom_call_target="tpu_custom_call" | custom-call | flops 4000000000 | bytes 10000000 | tf_op jit(solution)/shard_map/cost_share/pallas_call | solution.py:140
  27.0 4.7 %collective-permute-done.6.refs_1_ = bf16[64,4096]{1,0:T(8,128)(2,1)S(1)} collective-permute-done((bf16[64,4096]{1,0:T(8,128)(2,1)S(1)}, bf16[64,4096]{1,0:T(8,128)(2,1)S(1)}, u32[]{:S(2)}, u32[]{:S(2)}) %collective-permute-start.6) | collective-permute-done | bytes 524320 | tf_op jit(solution)/shard_map/ppermute | solution.py:440
  31.7 1.6 %collective-permute-done.7.refs_0_ = bf16[64,4096]{1,0:T(8,128)(2,1)S(1)} collective-permute-done((bf16[64,4096]{1,0:T(8,128)(2,1)S(1)}, bf16[64,4096]{1,0:T(8,128)(2,1)S(1)}, u32[]{:S(2)}, u32[]{:S(2)}) %collective-permute-start.7) | collective-permute-done | bytes 524320 | tf_op jit(solution)/shard_map/ppermute | solution.py:440
  33.3 2.9 %cost_share.11 = (f32[512,128]{1,0:T(8,128)S(1)}, f32[512,128]{1,0:T(8,128)S(1)}) custom-call(s32[3]{0:T(128)S(1)} %pad_add_fusion.core_ref.ids_ref, bf16[1024,4096]{1,0:T(8,128)(2,1)S(1)} %get-tuple-element.58.scen_ref, f32[1024,128]{1,0:T(8,128)S(1)} %norms.1.sq_ref, bf16[64,4096]{1,0:T(8,128)(2,1)S(1)} %collective-permute-done.7.refs_0_, ...), custom_call_target="tpu_custom_call" | custom-call | flops 4000000000 | bytes 10000000 | tf_op jit(solution)/shard_map/cost_share/pallas_call | solution.py:140
  36.3 1.6 %collective-permute-start.5 = (f32[512,128]{1,0:T(8,128)S(1)}, f32[512,128]{1,0:T(8,128)S(1)}, u32[]{:S(2)}, u32[]{:S(2)}) collective-permute-start(f32[512,128]{1,0:T(8,128)S(1)} %add.135), channel_id=1, source_target_pairs={{0,2},{1,3},{2,0},{3,1},{4,6},{5,7},{6,4},{7,5},{8,10},{9,11},{10,... | collective-permute-start | bytes 786440 | tf_op jit(solution)/shard_map/ppermute | solution.py:388
  38.0 1.6 %collective-permute-start.14 = (bf16[64,4096]{1,0:T(8,128)(2,1)S(1)}, bf16[64,4096]{1,0:T(8,128)(2,1)S(1)}, u32[]{:S(2)}, u32[]{:S(2)}) collective-permute-start(bf16[64,4096]{1,0:T(8,128)(2,1)S(1)} %collective-permute-done.6.refs_1_), channel_id=1, source_target_pairs={{0,8},{8,16},{16,24},{24,28},{28,20},{20,12},{12,4},{4,0},{1,9},{9... | collective-permute-start | bytes 1572872 | tf_op jit(solution)/shard_map/ppermute | solution.py:440
  40.1 2.9 %collective-permute-done.10.refs_0_ = bf16[64,4096]{1,0:T(8,128)(2,1)S(1)} collective-permute-done((bf16[64,4096]{1,0:T(8,128)(2,1)S(1)}, bf16[64,4096]{1,0:T(8,128)(2,1)S(1)}, u32[]{:S(2)}, u32[]{:S(2)}) %collective-permute-start.10) | collective-permute-done | bytes 524320 | tf_op jit(solution)/shard_map/ppermute | solution.py:440
  42.9 1.6 %collective-permute-done.11.refs_1_ = bf16[64,4096]{1,0:T(8,128)(2,1)S(1)} collective-permute-done((bf16[64,4096]{1,0:T(8,128)(2,1)S(1)}, bf16[64,4096]{1,0:T(8,128)(2,1)S(1)}, u32[]{:S(2)}, u32[]{:S(2)}) %collective-permute-start.11) | collective-permute-done | bytes 524320 | tf_op jit(solution)/shard_map/ppermute | solution.py:440
  44.6 1.5 %collective-permute-start.9 = (f32[512,128]{1,0:T(8,128)S(1)}, f32[512,128]{1,0:T(8,128)S(1)}, u32[]{:S(2)}, u32[]{:S(2)}) collective-permute-start(f32[512,128]{1,0:T(8,128)S(1)} %add.137), channel_id=1, source_target_pairs={{0,2},{1,3},{2,0},{3,1},{4,6},{5,7},{6,4},{7,5},{8,10},{9,11},{10,... | collective-permute-start | bytes 786440 | tf_op jit(solution)/shard_map/ppermute | solution.py:388
  46.1 1.6 %collective-permute-start.23 = (bf16[64,4096]{1,0:T(8,128)(2,1)S(1)}, bf16[64,4096]{1,0:T(8,128)(2,1)S(1)}, u32[]{:S(2)}, u32[]{:S(2)}) collective-permute-start(bf16[64,4096]{1,0:T(8,128)(2,1)S(1)} %collective-permute-done.10.refs_0_), channel_id=1, source_target_pairs={{0,8},{8,16},{16,24},{24,28},{28,20},{20,12},{12,4},{4,0},{1,9},{9... | collective-permute-start | bytes 1572872 | tf_op jit(solution)/shard_map/ppermute | solution.py:440
  47.7 2.9 %cost_share.12 = (f32[512,128]{1,0:T(8,128)S(1)}, f32[512,128]{1,0:T(8,128)S(1)}) custom-call(s32[3]{0:T(128)S(1)} %pad_add_fusion.core_ref.ids_ref, bf16[1024,4096]{1,0:T(8,128)(2,1)S(1)} %get-tuple-element.58.scen_ref, f32[1024,128]{1,0:T(8,128)S(1)} %norms.1.sq_ref, bf16[64,4096]{1,0:T(8,128)(2,1)S(1)} %collective-permute-done.10.refs_0_, ...), custom_call_target="tpu_custom_call" | custom-call | flops 4000000000 | bytes 10000000 | tf_op jit(solution)/shard_map/cost_share/pallas_call | solution.py:140
  51.3 2.9 %collective-permute-done.14.refs_1_ = bf16[64,4096]{1,0:T(8,128)(2,1)S(1)} collective-permute-done((bf16[64,4096]{1,0:T(8,128)(2,1)S(1)}, bf16[64,4096]{1,0:T(8,128)(2,1)S(1)}, u32[]{:S(2)}, u32[]{:S(2)}) %collective-permute-start.14) | collective-permute-done | bytes 524320 | tf_op jit(solution)/shard_map/ppermute | solution.py:440
  54.2 1.6 %collective-permute-done.15.refs_0_ = bf16[64,4096]{1,0:T(8,128)(2,1)S(1)} collective-permute-done((bf16[64,4096]{1,0:T(8,128)(2,1)S(1)}, bf16[64,4096]{1,0:T(8,128)(2,1)S(1)}, u32[]{:S(2)}, u32[]{:S(2)}) %collective-permute-start.15) | collective-permute-done | bytes 524320 | tf_op jit(solution)/shard_map/ppermute | solution.py:440
  55.8 2.9 %cost_share.13 = (f32[512,128]{1,0:T(8,128)S(1)}, f32[512,128]{1,0:T(8,128)S(1)}) custom-call(s32[3]{0:T(128)S(1)} %pad_add_fusion.core_ref.ids_ref, bf16[1024,4096]{1,0:T(8,128)(2,1)S(1)} %get-tuple-element.58.scen_ref, f32[1024,128]{1,0:T(8,128)S(1)} %norms.1.sq_ref, bf16[64,4096]{1,0:T(8,128)(2,1)S(1)} %collective-permute-done.15.refs_0_, ...), custom_call_target="tpu_custom_call" | custom-call | flops 4000000000 | bytes 10000000 | tf_op jit(solution)/shard_map/cost_share/pallas_call | solution.py:140
  59.3 1.7 %collective-permute-start.27 = (bf16[64,4096]{1,0:T(8,128)(2,1)S(1)}, bf16[64,4096]{1,0:T(8,128)(2,1)S(1)}, u32[]{:S(2)}, u32[]{:S(2)}) collective-permute-start(bf16[64,4096]{1,0:T(8,128)(2,1)S(1)} %collective-permute-done.14.refs_1_), channel_id=1, source_target_pairs={{0,8},{8,16},{16,24},{24,28},{28,20},{20,12},{12,4},{4,0},{1,9},{9... | collective-permute-start | bytes 1572872 | tf_op jit(solution)/shard_map/ppermute | solution.py:440
  61.5 1.6 %collective-permute-start.18 = (f32[512,128]{1,0:T(8,128)S(1)}, f32[512,128]{1,0:T(8,128)S(1)}, u32[]{:S(2)}, u32[]{:S(2)}) collective-permute-start(f32[512,128]{1,0:T(8,128)S(1)} %add.141), channel_id=1, source_target_pairs={{0,2},{1,3},{2,0},{3,1},{4,6},{5,7},{6,4},{7,5},{8,10},{9,11},{10,... | collective-permute-start | bytes 786440 | tf_op jit(solution)/shard_map/ppermute | solution.py:388
  63.1 2.3 %collective-permute-done.23.refs_0_ = bf16[64,4096]{1,0:T(8,128)(2,1)S(1)} collective-permute-done((bf16[64,4096]{1,0:T(8,128)(2,1)S(1)}, bf16[64,4096]{1,0:T(8,128)(2,1)S(1)}, u32[]{:S(2)}, u32[]{:S(2)}) %collective-permute-start.23) | collective-permute-done | bytes 524320 | tf_op jit(solution)/shard_map/ppermute | solution.py:440
  65.4 1.6 %collective-permute-done.24.refs_1_ = bf16[64,4096]{1,0:T(8,128)(2,1)S(1)} collective-permute-done((bf16[64,4096]{1,0:T(8,128)(2,1)S(1)}, bf16[64,4096]{1,0:T(8,128)(2,1)S(1)}, u32[]{:S(2)}, u32[]{:S(2)}) %collective-permute-start.24) | collective-permute-done | bytes 524320 | tf_op jit(solution)/shard_map/ppermute | solution.py:440
  67.0 2.9 %cost_share.14 = (f32[512,128]{1,0:T(8,128)S(1)}, f32[512,128]{1,0:T(8,128)S(1)}) custom-call(s32[3]{0:T(128)S(1)} %pad_add_fusion.core_ref.ids_ref, bf16[1024,4096]{1,0:T(8,128)(2,1)S(1)} %get-tuple-element.58.scen_ref, f32[1024,128]{1,0:T(8,128)S(1)} %norms.1.sq_ref, bf16[64,4096]{1,0:T(8,128)(2,1)S(1)} %collective-permute-done.23.refs_0_, ...), custom_call_target="tpu_custom_call" | custom-call | flops 4000000000 | bytes 10000000 | tf_op jit(solution)/shard_map/cost_share/pallas_call | solution.py:140
  70.5 1.5 %collective-permute-start.13 = (f32[512,128]{1,0:T(8,128)S(1)}, f32[512,128]{1,0:T(8,128)S(1)}, u32[]{:S(2)}, u32[]{:S(2)}) collective-permute-start(f32[512,128]{1,0:T(8,128)S(1)} %add.139), channel_id=1, source_target_pairs={{0,2},{1,3},{2,0},{3,1},{4,6},{5,7},{6,4},{7,5},{8,10},{9,11},{10,... | collective-permute-start | bytes 786440 | tf_op jit(solution)/shard_map/ppermute | solution.py:388
  72.1 1.6 %collective-permute-start.31 = (bf16[64,4096]{1,0:T(8,128)(2,1)S(1)}, bf16[64,4096]{1,0:T(8,128)(2,1)S(1)}, u32[]{:S(2)}, u32[]{:S(2)}) collective-permute-start(bf16[64,4096]{1,0:T(8,128)(2,1)S(1)} %collective-permute-done.23.refs_0_), channel_id=1, source_target_pairs={{0,8},{8,16},{16,24},{24,28},{28,20},{20,12},{12,4},{4,0},{1,9},{9... | collective-permute-start | bytes 1572872 | tf_op jit(solution)/shard_map/ppermute | solution.py:440
  74.3 2.4 %collective-permute-done.27.refs_1_ = bf16[64,4096]{1,0:T(8,128)(2,1)S(1)} collective-permute-done((bf16[64,4096]{1,0:T(8,128)(2,1)S(1)}, bf16[64,4096]{1,0:T(8,128)(2,1)S(1)}, u32[]{:S(2)}, u32[]{:S(2)}) %collective-permute-start.27) | collective-permute-done | bytes 524320 | tf_op jit(solution)/shard_map/ppermute | solution.py:440
  76.7 1.8 %collective-permute-start.26 = (f32[512,128]{1,0:T(8,128)S(1)}, f32[512,128]{1,0:T(8,128)S(1)}, u32[]{:S(2)}, u32[]{:S(2)}) collective-permute-start(f32[512,128]{1,0:T(8,128)S(1)} %add.143), channel_id=1, source_target_pairs={{0,2},{1,3},{2,0},{3,1},{4,6},{5,7},{6,4},{7,5},{8,10},{9,11},{10,... | collective-permute-start | bytes 786440 | tf_op jit(solution)/shard_map/ppermute | solution.py:388
  78.5 2.9 %cost_share.15 = (f32[512,128]{1,0:T(8,128)S(1)}, f32[512,128]{1,0:T(8,128)S(1)}) custom-call(s32[3]{0:T(128)S(1)} %pad_add_fusion.core_ref.ids_ref, bf16[1024,4096]{1,0:T(8,128)(2,1)S(1)} %get-tuple-element.58.scen_ref, f32[1024,128]{1,0:T(8,128)S(1)} %norms.1.sq_ref, bf16[64,4096]{1,0:T(8,128)(2,1)S(1)} %collective-permute-done.28.refs_0_, ...), custom_call_target="tpu_custom_call" | custom-call | flops 4000000000 | bytes 10000000 | tf_op jit(solution)/shard_map/cost_share/pallas_call | solution.py:140
  82.0 2.4 %collective-permute-done.26 = f32[512,128]{1,0:T(8,128)S(1)} collective-permute-done((f32[512,128]{1,0:T(8,128)S(1)}, f32[512,128]{1,0:T(8,128)S(1)}, u32[]{:S(2)}, u32[]{:S(2)}) %collective-permute-start.26) | collective-permute-done | bytes 262176 | tf_op jit(solution)/shard_map/ppermute | solution.py:388
  84.5 1.6 %collective-permute-start.30 = (f32[512,128]{1,0:T(8,128)S(1)}, f32[512,128]{1,0:T(8,128)S(1)}, u32[]{:S(2)}, u32[]{:S(2)}) collective-permute-start(f32[512,128]{1,0:T(8,128)S(1)} %add.145), channel_id=1, source_target_pairs={{0,2},{1,3},{2,0},{3,1},{4,6},{5,7},{6,4},{7,5},{8,10},{9,11},{10,... | collective-permute-start | bytes 786440 | tf_op jit(solution)/shard_map/ppermute | solution.py:388
  87.1 1.5 %collective-permute-done.32.refs_1_ = bf16[64,4096]{1,0:T(8,128)(2,1)S(1)} collective-permute-done((bf16[64,4096]{1,0:T(8,128)(2,1)S(1)}, bf16[64,4096]{1,0:T(8,128)(2,1)S(1)}, u32[]{:S(2)}, u32[]{:S(2)}) %collective-permute-start.32) | collective-permute-done | bytes 524320 | tf_op jit(solution)/shard_map/ppermute | solution.py:440
  88.6 1.8 %cost_share.16 = f32[512,128]{1,0:T(8,128)S(1)} custom-call(s32[3]{0:T(128)S(1)} %pad_add_fusion.core_ref.ids_ref, bf16[1024,4096]{1,0:T(8,128)(2,1)S(1)} %get-tuple-element.58.scen_ref, f32[1024,128]{1,0:T(8,128)S(1)} %norms.1.sq_ref, bf16[64,4096]{1,0:T(8,128)(2,1)S(1)} %collective-permute-done.31.refs_0_, bf16[64,4096]{1,0:T(8,128)(2,1)S(1)} %collective-permute-done.32.refs_1_), custom_call_target="tpu_custom_call" | custom-call | flops 4000000000 | bytes 10000000 | tf_op jit(solution)/shard_map/cost_share/pallas_call | solution.py:140
  90.5 1.8 %cost_share.17 = f32[512,128]{1,0:T(8,128)S(1)} custom-call(s32[3]{0:T(128)S(1)} %pad_add_fusion.core_ref.ids_ref, bf16[1024,4096]{1,0:T(8,128)(2,1)S(1)} %get-tuple-element.58.scen_ref, f32[1024,128]{1,0:T(8,128)S(1)} %norms.1.sq_ref, bf16[64,4096]{1,0:T(8,128)(2,1)S(1)} %collective-permute-done.31.refs_0_, bf16[64,4096]{1,0:T(8,128)(2,1)S(1)} %collective-permute-done.32.refs_1_), custom_call_target="tpu_custom_call" | custom-call | flops 4000000000 | bytes 10000000 | tf_op jit(solution)/shard_map/cost_share/pallas_call | solution.py:140
  92.4 1.6 %collective-permute-start.34 = (f32[512,128]{1,0:T(8,128)S(1)}, f32[512,128]{1,0:T(8,128)S(1)}, u32[]{:S(2)}, u32[]{:S(2)}) collective-permute-start(f32[512,128]{1,0:T(8,128)S(1)} %add.147), channel_id=1, source_target_pairs={{0,2},{1,3},{2,0},{3,1},{4,6},{5,7},{6,4},{7,5},{8,10},{9,11},{10,... | collective-permute-start | bytes 786440 | tf_op jit(solution)/shard_map/ppermute | solution.py:388
  93.9 1.3 early.1
  95.9 5.2 %collective-permute-done.34 = f32[512,128]{1,0:T(8,128)S(1)} collective-permute-done((f32[512,128]{1,0:T(8,128)S(1)}, f32[512,128]{1,0:T(8,128)S(1)}, u32[]{:S(2)}, u32[]{:S(2)}) %collective-permute-start.34) | collective-permute-done | bytes 262176 | tf_op jit(solution)/shard_map/ppermute | solution.py:388
  101.3 1.5 %collective-permute-done.37.refs_5_ = f32[512,128]{1,0:T(8,128)S(1)} collective-permute-done((f32[512,128]{1,0:T(8,128)S(1)}, f32[512,128]{1,0:T(8,128)S(1)}, u32[]{:S(2)}, u32[]{:S(2)}) %collective-permute-start.37) | collective-permute-done | bytes 262176 | tf_op jit(solution)/shard_map/ppermute | solution.py:388
  102.8 1.5 %late.1 = (f32[1024,1024]{1,0:T(8,128)S(1)}, f32[1024,128]{1,0:T(8,128)S(1)}, f32[8,8,128]{2,1,0:T(8,128)S(1)}) custom-call(s32[3]{0:T(128)S(1)} %pad_add_fusion.core_ref.ids_ref, f32[1024,640]{1,0:T(8,128)S(1)} %get-tuple-element.82.early_ref, f32[1024,128]{1,0:T(8,128)S(1)} %get-tuple-element.83.old_peak_ref, ...), custom_call_target="tpu_custom_call" | custom-call | tf_op jit(solution)/shard_map/late/pallas_call | solution.py:501
  104.2 11.3 %all_to_all.15.got_ref = f32[8,8,128]{2,1,0:T(8,128)S(1)} all-to-all(f32[8,8,128]{2,1,0:T(8,128)S(1)} %get-tuple-element.97), channel_id=1, replica_groups=mesh['scen'=8,'rep'=4] {'scen'}, dimensions={0} | all-to-all | bytes 65536 | tf_op jit(solution)/shard_map/all_to_all | solution.py:496
  115.5 1.1 step.1
  116.6 9.1 %all_to_all.16.got_ref = f32[8,8,128]{2,1,0:T(8,128)S(1)} all-to-all(f32[8,8,128]{2,1,0:T(8,128)S(1)} %step.1), channel_id=1, replica_groups=mesh['scen'=8,'rep'=4] {'scen'}, dimensions={0} | all-to-all | bytes 65536 | tf_op jit(solution)/shard_map/all_to_all | solution.py:496
  125.7 1.9 %last.1 = (f32[8,8,128]{2,1,0:T(8,128)S(1)}, f32[8,128]{1,0:T(8,128)}, f32[1024,128]{1,0:T(8,128)S(1)}) custom-call(s32[3]{0:T(128)S(1)} %pad_add_fusion.core_ref.ids_ref, f32[8,8,128]{2,1,0:T(8,128)S(1)} %all_to_all.16.got_ref, f32[1024,1024]{1,0:T(8,128)S(1)} %get-tuple-element.98.e_ref, f32[1024,128]{1,0:T(8,128)S(1)} %get-tuple-element.99.peak_ref), custom_call_target="tpu_custom_call" | custom-call | tf_op jit(solution)/shard_map/last/pallas_call | solution.py:519
  127.6 9.0 %all_to_all.17.got_ref = f32[8,8,128]{2,1,0:T(8,128)S(1)} all-to-all(f32[8,8,128]{2,1,0:T(8,128)S(1)} %get-tuple-element.101), channel_id=1, replica_groups=mesh['scen'=8,'rep'=4] {'scen'}, dimensions={0} | all-to-all | bytes 65536 | tf_op jit(solution)/shard_map/all_to_all | solution.py:496
  136.6 2.2 %out.1 = (f32[1,256]{1,0:T(1,128)}, bf16[256,1024]{1,0:T(8,128)(2,1)}) custom-call(s32[3]{0:T(128)S(1)} %pad_add_fusion.core_ref.ids_ref, f32[8,8,128]{2,1,0:T(8,128)S(1)} %all_to_all.17.got_ref, f32[1024,1024]{1,0:T(8,128)S(1)} %get-tuple-element.98.e_ref, f32[1024,128]{1,0:T(8,128)S(1)} %get-tuple-element.102.factor_ref, bf16[256,1024]{1,0:T(8,128)(2,1)S(1)} %fusion.perm_ref), custom_call_target="tpu_custom_call" | custom-call | tf_op jit(solution)/shard_map/out/pallas_call | solution.py:531
  (70 shorter events, 7.7 us)
Async XLA Ops:
  4.7 15.7 %collective-permute-start.2 = (bf16[64,4096]{1,0:T(8,128)(2,1)S(1)}, bf16[64,4096]{1,0:T(8,128)(2,1)S(1)}, u32[]{:S(2)}, u32[]{:S(2)}) collective-permute-start(bf16[64,4096]{1,0:T(8,128)(2,1)S(1)} %get-tuple-element.69.refs_0_), channel_id=1, source_target_pairs={{0,8},{8,16},{16,24},{24,28},{28,20},{20,12},{12,4},{4,0},{1,9},{9... | collective-permute-start | bytes 1572872 | tf_op jit(solution)/shard_map/ppermute | solution.py:440
  7.8 14.3 %collective-permute-start.3 = (bf16[64,4096]{1,0:T(8,128)(2,1)S(1)}, bf16[64,4096]{1,0:T(8,128)(2,1)S(1)}, u32[]{:S(2)}, u32[]{:S(2)}) collective-permute-start(bf16[64,4096]{1,0:T(8,128)(2,1)S(1)} %get-tuple-element.68.refs_1_), channel_id=1, source_target_pairs={{8,0},{16,8},{24,16},{28,24},{20,28},{12,20},{4,12},{0,4},{9,1},{1... | collective-permute-start | bytes 1572872 | tf_op jit(solution)/shard_map/ppermute | solution.py:440
  12.3 5.1 %copy-start = (s32[1024]{0:T(1024)S(1)}, s32[1024]{0:T(1024)}, u32[]{:S(2)}) copy-start(s32[1024]{0:T(1024)} %param.3) | copy-start | bytes 12292
  15.3 2.7 %collective-permute-start = (f32[512,128]{1,0:T(8,128)S(1)}, f32[512,128]{1,0:T(8,128)S(1)}, u32[]{:S(2)}, u32[]{:S(2)}) collective-permute-start(f32[512,128]{1,0:T(8,128)S(1)} %get-tuple-element.62), channel_id=1, source_target_pairs={{0,1},{1,0},{2,3},{3,2},{4,5},{5,4},{6,7},{7,6},{8,9},{9,8},{10,11... | collective-permute-start | bytes 786440 | tf_op jit(solution)/shard_map/ppermute | solution.py:388
  15.4 16.3 %collective-permute-start.6 = (bf16[64,4096]{1,0:T(8,128)(2,1)S(1)}, bf16[64,4096]{1,0:T(8,128)(2,1)S(1)}, u32[]{:S(2)}, u32[]{:S(2)}) collective-permute-start(bf16[64,4096]{1,0:T(8,128)(2,1)S(1)} %get-tuple-element.68.refs_1_), channel_id=1, source_target_pairs={{0,8},{8,16},{16,24},{24,28},{28,20},{20,12},{12,4},{4,0},{1,9},{9... | collective-permute-start | bytes 1572872 | tf_op jit(solution)/shard_map/ppermute | solution.py:440
  17.5 15.9 %collective-permute-start.7 = (bf16[64,4096]{1,0:T(8,128)(2,1)S(1)}, bf16[64,4096]{1,0:T(8,128)(2,1)S(1)}, u32[]{:S(2)}, u32[]{:S(2)}) collective-permute-start(bf16[64,4096]{1,0:T(8,128)(2,1)S(1)} %get-tuple-element.69.refs_0_), channel_id=1, source_target_pairs={{8,0},{16,8},{24,16},{28,24},{20,28},{12,20},{4,12},{0,4},{9,1},{1... | collective-permute-start | bytes 1572872 | tf_op jit(solution)/shard_map/ppermute | solution.py:440
  18.0 19.9 %collective-permute-start.1 = (f32[512,128]{1,0:T(8,128)S(1)}, f32[512,128]{1,0:T(8,128)S(1)}, u32[]{:S(2)}, u32[]{:S(2)}) collective-permute-start(f32[512,128]{1,0:T(8,128)S(1)} %add.123), channel_id=1, source_target_pairs={{0,2},{1,3},{2,0},{3,1},{4,6},{5,7},{6,4},{7,5},{8,10},{9,11},{10,... | collective-permute-start | bytes 786440 | tf_op jit(solution)/shard_map/ppermute | solution.py:388
  22.1 20.9 %collective-permute-start.10 = (bf16[64,4096]{1,0:T(8,128)(2,1)S(1)}, bf16[64,4096]{1,0:T(8,128)(2,1)S(1)}, u32[]{:S(2)}, u32[]{:S(2)}) collective-permute-start(bf16[64,4096]{1,0:T(8,128)(2,1)S(1)} %collective-permute-done.2.refs_0_), channel_id=1, source_target_pairs={{0,8},{8,16},{16,24},{24,28},{28,20},{20,12},{12,4},{4,0},{1,9},{9... | collective-permute-start | bytes 1572872 | tf_op jit(solution)/shard_map/ppermute | solution.py:440
  23.7 20.9 %collective-permute-start.11 = (bf16[64,4096]{1,0:T(8,128)(2,1)S(1)}, bf16[64,4096]{1,0:T(8,128)(2,1)S(1)}, u32[]{:S(2)}, u32[]{:S(2)}) collective-permute-start(bf16[64,4096]{1,0:T(8,128)(2,1)S(1)} %collective-permute-done.3.refs_1_), channel_id=1, source_target_pairs={{8,0},{16,8},{24,16},{28,24},{20,28},{12,20},{4,12},{0,4},{9,1},{1... | collective-permute-start | bytes 1572872 | tf_op jit(solution)/shard_map/ppermute | solution.py:440
  31.7 4.6 %collective-permute-start.4 = (f32[512,128]{1,0:T(8,128)S(1)}, f32[512,128]{1,0:T(8,128)S(1)}, u32[]{:S(2)}, u32[]{:S(2)}) collective-permute-start(f32[512,128]{1,0:T(8,128)S(1)} %get-tuple-element.67), channel_id=1, source_target_pairs={{0,1},{1,0},{2,3},{3,2},{4,5},{5,4},{6,7},{7,6},{8,9},{9,8},{10,11... | collective-permute-start | bytes 786440 | tf_op jit(solution)/shard_map/ppermute | solution.py:388
  36.2 3.3 %collective-permute-start.8 = (f32[512,128]{1,0:T(8,128)S(1)}, f32[512,128]{1,0:T(8,128)S(1)}, u32[]{:S(2)}, u32[]{:S(2)}) collective-permute-start(f32[512,128]{1,0:T(8,128)S(1)} %get-tuple-element.73), channel_id=1, source_target_pairs={{0,1},{1,0},{2,3},{3,2},{4,5},{5,4},{6,7},{7,6},{8,9},{9,8},{10,11... | collective-permute-start | bytes 786440 | tf_op jit(solution)/shard_map/ppermute | solution.py:388
  36.3 9.8 %collective-permute-start.5 = (f32[512,128]{1,0:T(8,128)S(1)}, f32[512,128]{1,0:T(8,128)S(1)}, u32[]{:S(2)}, u32[]{:S(2)}) collective-permute-start(f32[512,128]{1,0:T(8,128)S(1)} %add.135), channel_id=1, source_target_pairs={{0,2},{1,3},{2,0},{3,1},{4,6},{5,7},{6,4},{7,5},{8,10},{9,11},{10,... | collective-permute-start | bytes 786440 | tf_op jit(solution)/shard_map/ppermute | solution.py:388
  38.0 16.2 %collective-permute-start.14 = (bf16[64,4096]{1,0:T(8,128)(2,1)S(1)}, bf16[64,4096]{1,0:T(8,128)(2,1)S(1)}, u32[]{:S(2)}, u32[]{:S(2)}) collective-permute-start(bf16[64,4096]{1,0:T(8,128)(2,1)S(1)} %collective-permute-done.6.refs_1_), channel_id=1, source_target_pairs={{0,8},{8,16},{16,24},{24,28},{28,20},{20,12},{12,4},{4,0},{1,9},{9... | collective-permute-start | bytes 1572872 | tf_op jit(solution)/shard_map/ppermute | solution.py:440
  39.5 16.3 %collective-permute-start.15 = (bf16[64,4096]{1,0:T(8,128)(2,1)S(1)}, bf16[64,4096]{1,0:T(8,128)(2,1)S(1)}, u32[]{:S(2)}, u32[]{:S(2)}) collective-permute-start(bf16[64,4096]{1,0:T(8,128)(2,1)S(1)} %collective-permute-done.7.refs_0_), channel_id=1, source_target_pairs={{8,0},{16,8},{24,16},{28,24},{20,28},{12,20},{4,12},{0,4},{9,1},{1... | collective-permute-start | bytes 1572872 | tf_op jit(solution)/shard_map/ppermute | solution.py:440
  42.9 7.6 %collective-permute-start.16 = (f32[512,128]{1,0:T(8,128)S(1)}, f32[512,128]{1,0:T(8,128)S(1)}, u32[]{:S(2)}, u32[]{:S(2)}) collective-permute-start(f32[512,128]{1,0:T(8,128)S(1)} %add.124.refs_0_), channel_id=1, source_target_pairs={{0,1},{1,0},{2,3},{3,2},{4,5},{5,4},{6,7},{7,6},{8,9},{9,8},{10,11... | collective-permute-start | bytes 786440 | tf_op jit(solution)/shard_map/ppermute | solution.py:388
  44.6 14.2 %collective-permute-start.9 = (f32[512,128]{1,0:T(8,128)S(1)}, f32[512,128]{1,0:T(8,128)S(1)}, u32[]{:S(2)}, u32[]{:S(2)}) collective-permute-start(f32[512,128]{1,0:T(8,128)S(1)} %add.137), channel_id=1, source_target_pairs={{0,2},{1,3},{2,0},{3,1},{4,6},{5,7},{6,4},{7,5},{8,10},{9,11},{10,... | collective-permute-start | bytes 786440 | tf_op jit(solution)/shard_map/ppermute | solution.py:388
  46.1 19.3 %collective-permute-start.23 = (bf16[64,4096]{1,0:T(8,128)(2,1)S(1)}, bf16[64,4096]{1,0:T(8,128)(2,1)S(1)}, u32[]{:S(2)}, u32[]{:S(2)}) collective-permute-start(bf16[64,4096]{1,0:T(8,128)(2,1)S(1)} %collective-permute-done.10.refs_0_), channel_id=1, source_target_pairs={{0,8},{8,16},{16,24},{24,28},{28,20},{20,12},{12,4},{4,0},{1,9},{9... | collective-permute-start | bytes 1572872 | tf_op jit(solution)/shard_map/ppermute | solution.py:440
  50.6 16.4 %collective-permute-start.24 = (bf16[64,4096]{1,0:T(8,128)(2,1)S(1)}, bf16[64,4096]{1,0:T(8,128)(2,1)S(1)}, u32[]{:S(2)}, u32[]{:S(2)}) collective-permute-start(bf16[64,4096]{1,0:T(8,128)(2,1)S(1)} %collective-permute-done.11.refs_1_), channel_id=1, source_target_pairs={{8,0},{16,8},{24,16},{28,24},{20,28},{12,20},{4,12},{0,4},{9,1},{1... | collective-permute-start | bytes 1572872 | tf_op jit(solution)/shard_map/ppermute | solution.py:440
  54.2 5.1 %collective-permute-start.12 = (f32[512,128]{1,0:T(8,128)S(1)}, f32[512,128]{1,0:T(8,128)S(1)}, u32[]{:S(2)}, u32[]{:S(2)}) collective-permute-start(f32[512,128]{1,0:T(8,128)S(1)} %get-tuple-element.77), channel_id=1, source_target_pairs={{0,1},{1,0},{2,3},{3,2},{4,5},{5,4},{6,7},{7,6},{8,9},{9,8},{10,11... | collective-permute-start | bytes 786440 | tf_op jit(solution)/shard_map/ppermute | solution.py:388
  58.7 2.3 %collective-permute-start.17 = (f32[512,128]{1,0:T(8,128)S(1)}, f32[512,128]{1,0:T(8,128)S(1)}, u32[]{:S(2)}, u32[]{:S(2)}) collective-permute-start(f32[512,128]{1,0:T(8,128)S(1)} %get-tuple-element.81), channel_id=1, source_target_pairs={{0,1},{1,0},{2,3},{3,2},{4,5},{5,4},{6,7},{7,6},{8,9},{9,8},{10,11... | collective-permute-start | bytes 786440 | tf_op jit(solution)/shard_map/ppermute | solution.py:388
  58.8 2.7 %collective-permute-start.19 = (f32[512,128]{1,0:T(8,128)S(1)}, f32[512,128]{1,0:T(8,128)S(1)}, u32[]{:S(2)}, u32[]{:S(2)}) collective-permute-start(f32[512,128]{1,0:T(8,128)S(1)} %add.136.refs_1_), channel_id=1, source_target_pairs={{0,1},{1,0},{2,3},{3,2},{4,5},{5,4},{6,7},{7,6},{8,9},{9,8},{10,11... | collective-permute-start | bytes 786440 | tf_op jit(solution)/shard_map/ppermute | solution.py:388
  59.3 17.3 %collective-permute-start.27 = (bf16[64,4096]{1,0:T(8,128)(2,1)S(1)}, bf16[64,4096]{1,0:T(8,128)(2,1)S(1)}, u32[]{:S(2)}, u32[]{:S(2)}) collective-permute-start(bf16[64,4096]{1,0:T(8,128)(2,1)S(1)} %collective-permute-done.14.refs_1_), channel_id=1, source_target_pairs={{0,8},{8,16},{16,24},{24,28},{28,20},{20,12},{12,4},{4,0},{1,9},{9... | collective-permute-start | bytes 1572872 | tf_op jit(solution)/shard_map/ppermute | solution.py:440
  61.0 17.5 %collective-permute-start.28 = (bf16[64,4096]{1,0:T(8,128)(2,1)S(1)}, bf16[64,4096]{1,0:T(8,128)(2,1)S(1)}, u32[]{:S(2)}, u32[]{:S(2)}) collective-permute-start(bf16[64,4096]{1,0:T(8,128)(2,1)S(1)} %collective-permute-done.15.refs_0_), channel_id=1, source_target_pairs={{8,0},{16,8},{24,16},{28,24},{20,28},{12,20},{4,12},{0,4},{9,1},{1... | collective-permute-start | bytes 1572872 | tf_op jit(solution)/shard_map/ppermute | solution.py:440
  61.5 9.0 %collective-permute-start.18 = (f32[512,128]{1,0:T(8,128)S(1)}, f32[512,128]{1,0:T(8,128)S(1)}, u32[]{:S(2)}, u32[]{:S(2)}) collective-permute-start(f32[512,128]{1,0:T(8,128)S(1)} %add.141), channel_id=1, source_target_pairs={{0,2},{1,3},{2,0},{3,1},{4,6},{5,7},{6,4},{7,5},{8,10},{9,11},{10,... | collective-permute-start | bytes 786440 | tf_op jit(solution)/shard_map/ppermute | solution.py:388
  70.0 2.1 %collective-permute-start.25 = (f32[512,128]{1,0:T(8,128)S(1)}, f32[512,128]{1,0:T(8,128)S(1)}, u32[]{:S(2)}, u32[]{:S(2)}) collective-permute-start(f32[512,128]{1,0:T(8,128)S(1)} %get-tuple-element.88), channel_id=1, source_target_pairs={{0,1},{1,0},{2,3},{3,2},{4,5},{5,4},{6,7},{7,6},{8,9},{9,8},{10,11... | collective-permute-start | bytes 786440 | tf_op jit(solution)/shard_map/ppermute | solution.py:388
  70.0 3.7 %collective-permute-start.20 = (f32[512,128]{1,0:T(8,128)S(1)}, f32[512,128]{1,0:T(8,128)S(1)}, u32[]{:S(2)}, u32[]{:S(2)}) collective-permute-start(f32[512,128]{1,0:T(8,128)S(1)} %add.138.refs_2_), channel_id=1, source_target_pairs={{0,1},{1,0},{2,3},{3,2},{4,5},{5,4},{6,7},{7,6},{8,9},{9,8},{10,11... | collective-permute-start | bytes 786440 | tf_op jit(solution)/shard_map/ppermute | solution.py:388
  70.5 10.9 %collective-permute-start.13 = (f32[512,128]{1,0:T(8,128)S(1)}, f32[512,128]{1,0:T(8,128)S(1)}, u32[]{:S(2)}, u32[]{:S(2)}) collective-permute-start(f32[512,128]{1,0:T(8,128)S(1)} %add.139), channel_id=1, source_target_pairs={{0,2},{1,3},{2,0},{3,1},{4,6},{5,7},{6,4},{7,5},{8,10},{9,11},{10,... | collective-permute-start | bytes 786440 | tf_op jit(solution)/shard_map/ppermute | solution.py:388
  72.1 15.0 %collective-permute-start.31 = (bf16[64,4096]{1,0:T(8,128)(2,1)S(1)}, bf16[64,4096]{1,0:T(8,128)(2,1)S(1)}, u32[]{:S(2)}, u32[]{:S(2)}) collective-permute-start(bf16[64,4096]{1,0:T(8,128)(2,1)S(1)} %collective-permute-done.23.refs_0_), channel_id=1, source_target_pairs={{0,8},{8,16},{16,24},{24,28},{28,20},{20,12},{12,4},{4,0},{1,9},{9... | collective-permute-start | bytes 1572872 | tf_op jit(solution)/shard_map/ppermute | solution.py:440
  73.7 14.9 %collective-permute-start.32 = (bf16[64,4096]{1,0:T(8,128)(2,1)S(1)}, bf16[64,4096]{1,0:T(8,128)(2,1)S(1)}, u32[]{:S(2)}, u32[]{:S(2)}) collective-permute-start(bf16[64,4096]{1,0:T(8,128)(2,1)S(1)} %collective-permute-done.24.refs_1_), channel_id=1, source_target_pairs={{8,0},{16,8},{24,16},{28,24},{20,28},{12,20},{4,12},{0,4},{9,1},{1... | collective-permute-start | bytes 1572872 | tf_op jit(solution)/shard_map/ppermute | solution.py:440
  76.7 7.8 %collective-permute-start.26 = (f32[512,128]{1,0:T(8,128)S(1)}, f32[512,128]{1,0:T(8,128)S(1)}, u32[]{:S(2)}, u32[]{:S(2)}) collective-permute-start(f32[512,128]{1,0:T(8,128)S(1)} %add.143), channel_id=1, source_target_pairs={{0,2},{1,3},{2,0},{3,1},{4,6},{5,7},{6,4},{7,5},{8,10},{9,11},{10,... | collective-permute-start | bytes 786440 | tf_op jit(solution)/shard_map/ppermute | solution.py:388
  81.4 3.1 %collective-permute-start.29 = (f32[512,128]{1,0:T(8,128)S(1)}, f32[512,128]{1,0:T(8,128)S(1)}, u32[]{:S(2)}, u32[]{:S(2)}) collective-permute-start(f32[512,128]{1,0:T(8,128)S(1)} %get-tuple-element.91), channel_id=1, source_target_pairs={{0,1},{1,0},{2,3},{3,2},{4,5},{5,4},{6,7},{7,6},{8,9},{9,8},{10,11... | collective-permute-start | bytes 786440 | tf_op jit(solution)/shard_map/ppermute | solution.py:388
  81.5 4.6 %collective-permute-start.22 = (f32[512,128]{1,0:T(8,128)S(1)}, f32[512,128]{1,0:T(8,128)S(1)}, u32[]{:S(2)}, u32[]{:S(2)}) collective-permute-start(f32[512,128]{1,0:T(8,128)S(1)} %add.142.refs_4_), channel_id=1, source_target_pairs={{0,1},{1,0},{2,3},{3,2},{4,5},{5,4},{6,7},{7,6},{8,9},{9,8},{10,11... | collective-permute-start | bytes 786440 | tf_op jit(solution)/shard_map/ppermute | solution.py:388
  84.4 1.7 %collective-permute-start.21 = (f32[512,128]{1,0:T(8,128)S(1)}, f32[512,128]{1,0:T(8,128)S(1)}, u32[]{:S(2)}, u32[]{:S(2)}) collective-permute-start(f32[512,128]{1,0:T(8,128)S(1)} %add.140.refs_3_), channel_id=1, source_target_pairs={{0,1},{1,0},{2,3},{3,2},{4,5},{5,4},{6,7},{7,6},{8,9},{9,8},{10,11... | collective-permute-start | bytes 786440 | tf_op jit(solution)/shard_map/ppermute | solution.py:388
  84.5 11.0 %collective-permute-start.30 = (f32[512,128]{1,0:T(8,128)S(1)}, f32[512,128]{1,0:T(8,128)S(1)}, u32[]{:S(2)}, u32[]{:S(2)}) collective-permute-start(f32[512,128]{1,0:T(8,128)S(1)} %add.145), channel_id=1, source_target_pairs={{0,2},{1,3},{2,0},{3,1},{4,6},{5,7},{6,4},{7,5},{8,10},{9,11},{10,... | collective-permute-start | bytes 786440 | tf_op jit(solution)/shard_map/ppermute | solution.py:388
  90.4 1.9 %collective-permute-start.33 = (f32[512,128]{1,0:T(8,128)S(1)}, f32[512,128]{1,0:T(8,128)S(1)}, u32[]{:S(2)}, u32[]{:S(2)}) collective-permute-start(f32[512,128]{1,0:T(8,128)S(1)} %cost_share.16), channel_id=1, source_target_pairs={{0,1},{1,0},{2,3},{3,2},{4,5},{5,4},{6,7},{7,6},{8,9},{9,8},{10,11... | collective-permute-start | bytes 786440 | tf_op jit(solution)/shard_map/ppermute | solution.py:388
  92.4 8.8 %collective-permute-start.34 = (f32[512,128]{1,0:T(8,128)S(1)}, f32[512,128]{1,0:T(8,128)S(1)}, u32[]{:S(2)}, u32[]{:S(2)}) collective-permute-start(f32[512,128]{1,0:T(8,128)S(1)} %add.147), channel_id=1, source_target_pairs={{0,2},{1,3},{2,0},{3,1},{4,6},{5,7},{6,4},{7,5},{8,10},{9,11},{10,... | collective-permute-start | bytes 786440 | tf_op jit(solution)/shard_map/ppermute | solution.py:388
  95.3 6.0 %collective-permute-start.35 = (f32[512,128]{1,0:T(8,128)S(1)}, f32[512,128]{1,0:T(8,128)S(1)}, u32[]{:S(2)}, u32[]{:S(2)}) collective-permute-start(f32[512,128]{1,0:T(8,128)S(1)} %add.144.refs_0_), channel_id=1, source_target_pairs={{0,1},{1,0},{2,3},{3,2},{4,5},{5,4},{6,7},{7,6},{8,9},{9,8},{10,11... | collective-permute-start | bytes 786440 | tf_op jit(solution)/shard_map/ppermute | solution.py:388
  95.6 5.7 %collective-permute-start.36 = (f32[512,128]{1,0:T(8,128)S(1)}, f32[512,128]{1,0:T(8,128)S(1)}, u32[]{:S(2)}, u32[]{:S(2)}) collective-permute-start(f32[512,128]{1,0:T(8,128)S(1)} %add.146.refs_1_), channel_id=1, source_target_pairs={{0,1},{1,0},{2,3},{3,2},{4,5},{5,4},{6,7},{7,6},{8,9},{9,8},{10,11... | collective-permute-start | bytes 786440 | tf_op jit(solution)/shard_map/ppermute | solution.py:388
  101.2 1.6 %collective-permute-start.37 = (f32[512,128]{1,0:T(8,128)S(1)}, f32[512,128]{1,0:T(8,128)S(1)}, u32[]{:S(2)}, u32[]{:S(2)}) collective-permute-start(f32[512,128]{1,0:T(8,128)S(1)} %add.148.refs_2_), channel_id=1, source_target_pairs={{0,1},{1,0},{2,3},{3,2},{4,5},{5,4},{6,7},{7,6},{8,9},{9,8},{10,11... | collective-permute-start | bytes 786440 | tf_op jit(solution)/shard_map/ppermute | solution.py:388
